TPU v7x, 256 devices: a whole 4x4x8 slice. The times are simulated.
256 devices in a mesh: grp: 8 (over x, z_lo), freq: 32 (over y, z_hi, core).
Axes of the slice: x: 4, y: 4, z: 8 (z_hi: 4, z_lo: 2; z = z_hi * 2 + z_lo), core: 2. Of those that a mesh axis runs over, the one named last changes fastest.
Arguments:
- samples: int32 [1024, 268288], P(('grp', 'freq')), may hold values from -128 to 127
- window: float32 [4, 2048], replicated, may hold values from 0.2 to 1
Outputs:
- vis_real: bfloat16 [512, 1024, 1024], P('freq', 'grp')
- vis_imag: bfloat16 [512, 1024, 1024], P('freq', 'grp')
Inputs may be any that keep to these rules, and one draw needn't show every extreme that they name: `samples`: each word holds one signed 8-bit sample.
All inputs are finite; a program needn't handle non-finite values.
Results may differ from a plain program's by a relative error of at most 0.0065.
Values may be sent and summed in bfloat16 or wider, within the bound.
No kernel may reach another device: no remote copies, remote signals or barrier semaphores. Data moves between devices by JAX's collectives and lax.ppermute only.
A program may use at most 128 MiB of HBM per device.

v0:
```python
import math

import jax
import jax.numpy as jnp
from jax import lax
from jax.sharding import PartitionSpec as P

CHAN = 512


def dft_table(fft_len, chan_count):
    rows_idx = jnp.arange(fft_len, dtype=jnp.int32)
    cols_idx = jnp.arange(chan_count, dtype=jnp.int32)
    phase_idx = rows_idx[:, None] * cols_idx[None, :] % fft_len
    angles = phase_idx.astype(jnp.float32) * (2.0 * math.pi / fft_len)
    stacked = jnp.stack([jnp.cos(angles), -jnp.sin(angles)], axis=2)
    return stacked.reshape(fft_len, 2 * chan_count).astype(jnp.bfloat16)


def with_rotated(own_block, spec_count):
    rotated = jnp.concatenate([own_block[..., spec_count:], -own_block[..., :spec_count]], axis=-1)
    return jnp.stack([own_block, rotated], axis=0)


def on_device(samples, window):
    input_count = samples.shape[0]
    tap_count = window.shape[0]
    fft_len = window.shape[1]
    frame_count = samples.shape[1] // fft_len
    spec_count = frame_count - tap_count + 1
    voltage = samples.astype(jnp.float32).reshape(input_count, frame_count, fft_len) * (1.0 / 64.0)
    filtered = window[0] * voltage[:, 0:spec_count, :]
    for tap_idx in range(1, tap_count):
        filtered = filtered + window[tap_idx] * voltage[:, tap_idx : tap_idx + spec_count, :]
    filtered = filtered.astype(jnp.bfloat16)
    cosines = dft_table(fft_len, CHAN)
    raw_sum = jnp.einsum("isj,jm->ims", filtered, cosines, preferred_element_type=jnp.float32)
    raw_sum = raw_sum * (1.0 / math.sqrt(fft_len))
    spectra = raw_sum.reshape(input_count, CHAN, 2 * spec_count).astype(jnp.bfloat16)
    own_block = lax.all_to_all(spectra, "freq", split_axis=1, concat_axis=0, tiled=True)
    operands = with_rotated(own_block, spec_count)
    products = jnp.einsum(
        "pack,bck->pcab",
        operands,
        lax.all_gather(own_block, "grp", axis=0, tiled=True),
        preferred_element_type=jnp.float32,
    )
    scaled = products * (1.0 / spec_count)
    return (scaled[0].astype(jnp.bfloat16), scaled[1].astype(jnp.bfloat16))


def solution(mesh):
    return jax.shard_map(
        on_device,
        mesh=mesh,
        in_specs=(P(("grp", "freq"), None), P()),
        out_specs=(P("freq", "grp", None), P("freq", "grp", None)),
        check_vma=False,
    )
```

profile of v0, /device:TPU:8, one launch (start us, length us, event | category | flops | bytes accessed | tf_op | source)
XLA Modules:
  0.0 314.6 jit_solution(14175016956420036267)
XLA Ops:
  7.2 0.0 copy-start
  7.2 0.0 all-gather.2.cloned.1.call-start
  7.2 17.1 %negate_convert_fusion = (bf16[2048,512,1]{1,0,2:T(8,128)(2,1)S(1)}, bf16[2048,512,1]{1,0,2:T(8,128)(2,1)S(1)}) fusion(), kind=kLoop, calls=%fused_computation.21 | loop fusion | flops 17825792 | bytes 4194304 | tf_op jit(solution)/shard_map/convert.3
  24.3 0.0 copy-done
  24.4 2.4 pad_maximum_fusion
  26.8 11.3 %copy.18 = bf16[2048,512,2]{0,2,1:T(2,128)(2,1)} copy(bf16[2048,512,2]{1,0,2:T(8,128)(2,1)} %pad_maximum_fusion) | data formatting | bytes 8388608 | tf_op jit(solution)/shard_map/stack | solution.py:16
  38.0 7.2 %reshape.89 = bf16[2048,1024,1]{0,1,2:T(8,128)(2,1)} reshape(bf16[2048,512,2]{0,2,1:T(2,128)(2,1)} %copy.18) | data formatting | bytes 8388608 | tf_op jit(solution)/shard_map/convert_element_type | solution.py:17
  45.2 5.6 %convert_multiply_fusion = f32[4,268288]{1,0:T(4,128)} fusion(s32[4,268288]{1,0:T(4,128)} %param.2), kind=kLoop, calls=%fused_computation.6 | loop fusion | flops 2146304 | bytes 8585216 | tf_op jit(solution)/shard_map/mul | solution.py:31
  50.8 7.2 %mul.123 = f32[4,131,2048]{2,1,0:T(8,128)} reshape(f32[4,268288]{1,0:T(4,128)} %convert_multiply_fusion) | data formatting | bytes 8585216 | tf_op jit(solution)/shard_map/mul | solution.py:31
  58.0 10.0 %fusion.21 = bf16[4,1024,128]{2,1,0:T(8,128)(2,1)S(1)} fusion(bf16[2048,1024,1]{0,1,2:T(8,128)(2,1)} %reshape.89, f32[4,131,2048]{2,1,0:T(8,128)} %mul.123, f32[2048]{0:T(1024)S(1)} %bitcast.37, f32[2048]{0:T(1024)S(1)} %bitcast.38, f32[2048]{0:T(1024)S(1)} %bitcast.36, f32[2048]{0:T(1024)S(1)} %bitcast.35), kind=kOutput, calls=%fused_computation.31 | convolution fusion | flops 2156920832 | bytes 22052864 | tf_op jit(solution)/shard_map/isj,jm->ims/dot_general | solution.py:37
  67.9 0.4 convert_element_type.49
  68.3 0.8 copy.19
  69.2 39.1 %all_to_all.18 = bf16[4,512,256]{2,0,1:T(4,128)(2,1)S(1)} all-to-all(bf16[4,512,256]{2,0,1:T(4,128)(2,1)S(1)} %copy.19), channel_id=1, replica_groups=mesh['grp'=8,'freq'=32] {'freq'}, dimensions={1} | all-to-all | bytes 2097152 | tf_op jit(solution)/shard_map/all_to_all | solution.py:40
  108.3 0.5 copy.25
  108.8 1.1 all_to_all.16
  109.9 0.0 all-gather.2.cloned.1.call-update
  109.9 0.3 stack.16
  110.2 1.3 fusion.25
  111.5 0.1 maximum_bitcast_fusion
  111.7 167.1 %all-gather.2.cloned.1.call-done = bf16[1024,16,256]{2,0,1:T(8,128)(2,1)} async-done(((bf16[128,16,256]{2,0,1:T(8,128)(2,1)}), bf16[1024,16,256]{2,0,1:T(8,128)(2,1)}) %all-gather.2.cloned.1.call-update) | async-done | bytes 8388624 | tf_op jit(solution)/shard_map/all_gather | solution.py:45
  278.8 10.1 %fusion.1 = bf16[2,16,128,1024]{2,3,0,1:T(8,128)(2,1)} fusion(bf16[1024,16,256]{2,0,1:T(8,128)(2,1)} %all-gather.2.cloned.1.call-done, bf16[1,128,16,256]{3,1,0,2:T(8,128)(2,1)S(1)} %maximum_bitcast_fusion, bf16[1,128,16,256]{3,1,0,2:T(8,128)(2,1)S(1)} %stack.16), kind=kOutput, calls=%fused_computation.5 | convolution fusion | flops 2160066560 | bytes 18874368 | tf_op jit(solution)/shard_map/pack,bck->pcab/dot_general | solution.py:42
  289.0 6.0 %slice_bitcast_fusion = (bf16[16,128,1024]{1,2,0:T(8,128)(2,1)}, bf16[16,128,1024]{1,2,0:T(8,128)(2,1)}) fusion(bf16[2,16,128,1024]{2,3,0,1:T(8,128)(2,1)} %fusion.1), kind=kLoop, calls=%fused_computation.10 | loop fusion | bytes 16777216 | tf_op jit(solution)/shard_map/convert_element_type | solution.py:49
  294.9 6.4 %copy.22 = bf16[16,128,1024]{2,1,0:T(8,128)(2,1)} copy(bf16[16,128,1024]{1,2,0:T(8,128)(2,1)} %get-tuple-element.12) | data formatting | bytes 8388608
  301.3 6.4 %copy.21 = bf16[16,128,1024]{2,1,0:T(8,128)(2,1)} copy(bf16[16,128,1024]{1,2,0:T(8,128)(2,1)} %get-tuple-element.13) | data formatting | bytes 8388608
  (1 shorter events, 0.0 us)
Async XLA Ops:
  7.2 17.2 %copy-start = (f32[4,2048]{1,0:T(4,128)S(1)}, f32[4,2048]{1,0:T(4,128)}, u32[]{:S(2)}) copy-start(f32[4,2048]{1,0:T(4,128)} %param.3) | copy-start | bytes 98308
  7.2 271.6 %all-gather.2.cloned.1.call-start = ((), (), s32[]{:S(2)}) async-start(), calls=%async_computation.1 | async-start | bytes 9437184 | tf_op jit(solution)/shard_map/all_gather | solution.py:45
Sparse Core Ops, SparseCore 0:
  110.0 168.7 all-gather.1
where the time goes:
time: 316 us; the launch traced here: 315 us
  waiting for transfers between devices  167 us (53%)
  local copies, waits for them, and re-layouts  47.5 us (15%)
  blocking collectives  39.1 us (12%)
  other arithmetic  26.5 us (8%)
  matrix products  20.1 us (6%)
  between operations  14.1 us (4%)
    all_gather x1, waiting for transfers between devices, on_device(): lax.all_gather(own_block, 'grp', axis=0, tiled=True)  167 us
    all_to_all x1, blocking collectives, on_device(): lax.all_to_all(spectra, 'freq', split_axis=1, concat_axis=0, tiled=True)  39.1 us
    another operation x1, other arithmetic  17.1 us
    unnamed x4, local copies, waits for them, and re-layouts  12.8 us
    another operation x1, local copies, waits for them, and re-layouts, dft_table(): stacked = jnp.stack([jnp.cos(angles), -jnp.sin(angles)], axis=2)  11.3 us
    dot_general x1, matrix products, on_device(): jnp.einsum('pack,bck->pcab', operands, lax.all_gather(own_block, 'grp', a...  10.1 us
    dot_general x1, matrix products, on_device(): jnp.einsum('isj,jm->ims', filtered, cosines, preferred_element_type=jnp.f...  9.97 us
    mul x1, local copies, waits for them, and re-layouts, on_device(): samples.astype(jnp.float32).reshape(input_count, frame_count, fft_len)  7.17 us
  transfers between devices with their start and end apart: 1, of which 1 were waited for; matrix products, arithmetic and copies ran while one was open for 1% of the time, Pallas kernels for 0%

commit v1 on v0

v1 whole, which is shorter than its diff:
```python
import math

import jax
import jax.numpy as jnp
import ml_dtypes
import numpy as np
from jax import lax
from jax.experimental import pallas as pl
from jax.experimental.pallas import tpu as pltpu
from jax.sharding import Mesh, PartitionSpec as P

CHAN = 512
NFFT = 2048
TAPS = 4
SPEC = 128
FRAMES = SPEC + TAPS - 1
ROWS_IN = 4
GROUPS = 8
N_FREQ = 32
CH = CHAN // N_FREQ
LANES = 128
SUB = 8
STEPS = 8
TILES = NFFT // LANES // STEPS
F32 = jnp.float32
BF16 = jnp.bfloat16
NT = (((1,), (1,)), ((), ()))


def table_rows():
    j = np.arange(NFFT, dtype=np.int64)
    c = np.arange(CHAN, dtype=np.int64)
    angle = ((c[:, None] * j[None, :]) % NFFT).astype(np.float32) * np.float32(2.0 * math.pi / NFFT)
    both = np.stack([np.cos(angle), -np.sin(angle)], axis=0)
    both = both.reshape(2, N_FREQ, CH, NFFT).transpose(1, 0, 2, 3)
    return both.reshape(2 * CHAN, NFFT).astype(ml_dtypes.bfloat16)


def channelize_kernel(s_ref, w_ref, t_ref, o_ref, f_ref):
    g = pl.program_id(0)
    per = TILES * ROWS_IN
    flat = s_ref.reshape(FRAMES * per, LANES)
    groups = SPEC // SUB
    for jt in range(TILES):
        cols = slice(jt * LANES, (jt + 1) * LANES)
        taps = [jnp.broadcast_to(w_ref[t : t + 1, cols] * (1.0 / 64.0), (SUB, LANES)) for t in range(TAPS)]
        for i in range(ROWS_IN):
            v = [
                flat[pl.ds(r * per + jt * ROWS_IN + i, SUB, stride=groups * per), :].astype(F32)
                for r in range(groups + TAPS - 1)
            ]
            rows = []
            for r in range(groups):
                acc = taps[0] * v[r]
                for t in range(1, TAPS):
                    acc = acc + taps[t] * v[r + t]
                rows.append(acc)
            block = jnp.concatenate(rows, axis=0).astype(BF16)
            f_ref[i * SPEC : (i + 1) * SPEC, pl.ds(pl.multiple_of((g * TILES + jt) * LANES, LANES), LANES)] = block

    @pl.when(g == STEPS - 1)
    def _():
        per_dev = 2 * CH
        tile = 256
        for mt in range(2 * CHAN // tile):
            raw = lax.dot_general(t_ref[mt * tile : (mt + 1) * tile, :], f_ref[...], NT, preferred_element_type=F32)
            out = (raw * (1.0 / math.sqrt(NFFT))).astype(BF16)
            for d in range(tile // per_dev):
                for i in range(ROWS_IN):
                    o_ref[mt * (tile // per_dev) + d, i] = out[d * per_dev : (d + 1) * per_dev, i * SPEC : (i + 1) * SPEC]


def channelize(samples, window, table):
    view = samples.reshape(ROWS_IN, FRAMES, NFFT // LANES, LANES).transpose(1, 2, 0, 3)
    view = view.reshape(FRAMES, NFFT // LANES * ROWS_IN, LANES)
    return pl.pallas_call(
        channelize_kernel,
        out_shape=jax.ShapeDtypeStruct((N_FREQ, ROWS_IN, 2 * CH, SPEC), BF16),
        grid=(STEPS,),
        in_specs=[
            pl.BlockSpec((FRAMES, TILES * ROWS_IN, LANES), lambda g: (0, g, 0)),
            pl.BlockSpec((TAPS, TILES * LANES), lambda g: (0, g)),
            pl.BlockSpec((2 * CHAN, NFFT), lambda g: (0, 0)),
        ],
        out_specs=pl.BlockSpec((N_FREQ, ROWS_IN, 2 * CH, SPEC), lambda g: (0, 0, 0, 0)),
        scratch_shapes=[pltpu.VMEM((ROWS_IN * SPEC, NFFT), BF16)],
        compiler_params=pltpu.CompilerParams(vmem_limit_bytes=40 << 20),
        cost_estimate=pl.CostEstimate(flops=2 * 512 * 2048 * 1024, bytes_accessed=9 << 20, transcendentals=0),
        name="channelize",
    )(view, window, table)


PARTS = ((0, 10), (10, 13), (13, 16))


def assemble_kernel(x_ref, *refs):
    outs, wide = refs[:-1], refs[-1]
    per = 2 * CH
    wide[...] = x_ref[...].reshape(SPEC * per, SPEC).astype(F32)
    for out, (lo, hi) in zip(outs, PARTS):
        for c in range(lo, hi):
            for p in range(2):
                out[c - lo, :, p * SPEC : (p + 1) * SPEC] = wide[pl.ds(p * CH + c, SPEC, stride=per), :].astype(BF16)


def assemble(x):
    return pl.pallas_call(
        assemble_kernel,
        out_shape=[jax.ShapeDtypeStruct((hi - lo, SPEC, 2 * SPEC), BF16) for lo, hi in PARTS],
        scratch_shapes=[pltpu.VMEM((SPEC * 2 * CH, SPEC), F32)],
        compiler_params=pltpu.CompilerParams(vmem_limit_bytes=40 << 20),
        cost_estimate=pl.CostEstimate(flops=0, bytes_accessed=2 << 20, transcendentals=0),
        name="assemble",
    )(x)


def correlate_kernel(col_ref, *refs):
    blocks, (re_ref, im_ref) = refs[:GROUPS], refs[-2:]
    own = blocks[0][0]
    rotated = jnp.concatenate([own[:, SPEC:], -own[:, :SPEC]], axis=1)
    left = jnp.concatenate([own, rotated], axis=0)
    for b in range(GROUPS):
        prod = lax.dot_general(left, blocks[b][0], NT, preferred_element_type=F32) * (1.0 / SPEC)
        cols = pl.ds(pl.multiple_of(col_ref[b], SPEC), SPEC)
        re_ref[0, :, cols] = prod[:SPEC].astype(BF16)
        im_ref[0, :, cols] = prod[SPEC:].astype(BF16)


def correlate(cols, blocks, lo, earlier):
    count, width = blocks[0].shape[0], SPEC * GROUPS
    shape = jax.ShapeDtypeStruct((CH, SPEC, width), BF16)
    in_specs = [pl.BlockSpec((1, SPEC, 2 * SPEC), lambda c, s: (c, 0, 0)) for _ in blocks]
    operands = list(blocks)
    aliases = {}
    if earlier is not None:
        in_specs += [pl.BlockSpec(memory_space=pl.ANY)] * 2
        operands += list(earlier)
        aliases = {1 + GROUPS: 0, 2 + GROUPS: 1}
    return pl.pallas_call(
        correlate_kernel,
        out_shape=[shape, shape],
        grid_spec=pltpu.PrefetchScalarGridSpec(
            num_scalar_prefetch=1,
            grid=(count,),
            in_specs=in_specs,
            out_specs=[pl.BlockSpec((1, SPEC, width), lambda c, s: (c + lo, 0, 0))] * 2,
        ),
        input_output_aliases=aliases,
        compiler_params=pltpu.CompilerParams(vmem_limit_bytes=40 << 20),
        cost_estimate=pl.CostEstimate(flops=count * 2 * 256 * 256 * 1024, bytes_accessed=count << 20, transcendentals=0),
        name="correlate",
    )(cols, *operands)


def shift(v, axis, size, by):
    return lax.ppermute(v, axis, [(i, (i + by) % size) for i in range(size)])


def gather(own, c_one, c_two):
    east = lambda v: shift(v, "x", 4, 1)
    west = lambda v: shift(v, "x", 4, -1)
    across = lambda v: shift(v, "z_lo", 2, 1)
    z = across(own)
    one_w, two_w, one_e, two_e = east(c_one), east(c_two), west(c_one), west(c_two)
    own_w, own_e = east(own), west(own)
    z_w, z_e = east(z), west(z)
    one_o, two_o = east(one_w), west(two_e)
    own_o, z_o = east(own_w), west(z_e)
    main = (own, z, own_e, z_e, own_o, z_o, own_w, z_w)
    first = (c_one, one_e, one_o, one_w)
    second = (c_two, two_e, two_o, two_w)
    first = [b for v in first for b in (v, across(v))]
    second = [b for v in second for b in (v, across(v))]
    return main, first, second


def on_device(samples, window):
    table = jnp.asarray(table_rows())
    pieces = channelize(samples, window, table)
    arrived = lax.all_to_all(pieces, ("y", "z_hi", "core"), split_axis=0, concat_axis=0, tiled=True)
    parts = assemble(arrived.reshape(SPEC, 2 * CH, SPEC))
    gathered = gather(*parts)
    x, z = lax.axis_index("x"), lax.axis_index("z_lo")
    cols = jnp.stack([((x + dx) % 4 * 2 + (z + dz) % 2) * SPEC for dx in range(4) for dz in range(2)]).astype(jnp.int32)
    out = None
    for blocks, (lo, _) in reversed(list(zip(gathered, PARTS))):
        out = correlate(cols, blocks, lo, out)
    return tuple(out)


def solution(mesh):
    axes = ("x", "z_lo", "y", "z_hi", "core")
    fine = Mesh(mesh.devices.reshape(4, 2, 4, 4, 2), axes)
    return jax.shard_map(
        on_device,
        mesh=fine,
        in_specs=(P(axes, None), P()),
        out_specs=(P(axes[2:], axes[:2], None), P(axes[2:], axes[:2], None)),
        check_vma=False,
    )
```

time: 316 us -> 159 us (0.50)
  waiting for transfers between devices: 167 us -> 46.2 us
  other arithmetic: 26.5 us -> 0 us
  Pallas kernels: 0 us -> 24.3 us
  local copies, waits for them, and re-layouts: 47.5 us -> 26.1 us
  starting transfers between devices: 0.04 us -> 21.3 us
  matrix products: 20.1 us -> 0 us
  between operations: 14.1 us -> 0.75 us
    all_gather x1 -> x0, waiting for transfers between devices: 167 us -> none  [on_device(): lax.all_gather(own_block, 'grp', axis=0, tiled=True)]
    ppermute x0 -> x21, waiting for transfers between devices: none -> 46.2 us  [shift(): return lax.ppermute(v, axis, [(i, (i + by) % size) for i in range(size)])]
    pallas_call x0 -> x5, Pallas kernels: none -> 24.3 us  [the longest x3 16.5 us: correlate(): pl.pallas_call(correlate_kernel, out_shape=[shape, shape], grid_spec=pltp...]
    ppermute x0 -> x21, starting transfers between devices: none -> 21.3 us  [shift(): return lax.ppermute(v, axis, [(i, (i + by) % size) for i in range(size)])]
    dot_general x2 -> x0, matrix products: 20.1 us -> none  [the longest x1 10.1 us: on_device(): jnp.einsum('pack,bck->pcab', operands, lax.all_gather(own_block, 'grp', a...]
    another operation x3 -> x0, other arithmetic: 19.6 us -> none
    convert_element_type x4 -> x0, local copies, waits for them, and re-layouts: 14.3 us -> none  [the longest x1 7.17 us: dft_table(): return stacked.reshape(fft_len, 2 * chan_count).astype(jnp.bfloat16)]
    unnamed x4 -> x58, local copies, waits for them, and re-layouts: 12.8 us -> 26 us
  transfers between devices with their start and end apart: 1 -> 21, of which waited for: 1 -> 8; matrix products, arithmetic and copies ran while one was open for 1% -> 0% of each run, Pallas kernels for 0% -> 5%
where the time goes in v1:
time: 159 us; the launch traced here: 158 us
  waiting for transfers between devices  46.2 us (29%)
  blocking collectives  39.2 us (25%)
  local copies, waits for them, and re-layouts  26.1 us (16%)
  Pallas kernels  24.3 us (15%)
  starting transfers between devices  21.3 us (13%)
    ppermute x21, waiting for transfers between devices, shift(): return lax.ppermute(v, axis, [(i, (i + by) % size) for i in range(size)])  46.2 us
    all_to_all x1, blocking collectives, on_device(): lax.all_to_all(pieces, ('y', 'z_hi', 'core'), split_axis=0, concat_axis=0...  39.2 us
    unnamed x58, local copies, waits for them, and re-layouts  26 us
    ppermute x21, starting transfers between devices, shift(): return lax.ppermute(v, axis, [(i, (i + by) % size) for i in range(size)])  21.3 us
    pallas_call x3, Pallas kernels, correlate(): pl.pallas_call(correlate_kernel, out_shape=[shape, shape], grid_spec=pltp...  16.5 us
    pallas_call x1, Pallas kernels, channelize(): pl.pallas_call(channelize_kernel, out_shape=jax.ShapeDtypeStruct((N_FREQ,...  6.01 us
  transfers between devices with their start and end apart: 21, of which 8 were waited for; matrix products, arithmetic and copies ran while one was open for 0% of the time, Pallas kernels for 5%

profile of v1, /device:TPU:8, one launch (start us, length us, event | category | flops | bytes accessed | tf_op | source)
XLA Modules:
  0.0 157.8 jit_solution(15828321705382247872)
XLA Ops:
  0.6 2.2 %copy-done = s32[4,268288]{1,0:T(4,128)S(1)} copy-done((s32[4,268288]{1,0:T(4,128)S(1)}, s32[4,268288]{1,0:T(4,128)}, u32[]{:S(2)}) %copy-start) | copy-done | bytes 4292632
  2.8 2.2 %copy-done.1 = bf16[1024,2048]{1,0:T(8,128)(2,1)S(1)} copy-done((bf16[1024,2048]{1,0:T(8,128)(2,1)S(1)}, bf16[1024,2048]{1,0:T(8,128)(2,1)}, u32[]{:S(2)}) %copy-start.1) | copy-done | bytes 4194328
  5.0 0.8 copy-done.28
  5.8 6.0 %channelize.1 = bf16[32,4,32,128]{3,2,1,0:T(8,128)(2,1)S(1)} custom-call(s32[131,64,128]{2,1,0:T(8,128)S(1)} %bitcast.14, f32[4,2048]{1,0:T(4,128)S(1)} %copy-done.28, bf16[1024,2048]{1,0:T(8,128)(2,1)S(1)} %copy-done.1), custom_call_target="tpu_custom_call" | custom-call | flops 2147483648 | bytes 9437184 | tf_op jit(solution)/shard_map/channelize/pallas_call | solution.py:76
  11.8 39.2 %all_to_all.5 = bf16[32,4,32,128]{3,2,1,0:T(8,128)(2,1)S(1)} all-to-all(bf16[32,4,32,128]{3,2,1,0:T(8,128)(2,1)S(1)} %channelize.1), channel_id=1, replica_groups=mesh['x'=4,'z_lo'=2,'y'=4,'z_hi'=4,'core'=2] {'y','z_hi','core'}, dimensions={0} | all-to-all | bytes 2097152 | tf_op jit(solution)/shard_map/all_to_all | solution.py:180
  51.0 1.8 %assemble.1 = (bf16[10,128,256]{2,1,0:T(8,128)(2,1)S(1)}, bf16[3,128,256]{2,1,0:T(8,128)(2,1)S(1)}, bf16[3,128,256]{2,1,0:T(8,128)(2,1)S(1)}) custom-call(bf16[128,32,128]{2,1,0:T(8,128)(2,1)S(1)} %bitcast.15), custom_call_target="tpu_custom_call" | custom-call | bytes 2097152 | tf_op jit(solution)/shard_map/assemble/pallas_call | solution.py:107
  52.9 2.9 %collective-permute-start.15 = (bf16[3,128,256]{2,1,0:T(8,128)(2,1)S(1)}, bf16[3,128,256]{2,1,0:T(8,128)(2,1)S(1)}, u32[]{:S(2)}, u32[]{:S(2)}) collective-permute-start(bf16[3,128,256]{2,1,0:T(8,128)(2,1)S(1)} %get-tuple-element.11.refs_0_), channel_id=1, source_target_pairs={{0,192},{64,0},{128,64},{192,128},{1,193},{65,1},{129,65},{193,129... | collective-permute-start | bytes 589832 | tf_op jit(solution)/shard_map/ppermute | solution.py:156
  56.5 13.9 %collective-permute-done.refs_1_ = bf16[10,128,256]{2,1,0:T(8,128)(2,1)S(1)} collective-permute-done((bf16[10,128,256]{2,1,0:T(8,128)(2,1)S(1)}, bf16[10,128,256]{2,1,0:T(8,128)(2,1)S(1)}, u32[]{:S(2)}, u32[]{:S(2)}) %collective-permute-start) | collective-permute-done | bytes 655392 | tf_op jit(solution)/shard_map/ppermute | solution.py:156
  70.4 2.3 %collective-permute-start.2 = (bf16[10,128,256]{2,1,0:T(8,128)(2,1)S(1)}, bf16[10,128,256]{2,1,0:T(8,128)(2,1)S(1)}, u32[]{:S(2)}, u32[]{:S(2)}) collective-permute-start(bf16[10,128,256]{2,1,0:T(8,128)(2,1)S(1)} %collective-permute-done.refs_1_), channel_id=1, source_target_pairs={{0,192},{64,0},{128,64},{192,128},{1,193},{65,1},{129,65},{193,129... | collective-permute-start | bytes 1966088 | tf_op jit(solution)/shard_map/ppermute | solution.py:156
  72.8 3.2 %collective-permute-start.8 = (bf16[3,128,256]{2,1,0:T(8,128)(2,1)S(1)}, bf16[3,128,256]{2,1,0:T(8,128)(2,1)S(1)}, u32[]{:S(2)}, u32[]{:S(2)}) collective-permute-start(bf16[3,128,256]{2,1,0:T(8,128)(2,1)S(1)} %get-tuple-element.10.refs_0_), channel_id=1, source_target_pairs={{0,192},{64,0},{128,64},{192,128},{1,193},{65,1},{129,65},{193,129... | collective-permute-start | bytes 589832 | tf_op jit(solution)/shard_map/ppermute | solution.py:156
  76.0 2.9 %collective-permute-done.14.refs_1_ = bf16[3,128,256]{2,1,0:T(8,128)(2,1)S(1)} collective-permute-done((bf16[3,128,256]{2,1,0:T(8,128)(2,1)S(1)}, bf16[3,128,256]{2,1,0:T(8,128)(2,1)S(1)}, u32[]{:S(2)}, u32[]{:S(2)}) %collective-permute-start.14) | collective-permute-done | bytes 196640 | tf_op jit(solution)/shard_map/ppermute | solution.py:156
  78.9 0.7 copy-done.6
  79.5 1.1 collective-permute-start.7
  80.7 0.7 copy-done.16
  81.3 1.3 collective-permute-done.10.refs_6_
  82.6 9.6 %collective-permute-done.8.refs_2_ = bf16[3,128,256]{2,1,0:T(8,128)(2,1)S(1)} collective-permute-done((bf16[3,128,256]{2,1,0:T(8,128)(2,1)S(1)}, bf16[3,128,256]{2,1,0:T(8,128)(2,1)S(1)}, u32[]{:S(2)}, u32[]{:S(2)}) %collective-permute-start.8) | collective-permute-done | bytes 196640 | tf_op jit(solution)/shard_map/ppermute | solution.py:156
  92.2 0.7 copy-done.2
  92.9 0.7 copy-done.22
  93.6 2.0 %collective-permute-start.20 = (bf16[3,128,256]{2,1,0:T(8,128)(2,1)S(1)}, bf16[3,128,256]{2,1,0:T(8,128)(2,1)S(1)}, u32[]{:S(2)}, u32[]{:S(2)}) collective-permute-start(bf16[3,128,256]{2,1,0:T(8,128)(2,1)S(1)} %collective-permute-done.19.refs_6_), channel_id=1, source_target_pairs={{0,32},{32,0},{1,33},{33,1},{2,34},{34,2},{3,35},{35,3},{4,36},{36... | collective-permute-start | bytes 589832 | tf_op jit(solution)/shard_map/ppermute | solution.py:156
  96.3 1.5 collective-permute-start.11
  97.7 2.2 %collective-permute-done.16.refs_3_ = bf16[3,128,256]{2,1,0:T(8,128)(2,1)S(1)} collective-permute-done((bf16[3,128,256]{2,1,0:T(8,128)(2,1)S(1)}, bf16[3,128,256]{2,1,0:T(8,128)(2,1)S(1)}, u32[]{:S(2)}, u32[]{:S(2)}) %collective-permute-start.16) | collective-permute-done | bytes 196640 | tf_op jit(solution)/shard_map/ppermute | solution.py:156
  100.0 0.7 copy-done.10
  100.7 0.7 copy-done.18
  101.4 2.7 %collective-permute-done.20.refs_7_ = bf16[3,128,256]{2,1,0:T(8,128)(2,1)S(1)} collective-permute-done((bf16[3,128,256]{2,1,0:T(8,128)(2,1)S(1)}, bf16[3,128,256]{2,1,0:T(8,128)(2,1)S(1)}, u32[]{:S(2)}, u32[]{:S(2)}) %collective-permute-start.20) | collective-permute-done | bytes 196640 | tf_op jit(solution)/shard_map/ppermute | solution.py:156
  104.1 0.7 copy-done.12
  104.8 3.7 %collective-permute-start.1 = (bf16[10,128,256]{2,1,0:T(8,128)(2,1)S(1)}, bf16[10,128,256]{2,1,0:T(8,128)(2,1)S(1)}, u32[]{:S(2)}, u32[]{:S(2)}) collective-permute-start(bf16[10,128,256]{2,1,0:T(8,128)(2,1)S(1)} %get-tuple-element.9.refs_0_), channel_id=1, source_target_pairs={{0,192},{64,0},{128,64},{192,128},{1,193},{65,1},{129,65},{193,129... | collective-permute-start | bytes 1966088 | tf_op jit(solution)/shard_map/ppermute | solution.py:156
  108.6 3.2 %collective-permute-start.5 = (bf16[10,128,256]{2,1,0:T(8,128)(2,1)S(1)}, bf16[10,128,256]{2,1,0:T(8,128)(2,1)}, u32[]{:S(2)}, u32[]{:S(2)}) collective-permute-start(bf16[10,128,256]{2,1,0:T(8,128)(2,1)S(1)} %collective-permute-done.2.refs_3_), channel_id=1, source_target_pairs={{0,192},{64,0},{128,64},{192,128},{1,193},{65,1},{129,65},{193,129... | collective-permute-start | bytes 1966088 | tf_op jit(solution)/shard_map/ppermute | solution.py:156
  112.5 0.7 copy-done.20
  113.2 7.0 %collective-permute-done.9.refs_3_ = bf16[3,128,256]{2,1,0:T(8,128)(2,1)S(1)} collective-permute-done((bf16[3,128,256]{2,1,0:T(8,128)(2,1)S(1)}, bf16[3,128,256]{2,1,0:T(8,128)(2,1)S(1)}, u32[]{:S(2)}, u32[]{:S(2)}) %collective-permute-start.9) | collective-permute-done | bytes 196640 | tf_op jit(solution)/shard_map/ppermute | solution.py:156
  120.9 0.7 copy-done.8
  121.6 6.6 %collective-permute-done.18.refs_5_ = bf16[3,128,256]{2,1,0:T(8,128)(2,1)S(1)} collective-permute-done((bf16[3,128,256]{2,1,0:T(8,128)(2,1)S(1)}, bf16[3,128,256]{2,1,0:T(8,128)(2,1)S(1)}, u32[]{:S(2)}, u32[]{:S(2)}) %collective-permute-start.18) | collective-permute-done | bytes 196640 | tf_op jit(solution)/shard_map/ppermute | solution.py:156
  128.1 0.7 copy-done.14
  129.2 0.9 copy-done.3
  130.1 0.9 copy-done.5
  131.0 0.9 copy-done.7
  132.0 0.9 copy-done.9
  132.9 0.9 copy-done.11
  133.8 0.9 copy-done.13
  134.7 0.9 copy-done.15
  135.7 3.0 %correlate.3 = (bf16[16,128,1024]{2,1,0:T(8,128)(2,1)}, bf16[16,128,1024]{2,1,0:T(8,128)(2,1)}) custom-call(s32[8]{0:T(128)S(1)} %stack.35.col_ref, bf16[3,128,256]{2,1,0:T(8,128)(2,1)S(1)} %get-tuple-element.11.refs_0_, bf16[3,128,256]{2,1,0:T(8,128)(2,1)S(1)} %copy-done.7, bf16[3,128,256]{2,1,0:T(8,128)(2,1)S(1)} %copy-done.3, ...), custom_call_target="tpu_custom_call" | custom-call | flops 402653184 | bytes 3145728 | tf_op jit(solution)/shard_map/correlate/pallas_call | solution.py:139
  138.7 0.9 copy-done.17
  139.6 0.9 copy-done.19
  140.5 0.9 copy-done.21
  141.4 0.9 copy-done.23
  142.4 0.9 copy-done.25
  143.3 0.9 copy-done.27
  144.2 4.1 %correlate.4 = (bf16[16,128,1024]{2,1,0:T(8,128)(2,1)}, bf16[16,128,1024]{2,1,0:T(8,128)(2,1)}) custom-call(s32[8]{0:T(128)S(1)} %stack.35.col_ref, bf16[3,128,256]{2,1,0:T(8,128)(2,1)S(1)} %copy-done.17, bf16[3,128,256]{2,1,0:T(8,128)(2,1)S(1)} %copy-done.23, bf16[3,128,256]{2,1,0:T(8,128)(2,1)S(1)} %copy-done.21, ...), custom_call_target="tpu_custom_call", output_to_operand_aliasing={{0}: (9, {}), {1}: (10, {})} | custom-call | flops 402653184 | bytes 3145728 | tf_op jit(solution)/shard_map/correlate/pallas_call | solution.py:139
  148.4 9.4 %correlate.5 = (bf16[16,128,1024]{2,1,0:T(8,128)(2,1)}, bf16[16,128,1024]{2,1,0:T(8,128)(2,1)}) custom-call(s32[8]{0:T(128)S(1)} %stack.35.col_ref, bf16[10,128,256]{2,1,0:T(8,128)(2,1)S(1)} %get-tuple-element.9.refs_0_, bf16[10,128,256]{2,1,0:T(8,128)(2,1)S(1)} %collective-permute-done.refs_1_, ...), custom_call_target="tpu_custom_call", output_to_operand_aliasing={{0}: (9, {}), {1}: (10, {})} | custom-call | flops 1342177280 | bytes 10485760 | tf_op jit(solution)/shard_map/correlate/pallas_call | solution.py:139
  (59 shorter events, 3.4 us)
Async XLA Ops:
  0.6 2.2 %copy-start = (s32[4,268288]{1,0:T(4,128)S(1)}, s32[4,268288]{1,0:T(4,128)}, u32[]{:S(2)}) copy-start(s32[4,268288]{1,0:T(4,128)} %param.3) | copy-start | bytes 12877828
  2.8 2.2 %copy-start.1 = (bf16[1024,2048]{1,0:T(8,128)(2,1)S(1)}, bf16[1024,2048]{1,0:T(8,128)(2,1)}, u32[]{:S(2)}) copy-start(bf16[1024,2048]{1,0:T(8,128)(2,1)} %constant.77.clone.t_ref) | copy-start | bytes 12582916
  5.0 0.8 copy-start.28
  52.8 17.6 %collective-permute-start = (bf16[10,128,256]{2,1,0:T(8,128)(2,1)S(1)}, bf16[10,128,256]{2,1,0:T(8,128)(2,1)S(1)}, u32[]{:S(2)}, u32[]{:S(2)}) collective-permute-start(bf16[10,128,256]{2,1,0:T(8,128)(2,1)S(1)} %get-tuple-element.9.refs_0_), channel_id=1, source_target_pairs={{0,32},{32,0},{1,33},{33,1},{2,34},{34,2},{3,35},{35,3},{4,36},{36... | collective-permute-start | bytes 1966088 | tf_op jit(solution)/shard_map/ppermute | solution.py:156
  52.9 19.9 %collective-permute-start.15 = (bf16[3,128,256]{2,1,0:T(8,128)(2,1)S(1)}, bf16[3,128,256]{2,1,0:T(8,128)(2,1)S(1)}, u32[]{:S(2)}, u32[]{:S(2)}) collective-permute-start(bf16[3,128,256]{2,1,0:T(8,128)(2,1)S(1)} %get-tuple-element.11.refs_0_), channel_id=1, source_target_pairs={{0,192},{64,0},{128,64},{192,128},{1,193},{65,1},{129,65},{193,129... | collective-permute-start | bytes 589832 | tf_op jit(solution)/shard_map/ppermute | solution.py:156
  55.8 16.9 %collective-permute-start.19 = (bf16[3,128,256]{2,1,0:T(8,128)(2,1)S(1)}, bf16[3,128,256]{2,1,0:T(8,128)(2,1)S(1)}, u32[]{:S(2)}, u32[]{:S(2)}) collective-permute-start(bf16[3,128,256]{2,1,0:T(8,128)(2,1)S(1)} %get-tuple-element.11.refs_0_), channel_id=1, source_target_pairs={{0,64},{64,128},{128,192},{192,0},{1,65},{65,129},{129,193},{193,1... | collective-permute-start | bytes 589832 | tf_op jit(solution)/shard_map/ppermute | solution.py:156
  55.8 52.6 %collective-permute-start.3 = (bf16[10,128,256]{2,1,0:T(8,128)(2,1)S(1)}, bf16[10,128,256]{2,1,0:T(8,128)(2,1)S(1)}, u32[]{:S(2)}, u32[]{:S(2)}) collective-permute-start(bf16[10,128,256]{2,1,0:T(8,128)(2,1)S(1)} %get-tuple-element.9.refs_0_), channel_id=1, source_target_pairs={{0,64},{64,128},{128,192},{192,0},{1,65},{65,129},{129,193},{193,1... | collective-permute-start | bytes 1966088 | tf_op jit(solution)/shard_map/ppermute | solution.py:156
  70.4 38.1 %collective-permute-start.2 = (bf16[10,128,256]{2,1,0:T(8,128)(2,1)S(1)}, bf16[10,128,256]{2,1,0:T(8,128)(2,1)S(1)}, u32[]{:S(2)}, u32[]{:S(2)}) collective-permute-start(bf16[10,128,256]{2,1,0:T(8,128)(2,1)S(1)} %collective-permute-done.refs_1_), channel_id=1, source_target_pairs={{0,192},{64,0},{128,64},{192,128},{1,193},{65,1},{129,65},{193,129... | collective-permute-start | bytes 1966088 | tf_op jit(solution)/shard_map/ppermute | solution.py:156
  72.7 6.1 %collective-permute-start.14 = (bf16[3,128,256]{2,1,0:T(8,128)(2,1)S(1)}, bf16[3,128,256]{2,1,0:T(8,128)(2,1)S(1)}, u32[]{:S(2)}, u32[]{:S(2)}) collective-permute-start(bf16[3,128,256]{2,1,0:T(8,128)(2,1)S(1)} %get-tuple-element.11.refs_0_), channel_id=1, source_target_pairs={{0,32},{32,0},{1,33},{33,1},{2,34},{34,2},{3,35},{35,3},{4,36},{36... | collective-permute-start | bytes 589832 | tf_op jit(solution)/shard_map/ppermute | solution.py:156
  72.8 9.9 %collective-permute-start.10 = (bf16[3,128,256]{2,1,0:T(8,128)(2,1)S(1)}, bf16[3,128,256]{2,1,0:T(8,128)(2,1)S(1)}, u32[]{:S(2)}, u32[]{:S(2)}) collective-permute-start(bf16[3,128,256]{2,1,0:T(8,128)(2,1)S(1)} %get-tuple-element.10.refs_0_), channel_id=1, source_target_pairs={{0,64},{64,128},{128,192},{192,0},{1,65},{65,129},{129,193},{193,1... | collective-permute-start | bytes 589832 | tf_op jit(solution)/shard_map/ppermute | solution.py:156
  72.8 19.4 %collective-permute-start.8 = (bf16[3,128,256]{2,1,0:T(8,128)(2,1)S(1)}, bf16[3,128,256]{2,1,0:T(8,128)(2,1)S(1)}, u32[]{:S(2)}, u32[]{:S(2)}) collective-permute-start(bf16[3,128,256]{2,1,0:T(8,128)(2,1)S(1)} %get-tuple-element.10.refs_0_), channel_id=1, source_target_pairs={{0,192},{64,0},{128,64},{192,128},{1,193},{65,1},{129,65},{193,129... | collective-permute-start | bytes 589832 | tf_op jit(solution)/shard_map/ppermute | solution.py:156
  78.9 0.7 copy-start.6
  79.5 13.4 %collective-permute-start.7 = (bf16[3,128,256]{2,1,0:T(8,128)(2,1)S(1)}, bf16[3,128,256]{2,1,0:T(8,128)(2,1)S(1)}, u32[]{:S(2)}, u32[]{:S(2)}) collective-permute-start(bf16[3,128,256]{2,1,0:T(8,128)(2,1)S(1)} %get-tuple-element.10.refs_0_), channel_id=1, source_target_pairs={{0,32},{32,0},{1,33},{33,1},{2,34},{34,2},{3,35},{35,3},{4,36},{36... | collective-permute-start | bytes 589832 | tf_op jit(solution)/shard_map/ppermute | solution.py:156
  80.7 0.7 copy-start.16
  82.6 13.6 %collective-permute-start.17 = (bf16[3,128,256]{2,1,0:T(8,128)(2,1)S(1)}, bf16[3,128,256]{2,1,0:T(8,128)(2,1)S(1)}, u32[]{:S(2)}, u32[]{:S(2)}) collective-permute-start(bf16[3,128,256]{2,1,0:T(8,128)(2,1)S(1)} %collective-permute-done.15.refs_2_), channel_id=1, source_target_pairs={{0,192},{64,0},{128,64},{192,128},{1,193},{65,1},{129,65},{193,129... | collective-permute-start | bytes 589832 | tf_op jit(solution)/shard_map/ppermute | solution.py:156
  92.2 7.8 %collective-permute-start.16 = (bf16[3,128,256]{2,1,0:T(8,128)(2,1)S(1)}, bf16[3,128,256]{2,1,0:T(8,128)(2,1)S(1)}, u32[]{:S(2)}, u32[]{:S(2)}) collective-permute-start(bf16[3,128,256]{2,1,0:T(8,128)(2,1)S(1)} %collective-permute-done.15.refs_2_), channel_id=1, source_target_pairs={{0,32},{32,0},{1,33},{33,1},{2,34},{34,2},{3,35},{35,3},{4,36},{36... | collective-permute-start | bytes 589832 | tf_op jit(solution)/shard_map/ppermute | solution.py:156
  92.2 0.7 copy-start.2
  92.9 0.7 copy-start.22
  93.6 10.5 %collective-permute-start.20 = (bf16[3,128,256]{2,1,0:T(8,128)(2,1)S(1)}, bf16[3,128,256]{2,1,0:T(8,128)(2,1)S(1)}, u32[]{:S(2)}, u32[]{:S(2)}) collective-permute-start(bf16[3,128,256]{2,1,0:T(8,128)(2,1)S(1)} %collective-permute-done.19.refs_6_), channel_id=1, source_target_pairs={{0,32},{32,0},{1,33},{33,1},{2,34},{34,2},{3,35},{35,3},{4,36},{36... | collective-permute-start | bytes 589832 | tf_op jit(solution)/shard_map/ppermute | solution.py:156
  96.3 12.2 %collective-permute-start.11 = (bf16[3,128,256]{2,1,0:T(8,128)(2,1)S(1)}, bf16[3,128,256]{2,1,0:T(8,128)(2,1)}, u32[]{:S(2)}, u32[]{:S(2)}) collective-permute-start(bf16[3,128,256]{2,1,0:T(8,128)(2,1)S(1)} %collective-permute-done.10.refs_6_), channel_id=1, source_target_pairs={{0,64},{64,128},{128,192},{192,0},{1,65},{65,129},{129,193},{193,1... | collective-permute-start | bytes 589832 | tf_op jit(solution)/shard_map/ppermute | solution.py:156
  100.0 0.7 copy-start.10
  100.7 11.1 %collective-permute-start.13 = (bf16[3,128,256]{2,1,0:T(8,128)(2,1)S(1)}, bf16[3,128,256]{2,1,0:T(8,128)(2,1)S(1)}, u32[]{:S(2)}, u32[]{:S(2)}) collective-permute-start(bf16[3,128,256]{2,1,0:T(8,128)(2,1)S(1)} %collective-permute-done.10.refs_6_), channel_id=1, source_target_pairs={{0,32},{32,0},{1,33},{33,1},{2,34},{34,2},{3,35},{35,3},{4,36},{36... | collective-permute-start | bytes 589832 | tf_op jit(solution)/shard_map/ppermute | solution.py:156
  100.7 0.7 copy-start.18
  104.1 0.7 copy-start.12
  104.8 43.6 %collective-permute-start.1 = (bf16[10,128,256]{2,1,0:T(8,128)(2,1)S(1)}, bf16[10,128,256]{2,1,0:T(8,128)(2,1)S(1)}, u32[]{:S(2)}, u32[]{:S(2)}) collective-permute-start(bf16[10,128,256]{2,1,0:T(8,128)(2,1)S(1)} %get-tuple-element.9.refs_0_), channel_id=1, source_target_pairs={{0,192},{64,0},{128,64},{192,128},{1,193},{65,1},{129,65},{193,129... | collective-permute-start | bytes 1966088 | tf_op jit(solution)/shard_map/ppermute | solution.py:156
  108.5 39.9 %collective-permute-start.6 = (bf16[10,128,256]{2,1,0:T(8,128)(2,1)S(1)}, bf16[10,128,256]{2,1,0:T(8,128)(2,1)}, u32[]{:S(2)}, u32[]{:S(2)}) collective-permute-start(bf16[10,128,256]{2,1,0:T(8,128)(2,1)S(1)} %collective-permute-done.refs_1_), channel_id=1, source_target_pairs={{0,64},{64,128},{128,192},{192,0},{1,65},{65,129},{129,193},{193,1... | collective-permute-start | bytes 1966088 | tf_op jit(solution)/shard_map/ppermute | solution.py:156
  108.5 39.9 %collective-permute-start.4 = (bf16[10,128,256]{2,1,0:T(8,128)(2,1)S(1)}, bf16[10,128,256]{2,1,0:T(8,128)(2,1)}, u32[]{:S(2)}, u32[]{:S(2)}) collective-permute-start(bf16[10,128,256]{2,1,0:T(8,128)(2,1)S(1)} %collective-permute-done.3.refs_6_), channel_id=1, source_target_pairs={{0,64},{64,128},{128,192},{192,0},{1,65},{65,129},{129,193},{193,1... | collective-permute-start | bytes 1966088 | tf_op jit(solution)/shard_map/ppermute | solution.py:156
  108.6 39.8 %collective-permute-start.5 = (bf16[10,128,256]{2,1,0:T(8,128)(2,1)S(1)}, bf16[10,128,256]{2,1,0:T(8,128)(2,1)}, u32[]{:S(2)}, u32[]{:S(2)}) collective-permute-start(bf16[10,128,256]{2,1,0:T(8,128)(2,1)S(1)} %collective-permute-done.2.refs_3_), channel_id=1, source_target_pairs={{0,192},{64,0},{128,64},{192,128},{1,193},{65,1},{129,65},{193,129... | collective-permute-start | bytes 1966088 | tf_op jit(solution)/shard_map/ppermute | solution.py:156
  111.8 0.7 copy-start.24
  112.5 7.8 %collective-permute-start.9 = (bf16[3,128,256]{2,1,0:T(8,128)(2,1)S(1)}, bf16[3,128,256]{2,1,0:T(8,128)(2,1)S(1)}, u32[]{:S(2)}, u32[]{:S(2)}) collective-permute-start(bf16[3,128,256]{2,1,0:T(8,128)(2,1)S(1)} %collective-permute-done.8.refs_2_), channel_id=1, source_target_pairs={{0,32},{32,0},{1,33},{33,1},{2,34},{34,2},{3,35},{35,3},{4,36},{36... | collective-permute-start | bytes 589832 | tf_op jit(solution)/shard_map/ppermute | solution.py:156
  112.5 0.7 copy-start.20
  120.9 7.2 %collective-permute-start.18 = (bf16[3,128,256]{2,1,0:T(8,128)(2,1)S(1)}, bf16[3,128,256]{2,1,0:T(8,128)(2,1)S(1)}, u32[]{:S(2)}, u32[]{:S(2)}) collective-permute-start(bf16[3,128,256]{2,1,0:T(8,128)(2,1)S(1)} %collective-permute-done.17.refs_4_), channel_id=1, source_target_pairs={{0,32},{32,0},{1,33},{33,1},{2,34},{34,2},{3,35},{35,3},{4,36},{36... | collective-permute-start | bytes 589832 | tf_op jit(solution)/shard_map/ppermute | solution.py:156
  120.9 0.7 copy-start.8
  128.1 0.7 copy-start.14
  128.8 9.9 %collective-permute-start.12 = (bf16[3,128,256]{2,1,0:T(8,128)(2,1)}, bf16[3,128,256]{2,1,0:T(8,128)(2,1)}, u32[]{:S(2)}, u32[]{:S(2)}) collective-permute-start(bf16[3,128,256]{2,1,0:T(8,128)(2,1)} %collective-permute-done.11.refs_4_), channel_id=1, source_target_pairs={{0,32},{32,0},{1,33},{33,1},{2,34},{34,2},{3,35},{35,3},{4,36},{36... | collective-permute-start | bytes 589832 | tf_op jit(solution)/shard_map/ppermute | solution.py:156
  129.2 0.9 copy-start.3
  130.1 0.9 copy-start.5
  131.0 0.9 copy-start.7
  132.0 0.9 copy-start.9
  132.9 0.9 copy-start.11
  133.8 0.9 copy-start.13
  134.7 0.9 copy-start.15
  138.7 0.9 copy-start.17
  139.6 0.9 copy-start.19
  140.5 0.9 copy-start.21
  141.4 0.9 copy-start.23
  142.4 0.9 copy-start.25
  143.3 0.9 copy-start.27
  (2 other events, 1.3 us)

commit v2 on v1

v2 whole, which is shorter than its diff:
```python
import math

import jax
import jax.numpy as jnp
import ml_dtypes
import numpy as np
from jax import lax
from jax.experimental import pallas as pl
from jax.experimental.pallas import tpu as pltpu
from jax.sharding import Mesh, PartitionSpec as P

CHAN = 512
NFFT = 2048
TAPS = 4
SPEC = 128
FRAMES = SPEC + TAPS - 1
ROWS_IN = 4
GROUPS = 8
N_FREQ = 32
CH = CHAN // N_FREQ
LANES = 128
SUB = 8
F32 = jnp.float32
BF16 = jnp.bfloat16
NT = (((1,), (1,)), ((), ()))
MIB = 1 << 20
FREQ = ("y", "z_hi", "core")

CHUNKS = ((6, 2), (5, 3))
STARTS = (0, 8)


def table_rows(lo, count):
    j = np.arange(NFFT, dtype=np.int64)
    c = (np.arange(N_FREQ)[:, None] * CH + lo + np.arange(count)[None, :]).reshape(-1)
    angle = ((c[:, None] * j[None, :]) % NFFT).astype(np.float32) * np.float32(2.0 * math.pi / NFFT)
    both = np.stack([np.cos(angle), -np.sin(angle)], axis=0)
    both = both.reshape(2, N_FREQ, count, NFFT).transpose(1, 0, 2, 3)
    return jnp.asarray(both.reshape(2 * N_FREQ * count, NFFT).astype(ml_dtypes.bfloat16))


def store_spectra(raw, o_ref, first, per):
    out = (raw * (1.0 / math.sqrt(NFFT))).astype(BF16)
    for d in range(raw.shape[0] // per):
        for i in range(ROWS_IN):
            o_ref[first + d, i] = out[d * per : (d + 1) * per, i * SPEC : (i + 1) * SPEC]


def filter_kernel(rows, s_hbm, w_ref, t_hbm, o_ref, f_hbm, s_ref, t_ref, f_ref, wv_ref, s_sem, t_sem, f_sem):
    parts = 4
    span = SPEC // parts
    edges = [0] + [(h + 1) * span + TAPS - 1 for h in range(parts)]
    arrivals = []
    for h in range(parts):
        cut = pl.ds(edges[h], edges[h + 1] - edges[h])
        arrivals.append(pltpu.make_async_copy(s_hbm.at[cut], s_ref.at[cut], s_sem.at[h]))
    for copy in arrivals:
        copy.start()
    table_copy = pltpu.make_async_copy(t_hbm, t_ref, t_sem)
    table_copy.start()
    pairs = NFFT // LANES // 2
    for a in range(pairs):
        for t in range(TAPS):
            halves = [
                jnp.broadcast_to(w_ref[t : t + 1, (2 * a + b) * LANES : (2 * a + b + 1) * LANES] * (1.0 / 64.0), (ROWS_IN, LANES))
                for b in range(2)
            ]
            wv_ref[a, t] = jnp.concatenate(halves, axis=0)
    for h in range(parts):
        arrivals[h].wait()

        def step(a, carry):
            sub = pl.ds(pl.multiple_of(a * SUB, SUB), SUB)
            taps = [wv_ref[a, t] for t in range(TAPS)]
            for s0 in range(h * span, (h + 1) * span, 2 * SUB):
                v = [s_ref[s0 + k, sub, :].astype(F32) for k in range(2 * SUB + TAPS - 1)]
                sums = []
                for k in range(2 * SUB):
                    acc = taps[0] * v[k]
                    for t in range(1, TAPS):
                        acc = acc + taps[t] * v[k + t]
                    sums.append(acc)
                low = jnp.swapaxes(jnp.stack(sums[:SUB], axis=0), 0, 1)
                high = jnp.swapaxes(jnp.stack(sums[SUB:], axis=0), 0, 1)
                both = jnp.concatenate([low, high], axis=1).astype(BF16)
                for b in range(2):
                    lane = pl.ds(pl.multiple_of((2 * a + b) * LANES, LANES), LANES)
                    for i in range(ROWS_IN):
                        f_ref[i * SPEC + s0 : i * SPEC + s0 + 2 * SUB, lane] = both[b * ROWS_IN + i]
            return carry

        lax.fori_loop(0, pairs, step, 0)
    out_copy = pltpu.make_async_copy(f_ref, f_hbm, f_sem)
    out_copy.start()
    table_copy.wait()
    tile = 256
    per = rows // N_FREQ
    for m in range(rows // tile):
        raw = lax.dot_general(t_ref[m * tile : (m + 1) * tile, :], f_ref[...], NT, preferred_element_type=F32)
        store_spectra(raw, o_ref, m * (tile // per), per)
    out_copy.wait()


def filter_and_transform(samples, window, table):
    view = samples.reshape(ROWS_IN, FRAMES, NFFT // LANES, LANES).transpose(1, 2, 0, 3)
    view = view.reshape(FRAMES, NFFT // LANES * ROWS_IN, LANES)
    rows = table.shape[0]
    return pl.pallas_call(
        lambda *refs: filter_kernel(rows, *refs),
        out_shape=[
            jax.ShapeDtypeStruct((N_FREQ, ROWS_IN, rows // N_FREQ, SPEC), BF16),
            jax.ShapeDtypeStruct((ROWS_IN * SPEC, NFFT), BF16),
        ],
        in_specs=[
            pl.BlockSpec(memory_space=pl.ANY),
            pl.BlockSpec(memory_space=pltpu.VMEM),
            pl.BlockSpec(memory_space=pl.ANY),
        ],
        out_specs=[pl.BlockSpec(memory_space=pltpu.VMEM), pl.BlockSpec(memory_space=pl.ANY)],
        scratch_shapes=[
            pltpu.VMEM((FRAMES, NFFT // LANES * ROWS_IN, LANES), jnp.int32),
            pltpu.VMEM((rows, NFFT), BF16),
            pltpu.VMEM((ROWS_IN * SPEC, NFFT), BF16),
            pltpu.VMEM((NFFT // LANES // 2, TAPS, SUB, LANES), F32),
            pltpu.SemaphoreType.DMA((4,)),
            pltpu.SemaphoreType.DMA,
            pltpu.SemaphoreType.DMA,
        ],
        compiler_params=pltpu.CompilerParams(vmem_limit_bytes=60 * MIB),
        cost_estimate=pl.CostEstimate(flops=2 * rows * 512 * 2048, bytes_accessed=9 * MIB, transcendentals=0),
        name="filter_and_transform",
    )(view, window, table)


def transform_kernel(per, f_ref, t_ref, o_ref):
    raw = lax.dot_general(t_ref[...], f_ref[...], NT, preferred_element_type=F32)
    store_spectra(raw, o_ref, 0, per)


def transform(filtered, table):
    rows, tile = table.shape[0], 256
    per = rows // N_FREQ
    return pl.pallas_call(
        lambda *refs: transform_kernel(per, *refs),
        out_shape=jax.ShapeDtypeStruct((N_FREQ, ROWS_IN, per, SPEC), BF16),
        grid=(rows // tile,),
        in_specs=[pl.BlockSpec((ROWS_IN * SPEC, NFFT), lambda g: (0, 0)), pl.BlockSpec((tile, NFFT), lambda g: (g, 0))],
        out_specs=pl.BlockSpec((tile // per, ROWS_IN, per, SPEC), lambda g: (g, 0, 0, 0)),
        compiler_params=pltpu.CompilerParams(vmem_limit_bytes=12 * MIB),
        cost_estimate=pl.CostEstimate(flops=2 * rows * 512 * 2048, bytes_accessed=5 * MIB, transcendentals=0),
        name="transform",
    )(filtered, table)


def assemble_kernel(sizes, x_ref, *refs):
    outs, wide = refs[:-1], refs[-1]
    count = sum(sizes)
    wide[...] = x_ref[...].reshape(SPEC * 2 * count, SPEC).astype(F32)
    lo = 0
    for out, size in zip(outs, sizes):
        for c in range(size):
            for p in range(2):
                rows = pl.ds(p * count + lo + c, SPEC, stride=2 * count)
                out[c, :, p * SPEC : (p + 1) * SPEC] = wide[rows, :].astype(BF16)
        lo += size


def assemble(pieces, sizes):
    count = sum(sizes)
    return pl.pallas_call(
        lambda *refs: assemble_kernel(sizes, *refs),
        out_shape=[jax.ShapeDtypeStruct((size, SPEC, 2 * SPEC), BF16) for size in sizes],
        scratch_shapes=[pltpu.VMEM((SPEC * 2 * count, SPEC), F32)],
        compiler_params=pltpu.CompilerParams(vmem_limit_bytes=6 * MIB),
        cost_estimate=pl.CostEstimate(flops=0, bytes_accessed=2 * MIB, transcendentals=0),
        name="assemble",
    )(pieces.reshape(SPEC, 2 * count, SPEC))


def correlate_kernel(col_ref, *refs):
    blocks, (re_ref, im_ref) = refs[:GROUPS], refs[-2:]
    c = pl.program_id(0)
    own = blocks[0][c]
    rotated = jnp.concatenate([own[:, SPEC:], -own[:, :SPEC]], axis=1)
    left = jnp.concatenate([own, rotated], axis=0)
    for b in range(0, GROUPS, 2):
        right = jnp.concatenate([blocks[b][c], blocks[b + 1][c]], axis=0)
        prod = lax.dot_general(left, right, NT, preferred_element_type=F32) * (1.0 / SPEC)
        for h in range(2):
            cols = pl.ds(pl.multiple_of(col_ref[b + h], SPEC), SPEC)
            re_ref[0, :, cols] = prod[:SPEC, h * SPEC : (h + 1) * SPEC].astype(BF16)
            im_ref[0, :, cols] = prod[SPEC:, h * SPEC : (h + 1) * SPEC].astype(BF16)


def correlate(cols, blocks, lo, earlier):
    count, width = blocks[0].shape[0], SPEC * GROUPS
    shape = jax.ShapeDtypeStruct((CH, SPEC, width), BF16)
    in_specs = [pl.BlockSpec(memory_space=pltpu.VMEM) for _ in blocks]
    operands = list(blocks)
    aliases = {}
    if earlier is not None:
        in_specs += [pl.BlockSpec(memory_space=pl.ANY)] * 2
        operands += list(earlier)
        aliases = {1 + GROUPS: 0, 2 + GROUPS: 1}
    return pl.pallas_call(
        correlate_kernel,
        out_shape=[shape, shape],
        grid_spec=pltpu.PrefetchScalarGridSpec(
            num_scalar_prefetch=1,
            grid=(count,),
            in_specs=in_specs,
            out_specs=[pl.BlockSpec((1, SPEC, width), lambda c, s: (c + lo, 0, 0))] * 2,
        ),
        input_output_aliases=aliases,
        compiler_params=pltpu.CompilerParams(vmem_limit_bytes=8 * MIB),
        cost_estimate=pl.CostEstimate(flops=count * 2 * 256 * 256 * 1024, bytes_accessed=count * MIB, transcendentals=0),
        name="correlate",
    )(cols, *operands)


class Queue:
    def __init__(self, axis, size, by, depth):
        self.axis, self.pairs, self.depth = axis, [(i, (i + by) % size) for i in range(size)], depth
        self.ended = []

    def send(self, value):
        if len(self.ended) >= self.depth:
            value, _ = lax.optimization_barrier((value, self.ended[-self.depth]))
        self.ended.append(lax.ppermute(value, self.axis, self.pairs))
        return self.ended[-1]


def exchange(pieces):
    return lax.all_to_all(pieces, FREQ, split_axis=0, concat_axis=0, tiled=True)


def on_device(samples, window):
    tables = [table_rows(lo, sum(sizes)) for lo, sizes in zip(STARTS, CHUNKS)]
    x, z = lax.axis_index("x"), lax.axis_index("z_lo")
    cols = jnp.stack([((x + dx) % 4 * 2 + (z + dz) % 2) * SPEC for dx in range(4) for dz in range(2)]).astype(jnp.int32)
    up, down, across = Queue("x", 4, 1, 2), Queue("x", 4, -1, 2), Queue("z_lo", 2, 1, 1)

    pieces, filtered = filter_and_transform(samples, window, tables[0])
    arrived = exchange(pieces)
    main, late = assemble(arrived, CHUNKS[0])
    filtered, _ = lax.optimization_barrier((filtered, main))
    arrived = exchange(transform(filtered, tables[1]))

    def gather(main, late, late_first):
        z_main = across.send(main)
        if late_first:
            late_m, late_p = up.send(late), down.send(late)
        main_m, main_p = up.send(main), down.send(main)
        if not late_first:
            late_m, late_p = up.send(late), down.send(late)
            late_o = None
        else:
            late_o = down.send(late_p)
        z_late = across.send(late)
        z_m, z_p = up.send(z_main), down.send(z_main)
        z_late_m, z_late_p = across.send(late_m), across.send(late_p)
        main_o, z_o = up.send(main_m), down.send(z_p)
        if late_o is None:
            late_o = up.send(late_m)
        z_late_o = across.send(late_o)
        return (
            (main, z_main, main_p, z_p, main_o, z_o, main_m, z_m),
            (late, z_late, late_p, z_late_p, late_o, z_late_o, late_m, z_late_m),
        )

    first = gather(main, late, False)
    main, late = assemble(arrived, CHUNKS[1])
    second = gather(main, late, True)
    out = None
    for blocks, lo, sizes in ((first, STARTS[0], CHUNKS[0]), (second, STARTS[1], CHUNKS[1])):
        out = correlate(cols, blocks[0], lo, out)
        out = correlate(cols, blocks[1], lo + sizes[0], out)
    return tuple(out)


def solution(mesh):
    axes = ("x", "z_lo") + FREQ
    fine = Mesh(mesh.devices.reshape(4, 2, 4, 4, 2), axes)
    return jax.shard_map(
        on_device,
        mesh=fine,
        in_specs=(P(axes, None), P()),
        out_specs=(P(FREQ, axes[:2], None), P(FREQ, axes[:2], None)),
        check_vma=False,
    )
```

time: 159 us -> 143 us (0.90)
  local copies, waits for them, and re-layouts: 26.1 us -> 14.6 us
  blocking collectives: 39.2 us -> 28.2 us
  starting transfers between devices: 21.3 us -> 31.5 us
  waiting for transfers between devices: 46.2 us -> 40.2 us
  Pallas kernels: 24.3 us -> 27 us
    unnamed x58 -> x52, local copies, waits for them, and re-layouts: 26 us -> 14.5 us
    all_to_all x1, blocking collectives: 39.2 us -> 28.2 us  [exchange(): return lax.all_to_all(pieces, FREQ, split_axis=0, concat_axis=0, tiled=True)]
    all_to_all x0 -> x1, starting transfers between devices: none -> 6.07 us  [exchange(): return lax.all_to_all(pieces, FREQ, split_axis=0, concat_axis=0, tiled=True)]
    ppermute x21 -> x28, waiting for transfers between devices: 46.2 us -> 40.2 us  [send(): self.ended.append(lax.ppermute(value, self.axis, self.pairs))]
    ppermute x21 -> x28, starting transfers between devices: 21.3 us -> 25.4 us  [send(): self.ended.append(lax.ppermute(value, self.axis, self.pairs))]
    pallas_call x2 -> x4, Pallas kernels: 7.8 us -> 9.52 us  [the longest x1 6.49 us: filter_and_transform(): pl.pallas_call(lambda *refs: filter_kernel(rows, *refs), out_shape=[jax.S...]
    pallas_call x3 -> x4, Pallas kernels: 16.5 us -> 17.5 us  [correlate(): pl.pallas_call(correlate_kernel, out_shape=[shape, shape], grid_spec=pltp...]
  transfers between devices with their start and end apart: 21 -> 29, of which waited for: 8 -> 12; matrix products, arithmetic and copies ran while one was open for 0% -> 0% of each run, Pallas kernels for 5% -> 11%
where the time goes in v2:
time: 143 us; the launch traced here: 142 us
  waiting for transfers between devices  40.2 us (28%)
  starting transfers between devices  31.5 us (22%)
  blocking collectives  28.2 us (20%)
  Pallas kernels  27 us (19%)
  local copies, waits for them, and re-layouts  14.6 us (10%)
    ppermute x28, waiting for transfers between devices, send(): self.ended.append(lax.ppermute(value, self.axis, self.pairs))  40.2 us
    all_to_all x1, blocking collectives, exchange(): return lax.all_to_all(pieces, FREQ, split_axis=0, concat_axis=0, tiled=True)  28.2 us
    ppermute x28, starting transfers between devices, send(): self.ended.append(lax.ppermute(value, self.axis, self.pairs))  25.4 us
    pallas_call x4, Pallas kernels, correlate(): pl.pallas_call(correlate_kernel, out_shape=[shape, shape], grid_spec=pltp...  17.5 us
    unnamed x52, local copies, waits for them, and re-layouts  14.5 us
    pallas_call x1, Pallas kernels, filter_and_transform(): pl.pallas_call(lambda *refs: filter_kernel(rows, *refs), out_shape=[jax.S...  6.49 us
    all_to_all x1, starting transfers between devices, exchange(): return lax.all_to_all(pieces, FREQ, split_axis=0, concat_axis=0, tiled=True)  6.07 us
  transfers between devices with their start and end apart: 29, of which 12 were waited for; matrix products, arithmetic and copies ran while one was open for 0% of the time, Pallas kernels for 11%

profile of v2, /device:TPU:8, one launch (start us, length us, event | category | flops | bytes accessed | tf_op | source)
XLA Modules:
  0.0 142.4 jit_solution(17503306956027603714)
XLA Ops:
  0.6 6.5 %filter_and_transform.1 = (bf16[32,4,16,128]{3,2,1,0:T(8,128)(2,1)}, bf16[512,2048]{1,0:T(8,128)(2,1)}) custom-call(s32[131,64,128]{2,1,0:T(8,128)} %bitcast.17, f32[4,2048]{1,0:T(4,128)} %refs_1_.2, bf16[512,2048]{1,0:T(8,128)(2,1)} %constant.79.clone.refs_2_), custom_call_target="tpu_custom_call" | custom-call | flops 1073741824 | bytes 9437184 | tf_op jit(solution)/shard_map/filter_and_transform/pallas_call | solution.py:108
  7.1 28.2 %all_to_all.10 = bf16[32,4,16,128]{3,2,1,0:T(8,128)(2,1)S(1)} all-to-all(bf16[32,4,16,128]{3,2,1,0:T(8,128)(2,1)} %get-tuple-element.39), channel_id=1, replica_groups=mesh['x'=4,'z_lo'=2,'y'=4,'z_hi'=4,'core'=2] {'y','z_hi','core'}, dimensions={0} | all-to-all | bytes 1048576 | tf_op jit(solution)/shard_map/all_to_all | solution.py:234
  35.8 0.9 collective-permute-start.1
  36.8 2.8 %collective-permute-start.12 = (bf16[6,128,256]{2,1,0:T(8,128)(2,1)S(1)}, bf16[6,128,256]{2,1,0:T(8,128)(2,1)S(1)}, u32[]{:S(2)}, u32[]{:S(2)}) collective-permute-start(bf16[6,128,256]{2,1,0:T(8,128)(2,1)S(1)} %get-tuple-element.40.refs_0_), channel_id=1, source_target_pairs={{0,192},{64,0},{128,64},{192,128},{1,193},{65,1},{129,65},{193,129... | collective-permute-start | bytes 1179656 | tf_op jit(solution)/shard_map/ppermute | solution.py:229
  39.5 1.6 %copy-done.1 = bf16[512,2048]{1,0:T(8,128)(2,1)S(1)} copy-done((bf16[512,2048]{1,0:T(8,128)(2,1)S(1)}, bf16[512,2048]{1,0:T(8,128)(2,1)}, u32[]{:S(2)}) %copy-start.1) | copy-done | bytes 2097176
  41.1 2.2 %transform.1 = bf16[32,4,16,128]{3,2,1,0:T(8,128)(2,1)} custom-call(bf16[512,2048]{1,0:T(8,128)(2,1)S(1)} %copy-done.1, bf16[512,2048]{1,0:T(8,128)(2,1)S(1)} %copy-done), custom_call_target="tpu_custom_call" | custom-call | flops 1073741824 | bytes 5242880 | tf_op jit(solution)/shard_map/transform/pallas_call | solution.py:143
  43.3 6.1 %all-to-all-start.1 = ((bf16[32,4,16,128]{3,2,1,0:T(8,128)(2,1)}), bf16[32,4,16,128]{3,2,1,0:T(8,128)(2,1)S(1)}, u32[]{:S(2)}, u32[]{:S(2)}) async-start(bf16[32,4,16,128]{3,2,1,0:T(8,128)(2,1)} %transform.1), calls=%async_computation.1 | async-start | bytes 1048576 | tf_op jit(solution)/shard_map/all_to_all | solution.py:234
  49.4 3.3 %collective-permute-start.13 = (bf16[6,128,256]{2,1,0:T(8,128)(2,1)S(1)}, bf16[6,128,256]{2,1,0:T(8,128)(2,1)S(1)}, u32[]{:S(2)}, u32[]{:S(2)}) collective-permute-start(bf16[6,128,256]{2,1,0:T(8,128)(2,1)S(1)} %collective-permute-done.1.refs_1_), channel_id=1, source_target_pairs={{0,192},{64,0},{128,64},{192,128},{1,193},{65,1},{129,65},{193,129... | collective-permute-start | bytes 1179656 | tf_op jit(solution)/shard_map/ppermute | solution.py:229
  52.7 1.6 %collective-permute-start.6 = (bf16[2,128,256]{2,1,0:T(8,128)(2,1)S(1)}, bf16[2,128,256]{2,1,0:T(8,128)(2,1)S(1)}, u32[]{:S(2)}, u32[]{:S(2)}) collective-permute-start(bf16[2,128,256]{2,1,0:T(8,128)(2,1)S(1)} %get-tuple-element.47.refs_0_), channel_id=1, source_target_pairs={{0,32},{32,0},{1,33},{33,1},{2,34},{34,2},{3,35},{35,3},{4,36},{36... | collective-permute-start | bytes 393224 | tf_op jit(solution)/shard_map/ppermute | solution.py:229
  54.3 3.2 %collective-permute-start.5 = (bf16[2,128,256]{2,1,0:T(8,128)(2,1)S(1)}, bf16[2,128,256]{2,1,0:T(8,128)(2,1)S(1)}, u32[]{:S(2)}, u32[]{:S(2)}) collective-permute-start(bf16[2,128,256]{2,1,0:T(8,128)(2,1)S(1)} %get-tuple-element.47.refs_0_), channel_id=1, source_target_pairs={{0,192},{64,0},{128,64},{192,128},{1,193},{65,1},{129,65},{193,129... | collective-permute-start | bytes 393224 | tf_op jit(solution)/shard_map/ppermute | solution.py:229
  57.5 10.2 %collective-permute-done.refs_6_ = bf16[2,128,256]{2,1,0:T(8,128)(2,1)S(1)} collective-permute-done((bf16[2,128,256]{2,1,0:T(8,128)(2,1)S(1)}, bf16[2,128,256]{2,1,0:T(8,128)(2,1)S(1)}, u32[]{:S(2)}, u32[]{:S(2)}) %collective-permute-start) | collective-permute-done | bytes 131104 | tf_op jit(solution)/shard_map/ppermute | solution.py:229
  67.6 0.6 copy-done.18
  68.3 1.5 %collective-permute-start.7 = (bf16[2,128,256]{2,1,0:T(8,128)(2,1)S(1)}, bf16[2,128,256]{2,1,0:T(8,128)(2,1)S(1)}, u32[]{:S(2)}, u32[]{:S(2)}) collective-permute-start(bf16[2,128,256]{2,1,0:T(8,128)(2,1)S(1)} %collective-permute-done.refs_6_), channel_id=1, source_target_pairs={{0,32},{32,0},{1,33},{33,1},{2,34},{34,2},{3,35},{35,3},{4,36},{36... | collective-permute-start | bytes 393224 | tf_op jit(solution)/shard_map/ppermute | solution.py:229
  70.0 3.3 %collective-permute-done.7.refs_7_ = bf16[2,128,256]{2,1,0:T(8,128)(2,1)S(1)} collective-permute-done((bf16[2,128,256]{2,1,0:T(8,128)(2,1)S(1)}, bf16[2,128,256]{2,1,0:T(8,128)(2,1)S(1)}, u32[]{:S(2)}, u32[]{:S(2)}) %collective-permute-start.7) | collective-permute-done | bytes 131104 | tf_op jit(solution)/shard_map/ppermute | solution.py:229
  73.2 0.6 copy-done.22
  73.9 1.5 %collective-permute-start.8 = (bf16[2,128,256]{2,1,0:T(8,128)(2,1)S(1)}, bf16[2,128,256]{2,1,0:T(8,128)(2,1)S(1)}, u32[]{:S(2)}, u32[]{:S(2)}) collective-permute-start(bf16[2,128,256]{2,1,0:T(8,128)(2,1)S(1)} %collective-permute-done.5.refs_2_), channel_id=1, source_target_pairs={{0,32},{32,0},{1,33},{33,1},{2,34},{34,2},{3,35},{35,3},{4,36},{36... | collective-permute-start | bytes 393224 | tf_op jit(solution)/shard_map/ppermute | solution.py:229
  75.4 0.6 copy-done.20
  76.0 0.7 copy-done.16
  76.7 2.2 %collective-permute-done.8.refs_3_ = bf16[2,128,256]{2,1,0:T(8,128)(2,1)S(1)} collective-permute-done((bf16[2,128,256]{2,1,0:T(8,128)(2,1)S(1)}, bf16[2,128,256]{2,1,0:T(8,128)(2,1)S(1)}, u32[]{:S(2)}, u32[]{:S(2)}) %collective-permute-start.8) | collective-permute-done | bytes 131104 | tf_op jit(solution)/shard_map/ppermute | solution.py:229
  78.9 0.7 copy-done.24
  79.5 2.8 %collective-permute-done.4.refs_4_ = bf16[2,128,256]{2,1,0:T(8,128)(2,1)} collective-permute-done((bf16[2,128,256]{2,1,0:T(8,128)(2,1)S(1)}, bf16[2,128,256]{2,1,0:T(8,128)(2,1)}, u32[]{:S(2)}, u32[]{:S(2)}) %collective-permute-start.4) | collective-permute-done | bytes 131104 | tf_op jit(solution)/shard_map/ppermute | solution.py:229
  83.3 5.6 %collective-permute-done.9.refs_5_ = bf16[2,128,256]{2,1,0:T(8,128)(2,1)} collective-permute-done((bf16[2,128,256]{2,1,0:T(8,128)(2,1)}, bf16[2,128,256]{2,1,0:T(8,128)(2,1)}, u32[]{:S(2)}, u32[]{:S(2)}) %collective-permute-start.9) | collective-permute-done | bytes 131104 | tf_op jit(solution)/shard_map/ppermute | solution.py:229
  89.6 3.4 %collective-permute-done.15.refs_4_ = bf16[6,128,256]{2,1,0:T(8,128)(2,1)} collective-permute-done((bf16[6,128,256]{2,1,0:T(8,128)(2,1)S(1)}, bf16[6,128,256]{2,1,0:T(8,128)(2,1)}, u32[]{:S(2)}, u32[]{:S(2)}) %collective-permute-start.15) | collective-permute-done | bytes 393248 | tf_op jit(solution)/shard_map/ppermute | solution.py:229
  93.0 5.1 %collective-permute-done.10.refs_1_ = bf16[5,128,256]{2,1,0:T(8,128)(2,1)S(1)} collective-permute-done((bf16[5,128,256]{2,1,0:T(8,128)(2,1)S(1)}, bf16[5,128,256]{2,1,0:T(8,128)(2,1)S(1)}, u32[]{:S(2)}, u32[]{:S(2)}) %collective-permute-start.10) | collective-permute-done | bytes 327712 | tf_op jit(solution)/shard_map/ppermute | solution.py:229
  98.7 2.0 %collective-permute-start.24 = (bf16[5,128,256]{2,1,0:T(8,128)(2,1)S(1)}, bf16[5,128,256]{2,1,0:T(8,128)(2,1)}, u32[]{:S(2)}, u32[]{:S(2)}) collective-permute-start(bf16[5,128,256]{2,1,0:T(8,128)(2,1)S(1)} %get-tuple-element.64.refs_0_), channel_id=1, source_target_pairs={{0,64},{64,128},{128,192},{192,0},{1,65},{65,129},{129,193},{193,1... | collective-permute-start | bytes 983048 | tf_op jit(solution)/shard_map/ppermute | solution.py:229
  100.7 0.8 copy-done.2
  101.5 0.7 copy-done.4
  102.2 1.2 collective-permute-start.23
  103.4 1.5 %collective-permute-done.11.refs_1_ = bf16[3,128,256]{2,1,0:T(8,128)(2,1)S(1)} collective-permute-done((bf16[3,128,256]{2,1,0:T(8,128)(2,1)S(1)}, bf16[3,128,256]{2,1,0:T(8,128)(2,1)S(1)}, u32[]{:S(2)}, u32[]{:S(2)}) %collective-permute-start.11) | collective-permute-done | bytes 196640 | tf_op jit(solution)/shard_map/ppermute | solution.py:229
  105.0 0.7 copy-done.6
  106.4 1.0 collective-permute-start.19
  107.4 4.3 %collective-permute-done.17.refs_7_ = bf16[3,128,256]{2,1,0:T(8,128)(2,1)S(1)} collective-permute-done((bf16[3,128,256]{2,1,0:T(8,128)(2,1)S(1)}, bf16[3,128,256]{2,1,0:T(8,128)(2,1)S(1)}, u32[]{:S(2)}, u32[]{:S(2)}) %collective-permute-start.17) | collective-permute-done | bytes 196640 | tf_op jit(solution)/shard_map/ppermute | solution.py:229
  111.7 0.7 copy-done.10
  112.9 0.7 copy-done.8
  113.5 0.7 collective-permute-start.27
  114.6 2.3 %collective-permute-start.26 = (bf16[5,128,256]{2,1,0:T(8,128)(2,1)}, bf16[5,128,256]{2,1,0:T(8,128)(2,1)}, u32[]{:S(2)}, u32[]{:S(2)}) collective-permute-start(bf16[5,128,256]{2,1,0:T(8,128)(2,1)} %collective-permute-done.23.refs_3_), channel_id=1, source_target_pairs={{0,192},{64,0},{128,64},{192,128},{1,193},{65,1},{129,65},{193,129... | collective-permute-start | bytes 983048 | tf_op jit(solution)/shard_map/ppermute | solution.py:229
  116.9 1.2 collective-permute-done.18.refs_3_
  118.1 0.7 copy-done.12
  119.3 5.3 %correlate.4 = (bf16[16,128,1024]{2,1,0:T(8,128)(2,1)}, bf16[16,128,1024]{2,1,0:T(8,128)(2,1)}) custom-call(s32[8]{0:T(128)S(1)} %stack.35.col_ref, bf16[6,128,256]{2,1,0:T(8,128)(2,1)S(1)} %get-tuple-element.40.refs_0_, bf16[6,128,256]{2,1,0:T(8,128)(2,1)S(1)} %collective-permute-done.1.refs_1_, bf16[6,128,256]{2,1,0:T(8,128)(2,1)S(1)} %collective-permute-done.12.refs_2_, ...), custom_call_target="tpu_custom_call" | custom-call | flops 805306368 | bytes 6291456 | tf_op jit(solution)/shard_map/correlate/pallas_call | solution.py:205
  124.6 0.9 copy-done.15
  125.5 0.9 copy-done.17
  126.4 0.9 copy-done.19
  127.3 0.9 copy-done.21
  128.2 0.9 copy-done.23
  129.1 0.9 copy-done.25
  130.0 3.0 %correlate.5 = (bf16[16,128,1024]{2,1,0:T(8,128)(2,1)}, bf16[16,128,1024]{2,1,0:T(8,128)(2,1)}) custom-call(s32[8]{0:T(128)S(1)} %stack.35.col_ref, bf16[2,128,256]{2,1,0:T(8,128)(2,1)S(1)} %copy-done.15, bf16[2,128,256]{2,1,0:T(8,128)(2,1)S(1)} %copy-done.19, bf16[2,128,256]{2,1,0:T(8,128)(2,1)S(1)} %copy-done.21, ...), custom_call_target="tpu_custom_call", output_to_operand_aliasing={{0}: (9, {}), {1}: (10, {})} | custom-call | flops 268435456 | bytes 2097152 | tf_op jit(solution)/shard_map/correlate/pallas_call | solution.py:205
  133.2 5.3 %correlate.6 = (bf16[16,128,1024]{2,1,0:T(8,128)(2,1)}, bf16[16,128,1024]{2,1,0:T(8,128)(2,1)}) custom-call(s32[8]{0:T(128)S(1)} %stack.35.col_ref, bf16[5,128,256]{2,1,0:T(8,128)(2,1)S(1)} %copy-done.3, bf16[5,128,256]{2,1,0:T(8,128)(2,1)S(1)} %collective-permute-done.10.refs_1_, ...), custom_call_target="tpu_custom_call", output_to_operand_aliasing={{0}: (9, {}), {1}: (10, {})} | custom-call | flops 671088640 | bytes 5242880 | tf_op jit(solution)/shard_map/correlate/pallas_call | solution.py:205
  138.5 3.8 %correlate.7 = (bf16[16,128,1024]{2,1,0:T(8,128)(2,1)}, bf16[16,128,1024]{2,1,0:T(8,128)(2,1)}) custom-call(s32[8]{0:T(128)S(1)} %stack.35.col_ref, bf16[3,128,256]{2,1,0:T(8,128)(2,1)S(1)} %get-tuple-element.56.refs_0_, bf16[3,128,256]{2,1,0:T(8,128)(2,1)S(1)} %copy-done.7, ...), custom_call_target="tpu_custom_call", output_to_operand_aliasing={{0}: (9, {}), {1}: (10, {})} | custom-call | flops 402653184 | bytes 3145728 | tf_op jit(solution)/shard_map/correlate/pallas_call | solution.py:205
  (72 shorter events, 5.1 us)
Async XLA Ops:
  0.6 38.9 %copy-start = (bf16[512,2048]{1,0:T(8,128)(2,1)S(1)}, bf16[512,2048]{1,0:T(8,128)(2,1)}, u32[]{:S(2)}) copy-start(bf16[512,2048]{1,0:T(8,128)(2,1)} %constant.80.clone.refs_1_) | copy-start | bytes 6291460
  35.8 33.9 %copy-start.14 = (bf16[2,128,256]{2,1,0:T(8,128)(2,1)}, bf16[2,128,256]{2,1,0:T(8,128)(2,1)S(1)}, u32[]{:S(2)}) copy-start(bf16[2,128,256]{2,1,0:T(8,128)(2,1)S(1)} %get-tuple-element.47.refs_0_) | copy-start | bytes 393220
  35.8 13.6 %collective-permute-start.1 = (bf16[6,128,256]{2,1,0:T(8,128)(2,1)S(1)}, bf16[6,128,256]{2,1,0:T(8,128)(2,1)S(1)}, u32[]{:S(2)}, u32[]{:S(2)}) collective-permute-start(bf16[6,128,256]{2,1,0:T(8,128)(2,1)S(1)} %get-tuple-element.40.refs_0_), channel_id=1, source_target_pairs={{0,32},{32,0},{1,33},{33,1},{2,34},{34,2},{3,35},{35,3},{4,36},{36... | collective-permute-start | bytes 1179656 | tf_op jit(solution)/shard_map/ppermute | solution.py:229
  36.8 12.6 %collective-permute-start.12 = (bf16[6,128,256]{2,1,0:T(8,128)(2,1)S(1)}, bf16[6,128,256]{2,1,0:T(8,128)(2,1)S(1)}, u32[]{:S(2)}, u32[]{:S(2)}) collective-permute-start(bf16[6,128,256]{2,1,0:T(8,128)(2,1)S(1)} %get-tuple-element.40.refs_0_), channel_id=1, source_target_pairs={{0,192},{64,0},{128,64},{192,128},{1,193},{65,1},{129,65},{193,129... | collective-permute-start | bytes 1179656 | tf_op jit(solution)/shard_map/ppermute | solution.py:229
  39.5 13.2 %collective-permute-start.2 = (bf16[6,128,256]{2,1,0:T(8,128)(2,1)S(1)}, bf16[6,128,256]{2,1,0:T(8,128)(2,1)S(1)}, u32[]{:S(2)}, u32[]{:S(2)}) collective-permute-start(bf16[6,128,256]{2,1,0:T(8,128)(2,1)S(1)} %get-tuple-element.40.refs_0_), channel_id=1, source_target_pairs={{0,64},{64,128},{128,192},{192,0},{1,65},{65,129},{129,193},{193,1... | collective-permute-start | bytes 1179656 | tf_op jit(solution)/shard_map/ppermute | solution.py:229
  39.5 1.6 %copy-start.1 = (bf16[512,2048]{1,0:T(8,128)(2,1)S(1)}, bf16[512,2048]{1,0:T(8,128)(2,1)}, u32[]{:S(2)}) copy-start(bf16[512,2048]{1,0:T(8,128)(2,1)} %get-tuple-element.41.refs_0_) | copy-start | bytes 6291460
  43.3 39.5 %all-to-all-start.1 = ((bf16[32,4,16,128]{3,2,1,0:T(8,128)(2,1)}), bf16[32,4,16,128]{3,2,1,0:T(8,128)(2,1)S(1)}, u32[]{:S(2)}, u32[]{:S(2)}) async-start(bf16[32,4,16,128]{3,2,1,0:T(8,128)(2,1)} %transform.1), calls=%async_computation.1 | async-start | bytes 1048576 | tf_op jit(solution)/shard_map/all_to_all | solution.py:234
  49.4 20.3 %collective-permute-start.13 = (bf16[6,128,256]{2,1,0:T(8,128)(2,1)S(1)}, bf16[6,128,256]{2,1,0:T(8,128)(2,1)S(1)}, u32[]{:S(2)}, u32[]{:S(2)}) collective-permute-start(bf16[6,128,256]{2,1,0:T(8,128)(2,1)S(1)} %collective-permute-done.1.refs_1_), channel_id=1, source_target_pairs={{0,192},{64,0},{128,64},{192,128},{1,193},{65,1},{129,65},{193,129... | collective-permute-start | bytes 1179656 | tf_op jit(solution)/shard_map/ppermute | solution.py:229
  52.7 23.3 %collective-permute-start.3 = (bf16[6,128,256]{2,1,0:T(8,128)(2,1)S(1)}, bf16[6,128,256]{2,1,0:T(8,128)(2,1)S(1)}, u32[]{:S(2)}, u32[]{:S(2)}) collective-permute-start(bf16[6,128,256]{2,1,0:T(8,128)(2,1)S(1)} %collective-permute-done.1.refs_1_), channel_id=1, source_target_pairs={{0,64},{64,128},{128,192},{192,0},{1,65},{65,129},{129,193},{193,1... | collective-permute-start | bytes 1179656 | tf_op jit(solution)/shard_map/ppermute | solution.py:229
  52.7 14.9 %collective-permute-start = (bf16[2,128,256]{2,1,0:T(8,128)(2,1)S(1)}, bf16[2,128,256]{2,1,0:T(8,128)(2,1)S(1)}, u32[]{:S(2)}, u32[]{:S(2)}) collective-permute-start(bf16[2,128,256]{2,1,0:T(8,128)(2,1)S(1)} %get-tuple-element.47.refs_0_), channel_id=1, source_target_pairs={{0,64},{64,128},{128,192},{192,0},{1,65},{65,129},{129,193},{193,1... | collective-permute-start | bytes 393224 | tf_op jit(solution)/shard_map/ppermute | solution.py:229
  52.7 14.9 %collective-permute-start.6 = (bf16[2,128,256]{2,1,0:T(8,128)(2,1)S(1)}, bf16[2,128,256]{2,1,0:T(8,128)(2,1)S(1)}, u32[]{:S(2)}, u32[]{:S(2)}) collective-permute-start(bf16[2,128,256]{2,1,0:T(8,128)(2,1)S(1)} %get-tuple-element.47.refs_0_), channel_id=1, source_target_pairs={{0,32},{32,0},{1,33},{33,1},{2,34},{34,2},{3,35},{35,3},{4,36},{36... | collective-permute-start | bytes 393224 | tf_op jit(solution)/shard_map/ppermute | solution.py:229
  54.3 15.5 %collective-permute-start.5 = (bf16[2,128,256]{2,1,0:T(8,128)(2,1)S(1)}, bf16[2,128,256]{2,1,0:T(8,128)(2,1)S(1)}, u32[]{:S(2)}, u32[]{:S(2)}) collective-permute-start(bf16[2,128,256]{2,1,0:T(8,128)(2,1)S(1)} %get-tuple-element.47.refs_0_), channel_id=1, source_target_pairs={{0,192},{64,0},{128,64},{192,128},{1,193},{65,1},{129,65},{193,129... | collective-permute-start | bytes 393224 | tf_op jit(solution)/shard_map/ppermute | solution.py:229
  68.3 5.0 %collective-permute-start.7 = (bf16[2,128,256]{2,1,0:T(8,128)(2,1)S(1)}, bf16[2,128,256]{2,1,0:T(8,128)(2,1)S(1)}, u32[]{:S(2)}, u32[]{:S(2)}) collective-permute-start(bf16[2,128,256]{2,1,0:T(8,128)(2,1)S(1)} %collective-permute-done.refs_6_), channel_id=1, source_target_pairs={{0,32},{32,0},{1,33},{33,1},{2,34},{34,2},{3,35},{35,3},{4,36},{36... | collective-permute-start | bytes 393224 | tf_op jit(solution)/shard_map/ppermute | solution.py:229
  69.8 19.7 %collective-permute-start.21 = (bf16[6,128,256]{2,1,0:T(8,128)(2,1)S(1)}, bf16[6,128,256]{2,1,0:T(8,128)(2,1)S(1)}, u32[]{:S(2)}, u32[]{:S(2)}) collective-permute-start(bf16[6,128,256]{2,1,0:T(8,128)(2,1)S(1)} %collective-permute-done.13.refs_3_), channel_id=1, source_target_pairs={{0,192},{64,0},{128,64},{192,128},{1,193},{65,1},{129,65},{193,129... | collective-permute-start | bytes 1179656 | tf_op jit(solution)/shard_map/ppermute | solution.py:229
  73.9 5.0 %collective-permute-start.8 = (bf16[2,128,256]{2,1,0:T(8,128)(2,1)S(1)}, bf16[2,128,256]{2,1,0:T(8,128)(2,1)S(1)}, u32[]{:S(2)}, u32[]{:S(2)}) collective-permute-start(bf16[2,128,256]{2,1,0:T(8,128)(2,1)S(1)} %collective-permute-done.5.refs_2_), channel_id=1, source_target_pairs={{0,32},{32,0},{1,33},{33,1},{2,34},{34,2},{3,35},{35,3},{4,36},{36... | collective-permute-start | bytes 393224 | tf_op jit(solution)/shard_map/ppermute | solution.py:229
  76.0 6.3 %collective-permute-start.4 = (bf16[2,128,256]{2,1,0:T(8,128)(2,1)S(1)}, bf16[2,128,256]{2,1,0:T(8,128)(2,1)}, u32[]{:S(2)}, u32[]{:S(2)}) collective-permute-start(bf16[2,128,256]{2,1,0:T(8,128)(2,1)S(1)} %collective-permute-done.refs_6_), channel_id=1, source_target_pairs={{0,64},{64,128},{128,192},{192,0},{1,65},{65,129},{129,193},{193,1... | collective-permute-start | bytes 393224 | tf_op jit(solution)/shard_map/ppermute | solution.py:229
  82.3 6.6 %collective-permute-start.9 = (bf16[2,128,256]{2,1,0:T(8,128)(2,1)}, bf16[2,128,256]{2,1,0:T(8,128)(2,1)}, u32[]{:S(2)}, u32[]{:S(2)}) collective-permute-start(bf16[2,128,256]{2,1,0:T(8,128)(2,1)} %collective-permute-done.4.refs_4_), channel_id=1, source_target_pairs={{0,32},{32,0},{1,33},{33,1},{2,34},{34,2},{3,35},{35,3},{4,36},{36... | collective-permute-start | bytes 393224 | tf_op jit(solution)/shard_map/ppermute | solution.py:229
  82.9 10.1 %collective-permute-start.15 = (bf16[6,128,256]{2,1,0:T(8,128)(2,1)S(1)}, bf16[6,128,256]{2,1,0:T(8,128)(2,1)}, u32[]{:S(2)}, u32[]{:S(2)}) collective-permute-start(bf16[6,128,256]{2,1,0:T(8,128)(2,1)S(1)} %collective-permute-done.2.refs_6_), channel_id=1, source_target_pairs={{0,64},{64,128},{128,192},{192,0},{1,65},{65,129},{129,193},{193,1... | collective-permute-start | bytes 1179656 | tf_op jit(solution)/shard_map/ppermute | solution.py:229
  88.9 9.2 %collective-permute-start.10 = (bf16[5,128,256]{2,1,0:T(8,128)(2,1)S(1)}, bf16[5,128,256]{2,1,0:T(8,128)(2,1)S(1)}, u32[]{:S(2)}, u32[]{:S(2)}) collective-permute-start(bf16[5,128,256]{2,1,0:T(8,128)(2,1)S(1)} %get-tuple-element.64.refs_0_), channel_id=1, source_target_pairs={{0,32},{32,0},{1,33},{33,1},{2,34},{34,2},{3,35},{35,3},{4,36},{36... | collective-permute-start | bytes 983048 | tf_op jit(solution)/shard_map/ppermute | solution.py:229
  89.5 12.0 %collective-permute-start.22 = (bf16[5,128,256]{2,1,0:T(8,128)(2,1)S(1)}, bf16[5,128,256]{2,1,0:T(8,128)(2,1)S(1)}, u32[]{:S(2)}, u32[]{:S(2)}) collective-permute-start(bf16[5,128,256]{2,1,0:T(8,128)(2,1)S(1)} %get-tuple-element.64.refs_0_), channel_id=1, source_target_pairs={{0,192},{64,0},{128,64},{192,128},{1,193},{65,1},{129,65},{193,129... | collective-permute-start | bytes 983048 | tf_op jit(solution)/shard_map/ppermute | solution.py:229
  93.0 10.4 %collective-permute-start.16 = (bf16[3,128,256]{2,1,0:T(8,128)(2,1)S(1)}, bf16[3,128,256]{2,1,0:T(8,128)(2,1)S(1)}, u32[]{:S(2)}, u32[]{:S(2)}) collective-permute-start(bf16[3,128,256]{2,1,0:T(8,128)(2,1)S(1)} %get-tuple-element.56.refs_0_), channel_id=1, source_target_pairs={{0,64},{64,128},{128,192},{192,0},{1,65},{65,129},{129,193},{193,1... | collective-permute-start | bytes 589832 | tf_op jit(solution)/shard_map/ppermute | solution.py:229
  98.1 6.8 %collective-permute-start.11 = (bf16[3,128,256]{2,1,0:T(8,128)(2,1)S(1)}, bf16[3,128,256]{2,1,0:T(8,128)(2,1)S(1)}, u32[]{:S(2)}, u32[]{:S(2)}) collective-permute-start(bf16[3,128,256]{2,1,0:T(8,128)(2,1)S(1)} %get-tuple-element.56.refs_0_), channel_id=1, source_target_pairs={{0,32},{32,0},{1,33},{33,1},{2,34},{34,2},{3,35},{35,3},{4,36},{36... | collective-permute-start | bytes 589832 | tf_op jit(solution)/shard_map/ppermute | solution.py:229
  98.7 7.7 %collective-permute-start.14 = (bf16[3,128,256]{2,1,0:T(8,128)(2,1)S(1)}, bf16[3,128,256]{2,1,0:T(8,128)(2,1)S(1)}, u32[]{:S(2)}, u32[]{:S(2)}) collective-permute-start(bf16[3,128,256]{2,1,0:T(8,128)(2,1)S(1)} %get-tuple-element.56.refs_0_), channel_id=1, source_target_pairs={{0,192},{64,0},{128,64},{192,128},{1,193},{65,1},{129,65},{193,129... | collective-permute-start | bytes 589832 | tf_op jit(solution)/shard_map/ppermute | solution.py:229
  98.7 14.9 %collective-permute-start.24 = (bf16[5,128,256]{2,1,0:T(8,128)(2,1)S(1)}, bf16[5,128,256]{2,1,0:T(8,128)(2,1)}, u32[]{:S(2)}, u32[]{:S(2)}) collective-permute-start(bf16[5,128,256]{2,1,0:T(8,128)(2,1)S(1)} %get-tuple-element.64.refs_0_), channel_id=1, source_target_pairs={{0,64},{64,128},{128,192},{192,0},{1,65},{65,129},{129,193},{193,1... | collective-permute-start | bytes 983048 | tf_op jit(solution)/shard_map/ppermute | solution.py:229
  100.7 0.8 copy-start.2
  101.5 0.7 copy-start.4
  102.2 12.4 %collective-permute-start.23 = (bf16[5,128,256]{2,1,0:T(8,128)(2,1)S(1)}, bf16[5,128,256]{2,1,0:T(8,128)(2,1)}, u32[]{:S(2)}, u32[]{:S(2)}) collective-permute-start(bf16[5,128,256]{2,1,0:T(8,128)(2,1)S(1)} %collective-permute-done.10.refs_1_), channel_id=1, source_target_pairs={{0,192},{64,0},{128,64},{192,128},{1,193},{65,1},{129,65},{193,129... | collective-permute-start | bytes 983048 | tf_op jit(solution)/shard_map/ppermute | solution.py:229
  105.0 0.7 copy-start.6
  105.6 6.1 %collective-permute-start.17 = (bf16[3,128,256]{2,1,0:T(8,128)(2,1)S(1)}, bf16[3,128,256]{2,1,0:T(8,128)(2,1)S(1)}, u32[]{:S(2)}, u32[]{:S(2)}) collective-permute-start(bf16[3,128,256]{2,1,0:T(8,128)(2,1)S(1)} %collective-permute-done.16.refs_6_), channel_id=1, source_target_pairs={{0,32},{32,0},{1,33},{33,1},{2,34},{34,2},{3,35},{35,3},{4,36},{36... | collective-permute-start | bytes 589832 | tf_op jit(solution)/shard_map/ppermute | solution.py:229
  106.4 8.2 %collective-permute-start.19 = (bf16[3,128,256]{2,1,0:T(8,128)(2,1)S(1)}, bf16[3,128,256]{2,1,0:T(8,128)(2,1)}, u32[]{:S(2)}, u32[]{:S(2)}) collective-permute-start(bf16[3,128,256]{2,1,0:T(8,128)(2,1)S(1)} %collective-permute-done.14.refs_2_), channel_id=1, source_target_pairs={{0,192},{64,0},{128,64},{192,128},{1,193},{65,1},{129,65},{193,129... | collective-permute-start | bytes 589832 | tf_op jit(solution)/shard_map/ppermute | solution.py:229
  112.4 5.7 %collective-permute-start.18 = (bf16[3,128,256]{2,1,0:T(8,128)(2,1)S(1)}, bf16[3,128,256]{2,1,0:T(8,128)(2,1)S(1)}, u32[]{:S(2)}, u32[]{:S(2)}) collective-permute-start(bf16[3,128,256]{2,1,0:T(8,128)(2,1)S(1)} %collective-permute-done.14.refs_2_), channel_id=1, source_target_pairs={{0,32},{32,0},{1,33},{33,1},{2,34},{34,2},{3,35},{35,3},{4,36},{36... | collective-permute-start | bytes 589832 | tf_op jit(solution)/shard_map/ppermute | solution.py:229
  113.5 19.6 %collective-permute-start.25 = (bf16[5,128,256]{2,1,0:T(8,128)(2,1)}, bf16[5,128,256]{2,1,0:T(8,128)(2,1)}, u32[]{:S(2)}, u32[]{:S(2)}) collective-permute-start(bf16[5,128,256]{2,1,0:T(8,128)(2,1)} %collective-permute-done.24.refs_6_), channel_id=1, source_target_pairs={{0,64},{64,128},{128,192},{192,0},{1,65},{65,129},{129,193},{193,1... | collective-permute-start | bytes 983048 | tf_op jit(solution)/shard_map/ppermute | solution.py:229
  113.5 19.6 %collective-permute-start.27 = (bf16[5,128,256]{2,1,0:T(8,128)(2,1)S(1)}, bf16[5,128,256]{2,1,0:T(8,128)(2,1)}, u32[]{:S(2)}, u32[]{:S(2)}) collective-permute-start(bf16[5,128,256]{2,1,0:T(8,128)(2,1)S(1)} %collective-permute-done.10.refs_1_), channel_id=1, source_target_pairs={{0,64},{64,128},{128,192},{192,0},{1,65},{65,129},{129,193},{193,1... | collective-permute-start | bytes 983048 | tf_op jit(solution)/shard_map/ppermute | solution.py:229
  114.6 18.5 %collective-permute-start.26 = (bf16[5,128,256]{2,1,0:T(8,128)(2,1)}, bf16[5,128,256]{2,1,0:T(8,128)(2,1)}, u32[]{:S(2)}, u32[]{:S(2)}) collective-permute-start(bf16[5,128,256]{2,1,0:T(8,128)(2,1)} %collective-permute-done.23.refs_3_), channel_id=1, source_target_pairs={{0,192},{64,0},{128,64},{192,128},{1,193},{65,1},{129,65},{193,129... | collective-permute-start | bytes 983048 | tf_op jit(solution)/shard_map/ppermute | solution.py:229
  118.1 0.7 copy-start.12
  118.8 19.7 %collective-permute-start.20 = (bf16[3,128,256]{2,1,0:T(8,128)(2,1)}, bf16[3,128,256]{2,1,0:T(8,128)(2,1)}, u32[]{:S(2)}, u32[]{:S(2)}) collective-permute-start(bf16[3,128,256]{2,1,0:T(8,128)(2,1)} %collective-permute-done.19.refs_4_), channel_id=1, source_target_pairs={{0,32},{32,0},{1,33},{33,1},{2,34},{34,2},{3,35},{35,3},{4,36},{36... | collective-permute-start | bytes 589832 | tf_op jit(solution)/shard_map/ppermute | solution.py:229
  124.6 0.9 copy-start.15
  125.5 0.9 copy-start.17
  126.4 0.9 copy-start.19
  127.3 0.9 copy-start.21
  128.2 0.9 copy-start.23
  129.1 0.9 copy-start.25
  130.0 3.1 %copy-start.3 = (bf16[5,128,256]{2,1,0:T(8,128)(2,1)S(1)}, bf16[5,128,256]{2,1,0:T(8,128)(2,1)}, u32[]{:S(2)}) copy-start(bf16[5,128,256]{2,1,0:T(8,128)(2,1)} %copy-done.2) | copy-start | bytes 983044
  130.0 3.1 %copy-start.5 = (bf16[5,128,256]{2,1,0:T(8,128)(2,1)S(1)}, bf16[5,128,256]{2,1,0:T(8,128)(2,1)}, u32[]{:S(2)}) copy-start(bf16[5,128,256]{2,1,0:T(8,128)(2,1)} %copy-done.4) | copy-start | bytes 983044
  133.1 5.4 %copy-start.7 = (bf16[3,128,256]{2,1,0:T(8,128)(2,1)S(1)}, bf16[3,128,256]{2,1,0:T(8,128)(2,1)}, u32[]{:S(2)}) copy-start(bf16[3,128,256]{2,1,0:T(8,128)(2,1)} %copy-done.6) | copy-start | bytes 589828
  133.1 5.4 %copy-start.9 = (bf16[3,128,256]{2,1,0:T(8,128)(2,1)S(1)}, bf16[3,128,256]{2,1,0:T(8,128)(2,1)}, u32[]{:S(2)}) copy-start(bf16[3,128,256]{2,1,0:T(8,128)(2,1)} %copy-done.8) | copy-start | bytes 589828
  133.1 5.4 %copy-start.11 = (bf16[3,128,256]{2,1,0:T(8,128)(2,1)S(1)}, bf16[3,128,256]{2,1,0:T(8,128)(2,1)}, u32[]{:S(2)}) copy-start(bf16[3,128,256]{2,1,0:T(8,128)(2,1)} %copy-done.10) | copy-start | bytes 589828
  133.1 5.4 %copy-start.13 = (bf16[3,128,256]{2,1,0:T(8,128)(2,1)S(1)}, bf16[3,128,256]{2,1,0:T(8,128)(2,1)}, u32[]{:S(2)}) copy-start(bf16[3,128,256]{2,1,0:T(8,128)(2,1)} %copy-done.12) | copy-start | bytes 589828
  (7 other events, 4.6 us)

commit v3 on v2

v3 whole, which is shorter than its diff:
```python
import math

import jax
import jax.numpy as jnp
import ml_dtypes
import numpy as np
from jax import lax
from jax.experimental import pallas as pl
from jax.experimental.pallas import tpu as pltpu
from jax.sharding import Mesh, PartitionSpec as P

CHAN = 512
NFFT = 2048
TAPS = 4
SPEC = 128
FRAMES = SPEC + TAPS - 1
ROWS_IN = 4
GROUPS = 8
N_FREQ = 32
CH = CHAN // N_FREQ
LANES = 128
SUB = 8
F32 = jnp.float32
BF16 = jnp.bfloat16
NT = (((1,), (1,)), ((), ()))
MIB = 1 << 20
FREQ = ("y", "z_hi", "core")
LIGHT = pl.CostEstimate(flops=1000, bytes_accessed=1000, transcendentals=0)

EARLY = 8


def table_rows(lo, count):
    j = np.arange(NFFT, dtype=np.int64)
    c = (np.arange(N_FREQ)[:, None] * CH + lo + np.arange(count)[None, :]).reshape(-1)
    angle = ((c[:, None] * j[None, :]) % NFFT).astype(np.float32) * np.float32(2.0 * math.pi / NFFT)
    both = np.stack([np.cos(angle), -np.sin(angle)], axis=0)
    both = both.reshape(2, N_FREQ, count, NFFT).transpose(1, 0, 2, 3)
    return jnp.asarray(both.reshape(2 * N_FREQ * count, NFFT).astype(ml_dtypes.bfloat16))


def store_spectra(raw, o_ref, first, per):
    out = (raw * (1.0 / math.sqrt(NFFT))).astype(BF16)
    for d in range(raw.shape[0] // per):
        for i in range(ROWS_IN):
            o_ref[first + d, i] = out[d * per : (d + 1) * per, i * SPEC : (i + 1) * SPEC]


def filter_kernel(rows, s_hbm, w_ref, t_hbm, o_ref, s_ref, t_ref, f_ref, wv_ref, s_sem, t_sem):
    parts = 4
    span = SPEC // parts
    edges = [0] + [(h + 1) * span + TAPS - 1 for h in range(parts)]
    arrivals = []
    for h in range(parts):
        cut = pl.ds(edges[h], edges[h + 1] - edges[h])
        arrivals.append(pltpu.make_async_copy(s_hbm.at[cut], s_ref.at[cut], s_sem.at[h]))
    for copy in arrivals:
        copy.start()
    table_copy = pltpu.make_async_copy(t_hbm, t_ref, t_sem)
    table_copy.start()
    pairs = NFFT // LANES // 2
    for a in range(pairs):
        for t in range(TAPS):
            halves = [
                jnp.broadcast_to(w_ref[t : t + 1, (2 * a + b) * LANES : (2 * a + b + 1) * LANES] * (1.0 / 64.0), (ROWS_IN, LANES))
                for b in range(2)
            ]
            wv_ref[a, t] = jnp.concatenate(halves, axis=0)
    for h in range(parts):
        arrivals[h].wait()

        def step(a, carry):
            sub = pl.ds(pl.multiple_of(a * SUB, SUB), SUB)
            taps = [wv_ref[a, t] for t in range(TAPS)]
            for s0 in range(h * span, (h + 1) * span, 2 * SUB):
                v = [s_ref[s0 + k, sub, :].astype(F32) for k in range(2 * SUB + TAPS - 1)]
                sums = []
                for k in range(2 * SUB):
                    acc = taps[0] * v[k]
                    for t in range(1, TAPS):
                        acc = acc + taps[t] * v[k + t]
                    sums.append(acc)
                low = jnp.swapaxes(jnp.stack(sums[:SUB], axis=0), 0, 1)
                high = jnp.swapaxes(jnp.stack(sums[SUB:], axis=0), 0, 1)
                both = jnp.concatenate([low, high], axis=1).astype(BF16)
                for b in range(2):
                    lane = pl.ds(pl.multiple_of((2 * a + b) * LANES, LANES), LANES)
                    for i in range(ROWS_IN):
                        f_ref[i * SPEC + s0 : i * SPEC + s0 + 2 * SUB, lane] = both[b * ROWS_IN + i]
            return carry

        lax.fori_loop(0, pairs, step, 0)
    table_copy.wait()
    tile = 256
    per = rows // N_FREQ
    for m in range(rows // tile):
        raw = lax.dot_general(t_ref[m * tile : (m + 1) * tile, :], f_ref[...], NT, preferred_element_type=F32)
        store_spectra(raw, o_ref, m * (tile // per), per)


def filter_and_transform(samples, window, table):
    view = samples.reshape(ROWS_IN, FRAMES, NFFT // LANES, LANES).transpose(1, 2, 0, 3)
    view = view.reshape(FRAMES, NFFT // LANES * ROWS_IN, LANES)
    rows = table.shape[0]
    return pl.pallas_call(
        lambda *refs: filter_kernel(rows, *refs),
        out_shape=jax.ShapeDtypeStruct((N_FREQ, ROWS_IN, rows // N_FREQ, SPEC), BF16),
        in_specs=[
            pl.BlockSpec(memory_space=pl.ANY),
            pl.BlockSpec(memory_space=pltpu.VMEM),
            pl.BlockSpec(memory_space=pl.ANY),
        ],
        out_specs=pl.BlockSpec(memory_space=pltpu.VMEM),
        scratch_shapes=[
            pltpu.VMEM((FRAMES, NFFT // LANES * ROWS_IN, LANES), jnp.int32),
            pltpu.VMEM((rows, NFFT), BF16),
            pltpu.VMEM((ROWS_IN * SPEC, NFFT), BF16),
            pltpu.VMEM((NFFT // LANES // 2, TAPS, SUB, LANES), F32),
            pltpu.SemaphoreType.DMA((4,)),
            pltpu.SemaphoreType.DMA,
        ],
        compiler_params=pltpu.CompilerParams(vmem_limit_bytes=60 * MIB),
        cost_estimate=LIGHT,
        name="filter_and_transform",
    )(view, window, table)


def assemble_kernel(sizes, x_ref, *refs):
    outs, wide = refs[:-1], refs[-1]
    count, pitch = sum(sizes), wide.shape[1]
    wide[:, : 2 * count, :] = x_ref[...].astype(F32)
    flat = wide.reshape(SPEC * pitch, SPEC)
    lo = 0
    for out, size in zip(outs, sizes):
        for c in range(size):
            for p in range(2):
                rows = pl.ds(p * count + lo + c, SPEC, stride=pitch)
                out[c, :, p * SPEC : (p + 1) * SPEC] = flat[rows, :].astype(BF16)
        lo += size


def assemble(pieces, sizes):
    count = sum(sizes)
    pitch = 2 * count + SUB if 2 * count // SUB % 2 == 0 else 2 * count
    return pl.pallas_call(
        lambda *refs: assemble_kernel(sizes, *refs),
        out_shape=[jax.ShapeDtypeStruct((size, SPEC, 2 * SPEC), BF16) for size in sizes],
        scratch_shapes=[pltpu.VMEM((SPEC, pitch, SPEC), F32)],
        compiler_params=pltpu.CompilerParams(vmem_limit_bytes=8 * MIB),
        cost_estimate=LIGHT,
        name="assemble",
    )(pieces.reshape(SPEC, 2 * count, SPEC))


def products(own, other):
    rotated = jnp.concatenate([own[:, SPEC:], -own[:, :SPEC]], axis=1)
    left = jnp.concatenate([own, rotated], axis=0)
    return (lax.dot_general(left, other, NT, preferred_element_type=F32) * (1.0 / SPEC)).astype(BF16)


def correlate_kernel(plan, last, place_ref, *refs):
    count = 1 + max(k for part in plan for k in (part[1],) + tuple(b for b, _ in part[2]))
    blocks, refs = refs[:count], refs[count:]
    if last:
        re_ref, im_ref = refs[:2]
        re_out, im_out, sem = refs[-3:]
    else:
        re_ref, im_ref = refs[-2:]
    copies = []
    for lo, own, others in plan:
        size = blocks[own].shape[0]

        def one(c):
            for k in range(0, len(others), 2):
                pair = others[k : k + 2]
                right = jnp.concatenate([blocks[b][c] for b, _ in pair], axis=0)
                out = products(blocks[own][c], right)
                for h, (_, spot) in enumerate(pair):
                    cols = pl.ds(pl.multiple_of(place_ref[spot], SPEC), SPEC)
                    re_ref[lo + c, :, cols] = out[:SPEC, h * SPEC : (h + 1) * SPEC]
                    im_ref[lo + c, :, cols] = out[SPEC:, h * SPEC : (h + 1) * SPEC]

        if last:
            for c in range(size):
                one(c)
                for k, (src, dst) in enumerate(((re_ref, re_out), (im_ref, im_out))):
                    copies.append(pltpu.make_async_copy(src.at[lo + c], dst.at[lo + c], sem.at[k, lo + c]))
                    copies[-1].start()
        else:
            lax.fori_loop(0, size, lambda c, carry: (one(c), carry)[1], 0, unroll=4)
    for copy in copies:
        copy.wait()


def correlate(place, plan, blocks, so_far=None, last=False, earlier=None):
    shape = jax.ShapeDtypeStruct((CH, SPEC, SPEC * GROUPS), BF16)
    vmem = pl.BlockSpec(memory_space=pltpu.VMEM)
    operands = [place] + list(blocks) + list(so_far or ())
    in_specs = [pl.BlockSpec(memory_space=pltpu.SMEM)] + [vmem] * (len(operands) - 1)
    aliases, scratch, out_specs = {}, [], [vmem] * 2
    if last:
        out_specs = [pl.BlockSpec(memory_space=pl.ANY)] * 2
        scratch = [pltpu.SemaphoreType.DMA((2, CH))]
        if earlier is not None:
            aliases = {len(operands): 0, len(operands) + 1: 1}
            operands += list(earlier)
            in_specs += out_specs
    elif so_far is not None:
        aliases = {1 + len(blocks): 0, 2 + len(blocks): 1}
    return pl.pallas_call(
        lambda *refs: correlate_kernel(plan, last, *refs),
        out_shape=[shape, shape],
        in_specs=in_specs,
        out_specs=out_specs,
        scratch_shapes=scratch,
        input_output_aliases=aliases,
        compiler_params=pltpu.CompilerParams(vmem_limit_bytes=16 * MIB),
        cost_estimate=LIGHT,
        name="correlate",
    )(*operands)


def shift(value, axis, by):
    size = lax.axis_size(axis)
    return lax.ppermute(value, axis, [(i, (i + by) % size) for i in range(size)])


def up(value):
    return shift(value, "x", 1)


def down(value):
    return shift(value, "x", -1)


def across(value):
    return shift(value, "z_lo", 1)


def after(values, done):
    return lax.optimization_barrier((values, done))


def on_device(samples, window):
    x, z = lax.axis_index("x"), lax.axis_index("z_lo")
    place = jnp.stack([((x + dx) % 4 * 2 + (z + dz) % 2) * SPEC for dx in range(4) for dz in range(2)]).astype(jnp.int32)

    pieces = filter_and_transform(samples, window, table_rows(0, CH))
    arrived = lax.all_to_all(pieces, FREQ, split_axis=0, concat_axis=0, tiled=True)
    a, b = assemble(arrived, (EARLY, CH - EARLY))
    b_m, b_p, za = up(b), down(b), across(a)
    a_m, a_p, zb = up(a), down(a), across(b)
    (za, b_p, b_m), _ = after((za, b_p, b_m), (za, b_p, b_m))
    za_m, b_o, zb_m = up(za), down(b_p), across(b_m)
    a_o, za_p, zb_p = up(a_m), down(za), across(b_p)
    out = correlate(
        place,
        (
            (0, 0, ((0, 0), (2, 1), (3, 6), (4, 2))),
            (EARLY, 1, ((1, 0), (5, 1), (6, 6), (7, 2))),
        ),
        (a, b, za, a_m, a_p, zb, b_m, b_p),
    )
    (za_m, b_o), out = after((za_m, b_o), out)
    za_o, zb_o = up(za_m), across(b_o)
    out = correlate(
        place,
        (
            (0, 0, ((2, 7), (3, 3), (4, 4))),
            (EARLY, 1, ((5, 7), (6, 3), (7, 4))),
        ),
        (a, b, za_m, za_p, a_o, zb_m, zb_p, b_o),
        out,
    )
    done = correlate(place, ((0, 0, ((1, 5),)),), (a, za_o), out, last=True)
    done = correlate(place, ((EARLY, 0, ((1, 5),)),), (b, zb_o), out, last=True, earlier=done)
    return tuple(done)


def solution(mesh):
    axes = ("x", "z_lo") + FREQ
    fine = Mesh(mesh.devices.reshape(4, 2, 4, 4, 2), axes)
    return jax.shard_map(
        on_device,
        mesh=fine,
        in_specs=(P(axes, None), P()),
        out_specs=(P(FREQ, axes[:2], None), P(FREQ, axes[:2], None)),
        check_vma=False,
    )
```

time: 143 us -> 118 us (0.83)
  starting transfers between devices: 31.5 us -> 13.3 us
  local copies, waits for them, and re-layouts: 14.6 us -> 0.08 us
  blocking collectives: 28.2 us -> 39.4 us
  Pallas kernels: 27 us -> 21.1 us
  waiting for transfers between devices: 40.2 us -> 43.2 us
    unnamed x52 -> x0, local copies, waits for them, and re-layouts: 14.5 us -> none
    ppermute x28 -> x14, starting transfers between devices: 25.4 us -> 13.3 us  [shift(): lax.ppermute(value, axis, [(i, (i + by) % size) for i in range(size)])]
    all_to_all x1, blocking collectives: 28.2 us -> 39.4 us  [on_device(): lax.all_to_all(pieces, FREQ, split_axis=0, concat_axis=0, tiled=True)]
    all_to_all x1 -> x0, starting transfers between devices: 6.07 us -> none  [exchange(): return lax.all_to_all(pieces, FREQ, split_axis=0, concat_axis=0, tiled=True)]
    pallas_call x6 -> x5, Pallas kernels: 26.2 us -> 20.5 us  [the longest x4 12.9 us: correlate(): pl.pallas_call(lambda *refs: correlate_kernel(plan, last, *refs), out_sha...]
    ppermute x28 -> x14, waiting for transfers between devices: 40.2 us -> 43.2 us  [shift(): lax.ppermute(value, axis, [(i, (i + by) % size) for i in range(size)])]
  transfers between devices with their start and end apart: 29 -> 14, of which waited for: 12 -> 12; matrix products, arithmetic and copies ran while one was open for 0% -> 0% of each run, Pallas kernels for 11% -> 8%
where the time goes in v3:
time: 118 us
  waiting for transfers between devices  43.2 us (37%)
  blocking collectives  39.4 us (33%)
  Pallas kernels  21.1 us (18%)
  starting transfers between devices  13.3 us (11%)
    ppermute x14, waiting for transfers between devices, shift(): lax.ppermute(value, axis, [(i, (i + by) % size) for i in range(size)])  43.2 us
    all_to_all x1, blocking collectives, on_device(): lax.all_to_all(pieces, FREQ, split_axis=0, concat_axis=0, tiled=True)  39.4 us
    ppermute x14, starting transfers between devices, shift(): lax.ppermute(value, axis, [(i, (i + by) % size) for i in range(size)])  13.3 us
    pallas_call x4, Pallas kernels, correlate(): pl.pallas_call(lambda *refs: correlate_kernel(plan, last, *refs), out_sha...  12.9 us
    pallas_call x1, Pallas kernels, filter_and_transform(): pl.pallas_call(lambda *refs: filter_kernel(rows, *refs), out_shape=jax.Sh...  7.64 us
  transfers between devices with their start and end apart: 14, of which 12 were waited for; matrix products, arithmetic and copies ran while one was open for 0% of the time, Pallas kernels for 8%

profile of v3, /device:TPU:8, one launch (start us, length us, event | category | flops | bytes accessed | tf_op | source)
XLA Modules:
  0.0 118.0 jit_solution(10997203757275660381)
XLA Ops:
  0.6 7.6 %filter_and_transform.1 = bf16[32,4,32,128]{3,2,1,0:T(8,128)(2,1)} custom-call(s32[131,64,128]{2,1,0:T(8,128)} %bitcast.15, f32[4,2048]{1,0:T(4,128)} %refs_1_.1, bf16[1024,2048]{1,0:T(8,128)(2,1)} %constant.77.clone.refs_2_), custom_call_target="tpu_custom_call" | custom-call | flops 1000 | bytes 1000 | tf_op jit(solution)/shard_map/filter_and_transform/pallas_call | solution.py:105
  8.3 39.4 %all_to_all.5 = bf16[32,4,32,128]{3,2,1,0:T(8,128)(2,1)S(1)} all-to-all(bf16[32,4,32,128]{3,2,1,0:T(8,128)(2,1)} %filter_and_transform.1), channel_id=1, replica_groups=mesh['x'=4,'z_lo'=2,'y'=4,'z_hi'=4,'core'=2] {'y','z_hi','core'}, dimensions={0} | all-to-all | bytes 2097152 | tf_op jit(solution)/shard_map/all_to_all | solution.py:249
  47.7 0.6 assemble.1
  48.2 1.7 %collective-permute-start.2 = (bf16[8,128,256]{2,1,0:T(8,128)(2,1)S(1)}, bf16[8,128,256]{2,1,0:T(8,128)(2,1)S(1)}, u32[]{:S(2)}, u32[]{:S(2)}) collective-permute-start(bf16[8,128,256]{2,1,0:T(8,128)(2,1)S(1)} %get-tuple-element.17.refs_2_.refs_1_), channel_id=1, source_target_pairs={{0,64},{64,128},{128,192},{192,0},{1,65},{65,129},{129,193},{193,1... | collective-permute-start | bytes 1572872 | tf_op jit(solution)/shard_map/ppermute | solution.py:225
  49.9 1.6 %collective-permute-start.1 = (bf16[8,128,256]{2,1,0:T(8,128)(2,1)S(1)}, bf16[8,128,256]{2,1,0:T(8,128)(2,1)S(1)}, u32[]{:S(2)}, u32[]{:S(2)}) collective-permute-start(bf16[8,128,256]{2,1,0:T(8,128)(2,1)S(1)} %get-tuple-element.17.refs_2_.refs_1_), channel_id=1, source_target_pairs={{0,192},{64,0},{128,64},{192,128},{1,193},{65,1},{129,65},{193,129... | collective-permute-start | bytes 1572872 | tf_op jit(solution)/shard_map/ppermute | solution.py:225
  51.5 0.0 collective-permute-start
  51.6 0.4 collective-permute-start.5
  51.9 2.0 %collective-permute-start.7 = (bf16[8,128,256]{2,1,0:T(8,128)(2,1)S(1)}, bf16[8,128,256]{2,1,0:T(8,128)(2,1)}, u32[]{:S(2)}, u32[]{:S(2)}) collective-permute-start(bf16[8,128,256]{2,1,0:T(8,128)(2,1)S(1)} %get-tuple-element.17.refs_2_.refs_1_), channel_id=1, source_target_pairs={{0,32},{32,0},{1,33},{33,1},{2,34},{34,2},{3,35},{35,3},{4,36},{36... | collective-permute-start | bytes 1572872 | tf_op jit(solution)/shard_map/ppermute | solution.py:225
  53.9 10.4 %collective-permute-done.2.refs_7_ = bf16[8,128,256]{2,1,0:T(8,128)(2,1)S(1)} collective-permute-done((bf16[8,128,256]{2,1,0:T(8,128)(2,1)S(1)}, bf16[8,128,256]{2,1,0:T(8,128)(2,1)S(1)}, u32[]{:S(2)}, u32[]{:S(2)}) %collective-permute-start.2) | collective-permute-done | bytes 524320 | tf_op jit(solution)/shard_map/ppermute | solution.py:225
  64.3 1.5 %collective-permute-start.6 = (bf16[8,128,256]{2,1,0:T(8,128)(2,1)S(1)}, bf16[8,128,256]{2,1,0:T(8,128)(2,1)}, u32[]{:S(2)}, u32[]{:S(2)}) collective-permute-start(bf16[8,128,256]{2,1,0:T(8,128)(2,1)S(1)} %get-tuple-element.18.refs_1_), channel_id=1, source_target_pairs={{0,192},{64,0},{128,64},{192,128},{1,193},{65,1},{129,65},{193,129... | collective-permute-start | bytes 1572872 | tf_op jit(solution)/shard_map/ppermute | solution.py:225
  65.8 0.0 collective-permute-done.1.refs_8_
  65.9 0.4 collective-permute-done.refs_3_
  66.3 0.4 collective-permute-start.3
  66.7 2.8 %collective-permute-start.4 = (bf16[8,128,256]{2,1,0:T(8,128)(2,1)S(1)}, bf16[8,128,256]{2,1,0:T(8,128)(2,1)S(1)}, u32[]{:S(2)}, u32[]{:S(2)}) collective-permute-start(bf16[8,128,256]{2,1,0:T(8,128)(2,1)S(1)} %collective-permute-done.1.refs_8_), channel_id=1, source_target_pairs={{0,192},{64,0},{128,64},{192,128},{1,193},{65,1},{129,65},{193,129... | collective-permute-start | bytes 1572872 | tf_op jit(solution)/shard_map/ppermute | solution.py:225
  69.5 6.1 %collective-permute-done.5.refs_4_ = bf16[8,128,256]{2,1,0:T(8,128)(2,1)} collective-permute-done((bf16[8,128,256]{2,1,0:T(8,128)(2,1)S(1)}, bf16[8,128,256]{2,1,0:T(8,128)(2,1)}, u32[]{:S(2)}, u32[]{:S(2)}) %collective-permute-start.5) | collective-permute-done | bytes 524320 | tf_op jit(solution)/shard_map/ppermute | solution.py:225
  75.6 0.4 collective-permute-start.10
  76.0 0.1 stack.35.refs_0_
  76.1 0.9 collective-permute-done.7.refs_6_
  77.1 2.0 %collective-permute-start.9 = (bf16[8,128,256]{2,1,0:T(8,128)(2,1)S(1)}, bf16[8,128,256]{2,1,0:T(8,128)(2,1)S(1)}, u32[]{:S(2)}, u32[]{:S(2)}) collective-permute-start(bf16[8,128,256]{2,1,0:T(8,128)(2,1)S(1)} %collective-permute-done.refs_3_), channel_id=1, source_target_pairs={{0,192},{64,0},{128,64},{192,128},{1,193},{65,1},{129,65},{193,129... | collective-permute-start | bytes 1572872 | tf_op jit(solution)/shard_map/ppermute | solution.py:225
  79.0 0.2 collective-permute-done.6.refs_5_
  79.2 0.0 collective-permute-start.11
  79.2 3.7 %correlate.4 = (bf16[16,128,1024]{2,1,0:T(8,128)(2,1)S(1)}, bf16[16,128,1024]{2,1,0:T(8,128)(2,1)S(1)}) custom-call(s32[8]{0:T(128)S(1)} %stack.35.refs_0_, bf16[8,128,256]{2,1,0:T(8,128)(2,1)S(1)} %get-tuple-element.18.refs_1_, bf16[8,128,256]{2,1,0:T(8,128)(2,1)S(1)} %get-tuple-element.17.refs_2_.refs_1_, ...), custom_call_target="tpu_custom_call" | custom-call | flops 1000 | bytes 1000 | tf_op jit(solution)/shard_map/correlate/pallas_call | solution.py:210
  82.9 4.0 %collective-permute-done.3.refs_3_ = bf16[8,128,256]{2,1,0:T(8,128)(2,1)} collective-permute-done((bf16[8,128,256]{2,1,0:T(8,128)(2,1)S(1)}, bf16[8,128,256]{2,1,0:T(8,128)(2,1)}, u32[]{:S(2)}, u32[]{:S(2)}) %collective-permute-start.3) | collective-permute-done | bytes 524320 | tf_op jit(solution)/shard_map/ppermute | solution.py:225
  86.9 0.0 collective-permute-start.12
  86.9 3.4 %collective-permute-done.4.refs_8_ = bf16[8,128,256]{2,1,0:T(8,128)(2,1)S(1)} collective-permute-done((bf16[8,128,256]{2,1,0:T(8,128)(2,1)S(1)}, bf16[8,128,256]{2,1,0:T(8,128)(2,1)S(1)}, u32[]{:S(2)}, u32[]{:S(2)}) %collective-permute-start.4) | collective-permute-done | bytes 524320 | tf_op jit(solution)/shard_map/ppermute | solution.py:225
  90.3 0.4 collective-permute-start.13
  90.8 7.4 %collective-permute-done.10.refs_5_ = bf16[8,128,256]{2,1,0:T(8,128)(2,1)} collective-permute-done((bf16[8,128,256]{2,1,0:T(8,128)(2,1)}, bf16[8,128,256]{2,1,0:T(8,128)(2,1)}, u32[]{:S(2)}, u32[]{:S(2)}) %collective-permute-start.10) | collective-permute-done | bytes 524320 | tf_op jit(solution)/shard_map/ppermute | solution.py:225
  98.1 0.0 collective-permute-start.8
  98.1 0.0 collective-permute-done.11.refs_6_
  98.1 2.5 %collective-permute-done.9.refs_4_ = bf16[8,128,256]{2,1,0:T(8,128)(2,1)S(1)} collective-permute-done((bf16[8,128,256]{2,1,0:T(8,128)(2,1)S(1)}, bf16[8,128,256]{2,1,0:T(8,128)(2,1)S(1)}, u32[]{:S(2)}, u32[]{:S(2)}) %collective-permute-start.9) | collective-permute-done | bytes 524320 | tf_op jit(solution)/shard_map/ppermute | solution.py:225
  100.6 4.7 %collective-permute-done.12.refs_7_ = bf16[8,128,256]{2,1,0:T(8,128)(2,1)S(1)} collective-permute-done((bf16[8,128,256]{2,1,0:T(8,128)(2,1)S(1)}, bf16[8,128,256]{2,1,0:T(8,128)(2,1)S(1)}, u32[]{:S(2)}, u32[]{:S(2)}) %collective-permute-start.12) | collective-permute-done | bytes 524320 | tf_op jit(solution)/shard_map/ppermute | solution.py:225
  105.3 3.2 %correlate.5 = (bf16[16,128,1024]{2,1,0:T(8,128)(2,1)S(1)}, bf16[16,128,1024]{2,1,0:T(8,128)(2,1)S(1)}) custom-call(s32[8]{0:T(128)S(1)} %stack.35.refs_0_, bf16[8,128,256]{2,1,0:T(8,128)(2,1)S(1)} %get-tuple-element.18.refs_1_, bf16[8,128,256]{2,1,0:T(8,128)(2,1)S(1)} %get-tuple-element.17.refs_2_.refs_1_, ...), custom_call_target="tpu_custom_call", output_to_operand_aliasing={{0}: (9, {}), {1}: (10, {})} | custom-call | flops 1000 | bytes 1000 | tf_op jit(solution)/shard_map/correlate/pallas_call | solution.py:210
  108.5 0.7 collective-permute-done.13.refs_2_
  109.2 3.0 %correlate.6 = (bf16[16,128,1024]{2,1,0:T(8,128)(2,1)}, bf16[16,128,1024]{2,1,0:T(8,128)(2,1)}) custom-call(s32[8]{0:T(128)S(1)} %stack.35.refs_0_, bf16[8,128,256]{2,1,0:T(8,128)(2,1)S(1)} %get-tuple-element.18.refs_1_, bf16[8,128,256]{2,1,0:T(8,128)(2,1)S(1)} %collective-permute-done.13.refs_2_, bf16[16,128,1024]{2,1,0:T(8,128)(2,1)S(1)} %get-tuple-element.28.refs_3_, ...), custom_call_target="tpu_custom_call" | custom-call | flops 1000 | bytes 1000 | tf_op jit(solution)/shard_map/correlate/pallas_call | solution.py:210
  112.2 2.6 %collective-permute-done.8.refs_2_ = bf16[8,128,256]{2,1,0:T(8,128)(2,1)S(1)} collective-permute-done((bf16[8,128,256]{2,1,0:T(8,128)(2,1)S(1)}, bf16[8,128,256]{2,1,0:T(8,128)(2,1)S(1)}, u32[]{:S(2)}, u32[]{:S(2)}) %collective-permute-start.8) | collective-permute-done | bytes 524320 | tf_op jit(solution)/shard_map/ppermute | solution.py:225
  114.8 3.0 %correlate.7 = (bf16[16,128,1024]{2,1,0:T(8,128)(2,1)}, bf16[16,128,1024]{2,1,0:T(8,128)(2,1)}) custom-call(s32[8]{0:T(128)S(1)} %stack.35.refs_0_, bf16[8,128,256]{2,1,0:T(8,128)(2,1)S(1)} %get-tuple-element.17.refs_2_.refs_1_, bf16[8,128,256]{2,1,0:T(8,128)(2,1)S(1)} %collective-permute-done.8.refs_2_, ...), custom_call_target="tpu_custom_call", output_to_operand_aliasing={{0}: (5, {}), {1}: (6, {})} | custom-call | flops 1000 | bytes 1000 | tf_op jit(solution)/shard_map/correlate/pallas_call | solution.py:210
Async XLA Ops:
  48.2 16.1 %collective-permute-start.2 = (bf16[8,128,256]{2,1,0:T(8,128)(2,1)S(1)}, bf16[8,128,256]{2,1,0:T(8,128)(2,1)S(1)}, u32[]{:S(2)}, u32[]{:S(2)}) collective-permute-start(bf16[8,128,256]{2,1,0:T(8,128)(2,1)S(1)} %get-tuple-element.17.refs_2_.refs_1_), channel_id=1, source_target_pairs={{0,64},{64,128},{128,192},{192,0},{1,65},{65,129},{129,193},{193,1... | collective-permute-start | bytes 1572872 | tf_op jit(solution)/shard_map/ppermute | solution.py:225
  49.9 16.0 %collective-permute-start.1 = (bf16[8,128,256]{2,1,0:T(8,128)(2,1)S(1)}, bf16[8,128,256]{2,1,0:T(8,128)(2,1)S(1)}, u32[]{:S(2)}, u32[]{:S(2)}) collective-permute-start(bf16[8,128,256]{2,1,0:T(8,128)(2,1)S(1)} %get-tuple-element.17.refs_2_.refs_1_), channel_id=1, source_target_pairs={{0,192},{64,0},{128,64},{192,128},{1,193},{65,1},{129,65},{193,129... | collective-permute-start | bytes 1572872 | tf_op jit(solution)/shard_map/ppermute | solution.py:225
  51.5 14.7 %collective-permute-start = (bf16[8,128,256]{2,1,0:T(8,128)(2,1)S(1)}, bf16[8,128,256]{2,1,0:T(8,128)(2,1)S(1)}, u32[]{:S(2)}, u32[]{:S(2)}) collective-permute-start(bf16[8,128,256]{2,1,0:T(8,128)(2,1)S(1)} %get-tuple-element.18.refs_1_), channel_id=1, source_target_pairs={{0,32},{32,0},{1,33},{33,1},{2,34},{34,2},{3,35},{35,3},{4,36},{36... | collective-permute-start | bytes 1572872 | tf_op jit(solution)/shard_map/ppermute | solution.py:225
  51.6 24.1 %collective-permute-start.5 = (bf16[8,128,256]{2,1,0:T(8,128)(2,1)S(1)}, bf16[8,128,256]{2,1,0:T(8,128)(2,1)}, u32[]{:S(2)}, u32[]{:S(2)}) collective-permute-start(bf16[8,128,256]{2,1,0:T(8,128)(2,1)S(1)} %get-tuple-element.18.refs_1_), channel_id=1, source_target_pairs={{0,64},{64,128},{128,192},{192,0},{1,65},{65,129},{129,193},{193,1... | collective-permute-start | bytes 1572872 | tf_op jit(solution)/shard_map/ppermute | solution.py:225
  51.9 25.1 %collective-permute-start.7 = (bf16[8,128,256]{2,1,0:T(8,128)(2,1)S(1)}, bf16[8,128,256]{2,1,0:T(8,128)(2,1)}, u32[]{:S(2)}, u32[]{:S(2)}) collective-permute-start(bf16[8,128,256]{2,1,0:T(8,128)(2,1)S(1)} %get-tuple-element.17.refs_2_.refs_1_), channel_id=1, source_target_pairs={{0,32},{32,0},{1,33},{33,1},{2,34},{34,2},{3,35},{35,3},{4,36},{36... | collective-permute-start | bytes 1572872 | tf_op jit(solution)/shard_map/ppermute | solution.py:225
  64.3 14.9 %collective-permute-start.6 = (bf16[8,128,256]{2,1,0:T(8,128)(2,1)S(1)}, bf16[8,128,256]{2,1,0:T(8,128)(2,1)}, u32[]{:S(2)}, u32[]{:S(2)}) collective-permute-start(bf16[8,128,256]{2,1,0:T(8,128)(2,1)S(1)} %get-tuple-element.18.refs_1_), channel_id=1, source_target_pairs={{0,192},{64,0},{128,64},{192,128},{1,193},{65,1},{129,65},{193,129... | collective-permute-start | bytes 1572872 | tf_op jit(solution)/shard_map/ppermute | solution.py:225
  66.3 20.6 %collective-permute-start.3 = (bf16[8,128,256]{2,1,0:T(8,128)(2,1)S(1)}, bf16[8,128,256]{2,1,0:T(8,128)(2,1)}, u32[]{:S(2)}, u32[]{:S(2)}) collective-permute-start(bf16[8,128,256]{2,1,0:T(8,128)(2,1)S(1)} %collective-permute-done.refs_3_), channel_id=1, source_target_pairs={{0,64},{64,128},{128,192},{192,0},{1,65},{65,129},{129,193},{193,1... | collective-permute-start | bytes 1572872 | tf_op jit(solution)/shard_map/ppermute | solution.py:225
  66.7 23.6 %collective-permute-start.4 = (bf16[8,128,256]{2,1,0:T(8,128)(2,1)S(1)}, bf16[8,128,256]{2,1,0:T(8,128)(2,1)S(1)}, u32[]{:S(2)}, u32[]{:S(2)}) collective-permute-start(bf16[8,128,256]{2,1,0:T(8,128)(2,1)S(1)} %collective-permute-done.1.refs_8_), channel_id=1, source_target_pairs={{0,192},{64,0},{128,64},{192,128},{1,193},{65,1},{129,65},{193,129... | collective-permute-start | bytes 1572872 | tf_op jit(solution)/shard_map/ppermute | solution.py:225
  75.6 22.5 %collective-permute-start.10 = (bf16[8,128,256]{2,1,0:T(8,128)(2,1)}, bf16[8,128,256]{2,1,0:T(8,128)(2,1)}, u32[]{:S(2)}, u32[]{:S(2)}) collective-permute-start(bf16[8,128,256]{2,1,0:T(8,128)(2,1)} %collective-permute-done.5.refs_4_), channel_id=1, source_target_pairs={{0,64},{64,128},{128,192},{192,0},{1,65},{65,129},{129,193},{193,1... | collective-permute-start | bytes 1572872 | tf_op jit(solution)/shard_map/ppermute | solution.py:225
  77.1 23.5 %collective-permute-start.9 = (bf16[8,128,256]{2,1,0:T(8,128)(2,1)S(1)}, bf16[8,128,256]{2,1,0:T(8,128)(2,1)S(1)}, u32[]{:S(2)}, u32[]{:S(2)}) collective-permute-start(bf16[8,128,256]{2,1,0:T(8,128)(2,1)S(1)} %collective-permute-done.refs_3_), channel_id=1, source_target_pairs={{0,192},{64,0},{128,64},{192,128},{1,193},{65,1},{129,65},{193,129... | collective-permute-start | bytes 1572872 | tf_op jit(solution)/shard_map/ppermute | solution.py:225
  79.2 18.9 %collective-permute-start.11 = (bf16[8,128,256]{2,1,0:T(8,128)(2,1)S(1)}, bf16[8,128,256]{2,1,0:T(8,128)(2,1)S(1)}, u32[]{:S(2)}, u32[]{:S(2)}) collective-permute-start(bf16[8,128,256]{2,1,0:T(8,128)(2,1)S(1)} %collective-permute-done.2.refs_7_), channel_id=1, source_target_pairs={{0,32},{32,0},{1,33},{33,1},{2,34},{34,2},{3,35},{35,3},{4,36},{36... | collective-permute-start | bytes 1572872 | tf_op jit(solution)/shard_map/ppermute | solution.py:225
  86.9 18.4 %collective-permute-start.12 = (bf16[8,128,256]{2,1,0:T(8,128)(2,1)S(1)}, bf16[8,128,256]{2,1,0:T(8,128)(2,1)S(1)}, u32[]{:S(2)}, u32[]{:S(2)}) collective-permute-start(bf16[8,128,256]{2,1,0:T(8,128)(2,1)S(1)} %collective-permute-done.1.refs_8_), channel_id=1, source_target_pairs={{0,32},{32,0},{1,33},{33,1},{2,34},{34,2},{3,35},{35,3},{4,36},{36... | collective-permute-start | bytes 1572872 | tf_op jit(solution)/shard_map/ppermute | solution.py:225
  90.3 18.9 %collective-permute-start.13 = (bf16[8,128,256]{2,1,0:T(8,128)(2,1)}, bf16[8,128,256]{2,1,0:T(8,128)(2,1)S(1)}, u32[]{:S(2)}, u32[]{:S(2)}) collective-permute-start(bf16[8,128,256]{2,1,0:T(8,128)(2,1)} %collective-permute-done.3.refs_3_), channel_id=1, source_target_pairs={{0,64},{64,128},{128,192},{192,0},{1,65},{65,129},{129,193},{193,1... | collective-permute-start | bytes 1572872 | tf_op jit(solution)/shard_map/ppermute | solution.py:225
  98.1 16.7 %collective-permute-start.8 = (bf16[8,128,256]{2,1,0:T(8,128)(2,1)S(1)}, bf16[8,128,256]{2,1,0:T(8,128)(2,1)S(1)}, u32[]{:S(2)}, u32[]{:S(2)}) collective-permute-start(bf16[8,128,256]{2,1,0:T(8,128)(2,1)S(1)} %collective-permute-done.4.refs_8_), channel_id=1, source_target_pairs={{0,32},{32,0},{1,33},{33,1},{2,34},{34,2},{3,35},{35,3},{4,36},{36... | collective-permute-start | bytes 1572872 | tf_op jit(solution)/shard_map/ppermute | solution.py:225

commit v4 on v3

--- a/solution.py
+++ b/solution.py
@@ -158,19 +158,16 @@
     return (lax.dot_general(left, other, NT, preferred_element_type=F32) * (1.0 / SPEC)).astype(BF16)
 
 
-def correlate_kernel(plan, last, place_ref, *refs):
-    count = 1 + max(k for part in plan for k in (part[1],) + tuple(b for b, _ in part[2]))
+def correlate_kernel(plan, count, place_ref, *refs):
     blocks, refs = refs[:count], refs[count:]
-    if last:
-        re_ref, im_ref = refs[:2]
-        re_out, im_out, sem = refs[-3:]
+    copies = []
+    if len(refs) == 2:
+        re_ref, im_ref = refs
     else:
-        re_ref, im_ref = refs[-2:]
-    copies = []
+        re_ref, im_ref, re_out, im_out, sem = refs[-5:]
     for lo, own, others in plan:
-        size = blocks[own].shape[0]
-
-        def one(c):
+
+        def one(c, carry):
             for k in range(0, len(others), 2):
                 pair = others[k : k + 2]
                 right = jnp.concatenate([blocks[b][c] for b, _ in pair], axis=0)
@@ -179,45 +176,73 @@
                     cols = pl.ds(pl.multiple_of(place_ref[spot], SPEC), SPEC)
                     re_ref[lo + c, :, cols] = out[:SPEC, h * SPEC : (h + 1) * SPEC]
                     im_ref[lo + c, :, cols] = out[SPEC:, h * SPEC : (h + 1) * SPEC]
-
-        if last:
-            for c in range(size):
-                one(c)
-                for k, (src, dst) in enumerate(((re_ref, re_out), (im_ref, im_out))):
-                    copies.append(pltpu.make_async_copy(src.at[lo + c], dst.at[lo + c], sem.at[k, lo + c]))
+            return carry
+
+        size = blocks[own].shape[0]
+        lax.fori_loop(0, size, one, 0, unroll=4)
+        if len(refs) > 2:
+            for k, (src, dst) in enumerate(((re_ref, re_out), (im_ref, im_out))):
+                for c in range(lo, lo + size):
+                    copies.append(pltpu.make_async_copy(src.at[c], dst.at[c], sem.at[k, c]))
                     copies[-1].start()
-        else:
-            lax.fori_loop(0, size, lambda c, carry: (one(c), carry)[1], 0, unroll=4)
     for copy in copies:
         copy.wait()
 
 
-def correlate(place, plan, blocks, so_far=None, last=False, earlier=None):
+def correlate(place, plan, blocks, so_far=None):
     shape = jax.ShapeDtypeStruct((CH, SPEC, SPEC * GROUPS), BF16)
     vmem = pl.BlockSpec(memory_space=pltpu.VMEM)
+    count = len(blocks)
+    second = so_far is not None
     operands = [place] + list(blocks) + list(so_far or ())
-    in_specs = [pl.BlockSpec(memory_space=pltpu.SMEM)] + [vmem] * (len(operands) - 1)
-    aliases, scratch, out_specs = {}, [], [vmem] * 2
-    if last:
-        out_specs = [pl.BlockSpec(memory_space=pl.ANY)] * 2
-        scratch = [pltpu.SemaphoreType.DMA((2, CH))]
-        if earlier is not None:
-            aliases = {len(operands): 0, len(operands) + 1: 1}
-            operands += list(earlier)
-            in_specs += out_specs
-    elif so_far is not None:
-        aliases = {1 + len(blocks): 0, 2 + len(blocks): 1}
-    return pl.pallas_call(
-        lambda *refs: correlate_kernel(plan, last, *refs),
-        out_shape=[shape, shape],
-        in_specs=in_specs,
-        out_specs=out_specs,
-        scratch_shapes=scratch,
-        input_output_aliases=aliases,
+    out = pl.pallas_call(
+        lambda *refs: correlate_kernel(plan, count, *refs),
+        out_shape=[shape] * (4 if second else 2),
+        in_specs=[pl.BlockSpec(memory_space=pltpu.SMEM)] + [vmem] * (len(operands) - 1),
+        out_specs=[vmem] * 2 + [pl.BlockSpec(memory_space=pl.ANY)] * (2 if second else 0),
+        scratch_shapes=[pltpu.SemaphoreType.DMA((2, CH))] if second else [],
+        input_output_aliases={1 + count: 0, 2 + count: 1} if second else {},
         compiler_params=pltpu.CompilerParams(vmem_limit_bytes=16 * MIB),
         cost_estimate=LIGHT,
         name="correlate",
     )(*operands)
+    return out[-2:]
+
+
+def last_kernel(parts, place_ref, *refs):
+    blocks = refs[: 2 * parts]
+    re_out, im_out, re_ref, im_ref, sem = refs[-5:]
+    cols = pl.ds(pl.multiple_of(place_ref[5], SPEC), SPEC)
+    copies, at = [], 0
+    for k in range(parts):
+        own_ref, other_ref = blocks[2 * k : 2 * k + 2]
+        for c in range(own_ref.shape[0]):
+            out = products(own_ref[c], other_ref[c])
+            re_ref[at + c], im_ref[at + c] = out[:SPEC], out[SPEC:]
+        for c in range(at, at + own_ref.shape[0]):
+            for k2, (src, dst) in enumerate(((re_ref, re_out), (im_ref, im_out))):
+                copies.append(pltpu.make_async_copy(src.at[c], dst.at[c, :, cols], sem.at[k2, c]))
+                copies[-1].start()
+        at += own_ref.shape[0]
+    for copy in copies:
+        copy.wait()
+
+
+def correlate_last(place, blocks, done):
+    shape = jax.ShapeDtypeStruct((CH, SPEC, SPEC * GROUPS), BF16)
+    vmem, anywhere = pl.BlockSpec(memory_space=pltpu.VMEM), pl.BlockSpec(memory_space=pl.ANY)
+    count = len(blocks)
+    return pl.pallas_call(
+        lambda *refs: last_kernel(count // 2, *refs),
+        out_shape=[shape] * 2,
+        in_specs=[pl.BlockSpec(memory_space=pltpu.SMEM)] + [vmem] * count + [anywhere] * 2,
+        out_specs=[anywhere] * 2,
+        scratch_shapes=[pltpu.VMEM((CH, SPEC, SPEC), BF16)] * 2 + [pltpu.SemaphoreType.DMA((2, CH))],
+        input_output_aliases={1 + count: 0, 2 + count: 1},
+        compiler_params=pltpu.CompilerParams(vmem_limit_bytes=8 * MIB),
+        cost_estimate=LIGHT,
+        name="correlate_last",
+    )(place, *blocks, *done)
 
 
 def shift(value, axis, by):
@@ -252,7 +277,8 @@
     a_m, a_p, zb = up(a), down(a), across(b)
     (za, b_p, b_m), _ = after((za, b_p, b_m), (za, b_p, b_m))
     za_m, b_o, zb_m = up(za), down(b_p), across(b_m)
-    a_o, za_p, zb_p = up(a_m), down(za), across(b_p)
+    za_p = down(after(za, b_o)[0])
+    a_o, zb_p = up(a_m), across(b_p)
     out = correlate(
         place,
         (
@@ -272,9 +298,7 @@
         (a, b, za_m, za_p, a_o, zb_m, zb_p, b_o),
         out,
     )
-    done = correlate(place, ((0, 0, ((1, 5),)),), (a, za_o), out, last=True)
-    done = correlate(place, ((EARLY, 0, ((1, 5),)),), (b, zb_o), out, last=True, earlier=done)
-    return tuple(done)
+    return tuple(correlate_last(place, (a, za_o, b, zb_o), out))
 
 
 def solution(mesh):

time: 118 us -> 117 us (level)
  Pallas kernels: 21.1 us -> 19.9 us
    pallas_call x4 -> x3, Pallas kernels: 12.9 us -> 11.7 us  [the longest x2 9.42 us: correlate(): pl.pallas_call(lambda *refs: correlate_kernel(plan, count, *refs), out_sh...]
  transfers between devices with their start and end apart: 14 -> 14, of which waited for: 12 -> 10; matrix products, arithmetic and copies ran while one was open for 0% -> 0% of each run, Pallas kernels for 8% -> 8%
where the time goes in v4:
time: 117 us
  waiting for transfers between devices  42.5 us (36%)
  blocking collectives  39.4 us (34%)
  Pallas kernels  19.9 us (17%)
  starting transfers between devices  14.3 us (12%)
    ppermute x14, waiting for transfers between devices, shift(): lax.ppermute(value, axis, [(i, (i + by) % size) for i in range(size)])  42.5 us
    all_to_all x1, blocking collectives, on_device(): lax.all_to_all(pieces, FREQ, split_axis=0, concat_axis=0, tiled=True)  39.4 us
    ppermute x14, starting transfers between devices, shift(): lax.ppermute(value, axis, [(i, (i + by) % size) for i in range(size)])  14.3 us
    pallas_call x2, Pallas kernels, correlate(): pl.pallas_call(lambda *refs: correlate_kernel(plan, count, *refs), out_sh...  9.42 us
    pallas_call x1, Pallas kernels, filter_and_transform(): pl.pallas_call(lambda *refs: filter_kernel(rows, *refs), out_shape=jax.Sh...  7.64 us
  transfers between devices with their start and end apart: 14, of which 10 were waited for; matrix products, arithmetic and copies ran while one was open for 0% of the time, Pallas kernels for 8%

profile of v4, /device:TPU:8, one launch (start us, length us, event | category | flops | bytes accessed | tf_op | source)
XLA Modules:
  0.0 117.0 jit_solution(10949579038905363056)
XLA Ops:
  0.6 7.6 %filter_and_transform.1 = bf16[32,4,32,128]{3,2,1,0:T(8,128)(2,1)} custom-call(s32[131,64,128]{2,1,0:T(8,128)} %bitcast.15, f32[4,2048]{1,0:T(4,128)} %refs_1_.1, bf16[1024,2048]{1,0:T(8,128)(2,1)} %constant.77.clone.refs_2_), custom_call_target="tpu_custom_call" | custom-call | flops 1000 | bytes 1000 | tf_op jit(solution)/shard_map/filter_and_transform/pallas_call | solution.py:105
  8.3 39.4 %all_to_all.5 = bf16[32,4,32,128]{3,2,1,0:T(8,128)(2,1)S(1)} all-to-all(bf16[32,4,32,128]{3,2,1,0:T(8,128)(2,1)} %filter_and_transform.1), channel_id=1, replica_groups=mesh['x'=4,'z_lo'=2,'y'=4,'z_hi'=4,'core'=2] {'y','z_hi','core'}, dimensions={0} | all-to-all | bytes 2097152 | tf_op jit(solution)/shard_map/all_to_all | solution.py:274
  47.7 0.6 assemble.1
  48.2 0.1 collective-permute-start
  48.3 2.8 %collective-permute-start.1 = (bf16[8,128,256]{2,1,0:T(8,128)(2,1)S(1)}, bf16[8,128,256]{2,1,0:T(8,128)(2,1)}, u32[]{:S(2)}, u32[]{:S(2)}) collective-permute-start(bf16[8,128,256]{2,1,0:T(8,128)(2,1)S(1)} %get-tuple-element.17.refs_2_.refs_3_), channel_id=1, source_target_pairs={{0,192},{64,0},{128,64},{192,128},{1,193},{65,1},{129,65},{193,129... | collective-permute-start | bytes 1572872 | tf_op jit(solution)/shard_map/ppermute | solution.py:250
  51.2 0.0 collective-permute-start.2
  51.2 0.9 collective-permute-start.5
  52.0 2.4 %collective-permute-start.6 = (bf16[8,128,256]{2,1,0:T(8,128)(2,1)S(1)}, bf16[8,128,256]{2,1,0:T(8,128)(2,1)}, u32[]{:S(2)}, u32[]{:S(2)}) collective-permute-start(bf16[8,128,256]{2,1,0:T(8,128)(2,1)S(1)} %get-tuple-element.16.refs_1_), channel_id=1, source_target_pairs={{0,192},{64,0},{128,64},{192,128},{1,193},{65,1},{129,65},{193,129... | collective-permute-start | bytes 1572872 | tf_op jit(solution)/shard_map/ppermute | solution.py:250
  54.4 8.6 %collective-permute-done.refs_3_ = bf16[8,128,256]{2,1,0:T(8,128)(2,1)S(1)} collective-permute-done((bf16[8,128,256]{2,1,0:T(8,128)(2,1)S(1)}, bf16[8,128,256]{2,1,0:T(8,128)(2,1)S(1)}, u32[]{:S(2)}, u32[]{:S(2)}) %collective-permute-start) | collective-permute-done | bytes 524320 | tf_op jit(solution)/shard_map/ppermute | solution.py:250
  63.0 0.0 collective-permute-start.7
  63.0 0.4 collective-permute-done.1.refs_8_
  63.4 3.7 %collective-permute-done.2.refs_7_ = bf16[8,128,256]{2,1,0:T(8,128)(2,1)S(1)} collective-permute-done((bf16[8,128,256]{2,1,0:T(8,128)(2,1)S(1)}, bf16[8,128,256]{2,1,0:T(8,128)(2,1)S(1)}, u32[]{:S(2)}, u32[]{:S(2)}) %collective-permute-start.2) | collective-permute-done | bytes 524320 | tf_op jit(solution)/shard_map/ppermute | solution.py:250
  67.2 0.1 collective-permute-start.4
  67.2 2.0 %collective-permute-start.3 = (bf16[8,128,256]{2,1,0:T(8,128)(2,1)S(1)}, bf16[8,128,256]{2,1,0:T(8,128)(2,1)}, u32[]{:S(2)}, u32[]{:S(2)}) collective-permute-start(bf16[8,128,256]{2,1,0:T(8,128)(2,1)S(1)} %collective-permute-done.refs_3_), channel_id=1, source_target_pairs={{0,64},{64,128},{128,192},{192,0},{1,65},{65,129},{129,193},{193,1... | collective-permute-start | bytes 1572872 | tf_op jit(solution)/shard_map/ppermute | solution.py:250
  69.2 9.2 %collective-permute-done.5.refs_4_ = bf16[8,128,256]{2,1,0:T(8,128)(2,1)S(1)} collective-permute-done((bf16[8,128,256]{2,1,0:T(8,128)(2,1)S(1)}, bf16[8,128,256]{2,1,0:T(8,128)(2,1)S(1)}, u32[]{:S(2)}, u32[]{:S(2)}) %collective-permute-start.5) | collective-permute-done | bytes 524320 | tf_op jit(solution)/shard_map/ppermute | solution.py:250
  78.4 1.9 %collective-permute-start.13 = (bf16[8,128,256]{2,1,0:T(8,128)(2,1)}, bf16[8,128,256]{2,1,0:T(8,128)(2,1)}, u32[]{:S(2)}, u32[]{:S(2)}) collective-permute-start(bf16[8,128,256]{2,1,0:T(8,128)(2,1)} %collective-permute-done.1.refs_8_), channel_id=1, source_target_pairs={{0,32},{32,0},{1,33},{33,1},{2,34},{34,2},{3,35},{35,3},{4,36},{36... | collective-permute-start | bytes 1572872 | tf_op jit(solution)/shard_map/ppermute | solution.py:250
  80.3 0.1 stack.35.refs_0_
  80.4 0.0 collective-permute-done.6.refs_5_
  80.4 0.2 collective-permute-start.12
  80.6 0.0 collective-permute-done.7.refs_6_
  80.6 0.0 collective-permute-start.11
  80.6 3.7 %correlate.2 = (bf16[16,128,1024]{2,1,0:T(8,128)(2,1)S(1)}, bf16[16,128,1024]{2,1,0:T(8,128)(2,1)S(1)}) custom-call(s32[8]{0:T(128)S(1)} %stack.35.refs_0_, bf16[8,128,256]{2,1,0:T(8,128)(2,1)S(1)} %get-tuple-element.16.refs_1_, bf16[8,128,256]{2,1,0:T(8,128)(2,1)S(1)} %get-tuple-element.17.refs_2_.refs_3_, ...), custom_call_target="tpu_custom_call" | custom-call | flops 1000 | bytes 1000 | tf_op jit(solution)/shard_map/correlate/pallas_call | solution.py:198
  84.3 1.7 %collective-permute-done.4.refs_8_ = bf16[8,128,256]{2,1,0:T(8,128)(2,1)S(1)} collective-permute-done((bf16[8,128,256]{2,1,0:T(8,128)(2,1)}, bf16[8,128,256]{2,1,0:T(8,128)(2,1)S(1)}, u32[]{:S(2)}, u32[]{:S(2)}) %collective-permute-start.4) | collective-permute-done | bytes 524320 | tf_op jit(solution)/shard_map/ppermute | solution.py:250
  86.0 3.7 %collective-permute-done.3.refs_3_ = bf16[8,128,256]{2,1,0:T(8,128)(2,1)} collective-permute-done((bf16[8,128,256]{2,1,0:T(8,128)(2,1)S(1)}, bf16[8,128,256]{2,1,0:T(8,128)(2,1)}, u32[]{:S(2)}, u32[]{:S(2)}) %collective-permute-start.3) | collective-permute-done | bytes 524320 | tf_op jit(solution)/shard_map/ppermute | solution.py:250
  89.7 0.0 collective-permute-start.10
  89.7 2.0 %collective-permute-start.8 = (bf16[8,128,256]{2,1,0:T(8,128)(2,1)}, bf16[8,128,256]{2,1,0:T(8,128)(2,1)S(1)}, u32[]{:S(2)}, u32[]{:S(2)}) collective-permute-start(bf16[8,128,256]{2,1,0:T(8,128)(2,1)} %collective-permute-done.3.refs_3_), channel_id=1, source_target_pairs={{0,64},{64,128},{128,192},{192,0},{1,65},{65,129},{129,193},{193,1... | collective-permute-start | bytes 1572872 | tf_op jit(solution)/shard_map/ppermute | solution.py:250
  91.8 1.8 %collective-permute-done.13.refs_7_ = bf16[8,128,256]{2,1,0:T(8,128)(2,1)} collective-permute-done((bf16[8,128,256]{2,1,0:T(8,128)(2,1)}, bf16[8,128,256]{2,1,0:T(8,128)(2,1)}, u32[]{:S(2)}, u32[]{:S(2)}) %collective-permute-start.13) | collective-permute-done | bytes 524320 | tf_op jit(solution)/shard_map/ppermute | solution.py:250
  93.6 1.9 %collective-permute-start.9 = (bf16[8,128,256]{2,1,0:T(8,128)(2,1)S(1)}, bf16[8,128,256]{2,1,0:T(8,128)(2,1)S(1)}, u32[]{:S(2)}, u32[]{:S(2)}) collective-permute-start(bf16[8,128,256]{2,1,0:T(8,128)(2,1)S(1)} %collective-permute-done.4.refs_8_), channel_id=1, source_target_pairs={{0,32},{32,0},{1,33},{33,1},{2,34},{34,2},{3,35},{35,3},{4,36},{36... | collective-permute-start | bytes 1572872 | tf_op jit(solution)/shard_map/ppermute | solution.py:250
  95.5 9.2 %collective-permute-done.12.refs_6_ = bf16[8,128,256]{2,1,0:T(8,128)(2,1)S(1)} collective-permute-done((bf16[8,128,256]{2,1,0:T(8,128)(2,1)S(1)}, bf16[8,128,256]{2,1,0:T(8,128)(2,1)S(1)}, u32[]{:S(2)}, u32[]{:S(2)}) %collective-permute-start.12) | collective-permute-done | bytes 524320 | tf_op jit(solution)/shard_map/ppermute | solution.py:250
  104.7 0.0 collective-permute-done.11.refs_5_
  104.7 0.0 collective-permute-done.10.refs_4_
  104.7 5.7 %correlate.3 = (bf16[16,128,1024]{2,1,0:T(8,128)(2,1)S(1)}, bf16[16,128,1024]{2,1,0:T(8,128)(2,1)S(1)}, bf16[16,128,1024]{2,1,0:T(8,128)(2,1)}, bf16[16,128,1024]{2,1,0:T(8,128)(2,1)}) custom-call(s32[8]{0:T(128)S(1)} %stack.35.refs_0_, bf16[8,128,256]{2,1,0:T(8,128)(2,1)S(1)} %get-tuple-element.16.refs_1_, ...), custom_call_target="tpu_custom_call", output_to_operand_aliasing={{0}: (9, {}), {1}: (10, {})} | custom-call | flops 1000 | bytes 1000 | tf_op jit(solution)/shard_map/correlate/pallas_call | solution.py:198
  110.4 1.5 %collective-permute-done.8.refs_2_ = bf16[8,128,256]{2,1,0:T(8,128)(2,1)S(1)} collective-permute-done((bf16[8,128,256]{2,1,0:T(8,128)(2,1)}, bf16[8,128,256]{2,1,0:T(8,128)(2,1)S(1)}, u32[]{:S(2)}, u32[]{:S(2)}) %collective-permute-start.8) | collective-permute-done | bytes 524320 | tf_op jit(solution)/shard_map/ppermute | solution.py:250
  111.9 2.7 %collective-permute-done.9.refs_4_ = bf16[8,128,256]{2,1,0:T(8,128)(2,1)S(1)} collective-permute-done((bf16[8,128,256]{2,1,0:T(8,128)(2,1)S(1)}, bf16[8,128,256]{2,1,0:T(8,128)(2,1)S(1)}, u32[]{:S(2)}, u32[]{:S(2)}) %collective-permute-start.9) | collective-permute-done | bytes 524320 | tf_op jit(solution)/shard_map/ppermute | solution.py:250
  114.6 2.3 %correlate_last.1 = (bf16[16,128,1024]{2,1,0:T(8,128)(2,1)}, bf16[16,128,1024]{2,1,0:T(8,128)(2,1)}) custom-call(s32[8]{0:T(128)S(1)} %stack.35.refs_0_, bf16[8,128,256]{2,1,0:T(8,128)(2,1)S(1)} %get-tuple-element.16.refs_1_, bf16[8,128,256]{2,1,0:T(8,128)(2,1)S(1)} %collective-permute-done.8.refs_2_, ...), custom_call_target="tpu_custom_call", output_to_operand_aliasing={{0}: (5, {}), {1}: (6, {})} | custom-call | flops 1000 | bytes 1000 | tf_op jit(solution)/shard_map/correlate_last/pallas_call | solution.py:235
Async XLA Ops:
  48.2 14.8 %collective-permute-start = (bf16[8,128,256]{2,1,0:T(8,128)(2,1)S(1)}, bf16[8,128,256]{2,1,0:T(8,128)(2,1)S(1)}, u32[]{:S(2)}, u32[]{:S(2)}) collective-permute-start(bf16[8,128,256]{2,1,0:T(8,128)(2,1)S(1)} %get-tuple-element.16.refs_1_), channel_id=1, source_target_pairs={{0,32},{32,0},{1,33},{33,1},{2,34},{34,2},{3,35},{35,3},{4,36},{36... | collective-permute-start | bytes 1572872 | tf_op jit(solution)/shard_map/ppermute | solution.py:250
  48.3 15.1 %collective-permute-start.1 = (bf16[8,128,256]{2,1,0:T(8,128)(2,1)S(1)}, bf16[8,128,256]{2,1,0:T(8,128)(2,1)}, u32[]{:S(2)}, u32[]{:S(2)}) collective-permute-start(bf16[8,128,256]{2,1,0:T(8,128)(2,1)S(1)} %get-tuple-element.17.refs_2_.refs_3_), channel_id=1, source_target_pairs={{0,192},{64,0},{128,64},{192,128},{1,193},{65,1},{129,65},{193,129... | collective-permute-start | bytes 1572872 | tf_op jit(solution)/shard_map/ppermute | solution.py:250
  51.2 16.0 %collective-permute-start.2 = (bf16[8,128,256]{2,1,0:T(8,128)(2,1)S(1)}, bf16[8,128,256]{2,1,0:T(8,128)(2,1)S(1)}, u32[]{:S(2)}, u32[]{:S(2)}) collective-permute-start(bf16[8,128,256]{2,1,0:T(8,128)(2,1)S(1)} %get-tuple-element.17.refs_2_.refs_3_), channel_id=1, source_target_pairs={{0,64},{64,128},{128,192},{192,0},{1,65},{65,129},{129,193},{193,1... | collective-permute-start | bytes 1572872 | tf_op jit(solution)/shard_map/ppermute | solution.py:250
  51.2 27.2 %collective-permute-start.5 = (bf16[8,128,256]{2,1,0:T(8,128)(2,1)S(1)}, bf16[8,128,256]{2,1,0:T(8,128)(2,1)S(1)}, u32[]{:S(2)}, u32[]{:S(2)}) collective-permute-start(bf16[8,128,256]{2,1,0:T(8,128)(2,1)S(1)} %get-tuple-element.16.refs_1_), channel_id=1, source_target_pairs={{0,64},{64,128},{128,192},{192,0},{1,65},{65,129},{129,193},{193,1... | collective-permute-start | bytes 1572872 | tf_op jit(solution)/shard_map/ppermute | solution.py:250
  52.0 28.3 %collective-permute-start.6 = (bf16[8,128,256]{2,1,0:T(8,128)(2,1)S(1)}, bf16[8,128,256]{2,1,0:T(8,128)(2,1)}, u32[]{:S(2)}, u32[]{:S(2)}) collective-permute-start(bf16[8,128,256]{2,1,0:T(8,128)(2,1)S(1)} %get-tuple-element.16.refs_1_), channel_id=1, source_target_pairs={{0,192},{64,0},{128,64},{192,128},{1,193},{65,1},{129,65},{193,129... | collective-permute-start | bytes 1572872 | tf_op jit(solution)/shard_map/ppermute | solution.py:250
  63.0 17.6 %collective-permute-start.7 = (bf16[8,128,256]{2,1,0:T(8,128)(2,1)S(1)}, bf16[8,128,256]{2,1,0:T(8,128)(2,1)}, u32[]{:S(2)}, u32[]{:S(2)}) collective-permute-start(bf16[8,128,256]{2,1,0:T(8,128)(2,1)S(1)} %get-tuple-element.17.refs_2_.refs_3_), channel_id=1, source_target_pairs={{0,32},{32,0},{1,33},{33,1},{2,34},{34,2},{3,35},{35,3},{4,36},{36... | collective-permute-start | bytes 1572872 | tf_op jit(solution)/shard_map/ppermute | solution.py:250
  67.2 18.8 %collective-permute-start.4 = (bf16[8,128,256]{2,1,0:T(8,128)(2,1)}, bf16[8,128,256]{2,1,0:T(8,128)(2,1)S(1)}, u32[]{:S(2)}, u32[]{:S(2)}) collective-permute-start(bf16[8,128,256]{2,1,0:T(8,128)(2,1)} %collective-permute-done.1.refs_8_), channel_id=1, source_target_pairs={{0,192},{64,0},{128,64},{192,128},{1,193},{65,1},{129,65},{193,129... | collective-permute-start | bytes 1572872 | tf_op jit(solution)/shard_map/ppermute | solution.py:250
  67.2 22.5 %collective-permute-start.3 = (bf16[8,128,256]{2,1,0:T(8,128)(2,1)S(1)}, bf16[8,128,256]{2,1,0:T(8,128)(2,1)}, u32[]{:S(2)}, u32[]{:S(2)}) collective-permute-start(bf16[8,128,256]{2,1,0:T(8,128)(2,1)S(1)} %collective-permute-done.refs_3_), channel_id=1, source_target_pairs={{0,64},{64,128},{128,192},{192,0},{1,65},{65,129},{129,193},{193,1... | collective-permute-start | bytes 1572872 | tf_op jit(solution)/shard_map/ppermute | solution.py:250
  78.4 15.2 %collective-permute-start.13 = (bf16[8,128,256]{2,1,0:T(8,128)(2,1)}, bf16[8,128,256]{2,1,0:T(8,128)(2,1)}, u32[]{:S(2)}, u32[]{:S(2)}) collective-permute-start(bf16[8,128,256]{2,1,0:T(8,128)(2,1)} %collective-permute-done.1.refs_8_), channel_id=1, source_target_pairs={{0,32},{32,0},{1,33},{33,1},{2,34},{34,2},{3,35},{35,3},{4,36},{36... | collective-permute-start | bytes 1572872 | tf_op jit(solution)/shard_map/ppermute | solution.py:250
  80.4 24.3 %collective-permute-start.12 = (bf16[8,128,256]{2,1,0:T(8,128)(2,1)S(1)}, bf16[8,128,256]{2,1,0:T(8,128)(2,1)S(1)}, u32[]{:S(2)}, u32[]{:S(2)}) collective-permute-start(bf16[8,128,256]{2,1,0:T(8,128)(2,1)S(1)} %collective-permute-done.2.refs_7_), channel_id=1, source_target_pairs={{0,32},{32,0},{1,33},{33,1},{2,34},{34,2},{3,35},{35,3},{4,36},{36... | collective-permute-start | bytes 1572872 | tf_op jit(solution)/shard_map/ppermute | solution.py:250
  80.6 24.1 %collective-permute-start.11 = (bf16[8,128,256]{2,1,0:T(8,128)(2,1)S(1)}, bf16[8,128,256]{2,1,0:T(8,128)(2,1)S(1)}, u32[]{:S(2)}, u32[]{:S(2)}) collective-permute-start(bf16[8,128,256]{2,1,0:T(8,128)(2,1)S(1)} %collective-permute-done.5.refs_4_), channel_id=1, source_target_pairs={{0,64},{64,128},{128,192},{192,0},{1,65},{65,129},{129,193},{193,1... | collective-permute-start | bytes 1572872 | tf_op jit(solution)/shard_map/ppermute | solution.py:250
  89.7 14.9 %collective-permute-start.10 = (bf16[8,128,256]{2,1,0:T(8,128)(2,1)S(1)}, bf16[8,128,256]{2,1,0:T(8,128)(2,1)S(1)}, u32[]{:S(2)}, u32[]{:S(2)}) collective-permute-start(bf16[8,128,256]{2,1,0:T(8,128)(2,1)S(1)} %collective-permute-done.refs_3_), channel_id=1, source_target_pairs={{0,192},{64,0},{128,64},{192,128},{1,193},{65,1},{129,65},{193,129... | collective-permute-start | bytes 1572872 | tf_op jit(solution)/shard_map/ppermute | solution.py:250
  89.7 22.1 %collective-permute-start.8 = (bf16[8,128,256]{2,1,0:T(8,128)(2,1)}, bf16[8,128,256]{2,1,0:T(8,128)(2,1)S(1)}, u32[]{:S(2)}, u32[]{:S(2)}) collective-permute-start(bf16[8,128,256]{2,1,0:T(8,128)(2,1)} %collective-permute-done.3.refs_3_), channel_id=1, source_target_pairs={{0,64},{64,128},{128,192},{192,0},{1,65},{65,129},{129,193},{193,1... | collective-permute-start | bytes 1572872 | tf_op jit(solution)/shard_map/ppermute | solution.py:250
  93.6 21.0 %collective-permute-start.9 = (bf16[8,128,256]{2,1,0:T(8,128)(2,1)S(1)}, bf16[8,128,256]{2,1,0:T(8,128)(2,1)S(1)}, u32[]{:S(2)}, u32[]{:S(2)}) collective-permute-start(bf16[8,128,256]{2,1,0:T(8,128)(2,1)S(1)} %collective-permute-done.4.refs_8_), channel_id=1, source_target_pairs={{0,32},{32,0},{1,33},{33,1},{2,34},{34,2},{3,35},{35,3},{4,36},{36... | collective-permute-start | bytes 1572872 | tf_op jit(solution)/shard_map/ppermute | solution.py:250

commit v5 on v4

--- a/solution.py
+++ b/solution.py
@@ -27,7 +27,8 @@
 FREQ = ("y", "z_hi", "core")
 LIGHT = pl.CostEstimate(flops=1000, bytes_accessed=1000, transcendentals=0)
 
-EARLY = 8
+EARLY = 9
+HALF = 4
 
 
 def table_rows(lo, count):
@@ -209,31 +210,32 @@
     return out[-2:]
 
 
-def last_kernel(parts, place_ref, *refs):
-    blocks = refs[: 2 * parts]
+def last_kernel(plan, count, place_ref, *refs):
+    blocks = refs[:count]
     re_out, im_out, re_ref, im_ref, sem = refs[-5:]
     cols = pl.ds(pl.multiple_of(place_ref[5], SPEC), SPEC)
     copies, at = [], 0
-    for k in range(parts):
-        own_ref, other_ref = blocks[2 * k : 2 * k + 2]
-        for c in range(own_ref.shape[0]):
-            out = products(own_ref[c], other_ref[c])
+    for own, first, other in plan:
+        own_ref, other_ref = blocks[own], blocks[other]
+        size = other_ref.shape[0]
+        for c in range(size):
+            out = products(own_ref[first + c], other_ref[c])
             re_ref[at + c], im_ref[at + c] = out[:SPEC], out[SPEC:]
-        for c in range(at, at + own_ref.shape[0]):
+        for c in range(at, at + size):
             for k2, (src, dst) in enumerate(((re_ref, re_out), (im_ref, im_out))):
                 copies.append(pltpu.make_async_copy(src.at[c], dst.at[c, :, cols], sem.at[k2, c]))
                 copies[-1].start()
-        at += own_ref.shape[0]
+        at += size
     for copy in copies:
         copy.wait()
 
 
-def correlate_last(place, blocks, done):
+def correlate_last(place, plan, blocks, done):
     shape = jax.ShapeDtypeStruct((CH, SPEC, SPEC * GROUPS), BF16)
     vmem, anywhere = pl.BlockSpec(memory_space=pltpu.VMEM), pl.BlockSpec(memory_space=pl.ANY)
     count = len(blocks)
     return pl.pallas_call(
-        lambda *refs: last_kernel(count // 2, *refs),
+        lambda *refs: last_kernel(plan, count, *refs),
         out_shape=[shape] * 2,
         in_specs=[pl.BlockSpec(memory_space=pltpu.SMEM)] + [vmem] * count + [anywhere] * 2,
         out_specs=[anywhere] * 2,
@@ -277,8 +279,7 @@
     a_m, a_p, zb = up(a), down(a), across(b)
     (za, b_p, b_m), _ = after((za, b_p, b_m), (za, b_p, b_m))
     za_m, b_o, zb_m = up(za), down(b_p), across(b_m)
-    za_p = down(after(za, b_o)[0])
-    a_o, zb_p = up(a_m), across(b_p)
+    a_o, za_p, zb_p = up(a_m), down(za), across(b_p)
     out = correlate(
         place,
         (
@@ -288,7 +289,8 @@
         (a, b, za, a_m, a_p, zb, b_m, b_p),
     )
     (za_m, b_o), out = after((za_m, b_o), out)
-    za_o, zb_o = up(za_m), across(b_o)
+    za_lo, zb_o = up(za_m[:HALF]), across(b_o)
+    za_hi = down(za_p[HALF:])
     out = correlate(
         place,
         (
@@ -298,7 +300,8 @@
         (a, b, za_m, za_p, a_o, zb_m, zb_p, b_o),
         out,
     )
-    return tuple(correlate_last(place, (a, za_o, b, zb_o), out))
+    plan = ((0, 0, 2), (0, HALF, 3), (1, 0, 4))
+    return tuple(correlate_last(place, plan, (a, b, za_lo, za_hi, zb_o), out))
 
 
 def solution(mesh):

time: 117 us -> 116 us (level)
  waiting for transfers between devices: 42.5 us -> 25.1 us
  starting transfers between devices: 14.3 us -> 24.7 us
  local copies, waits for them, and re-layouts: 0.08 us -> 5.58 us
    ppermute x14 -> x15, waiting for transfers between devices: 42.5 us -> 25.1 us  [shift(): lax.ppermute(value, axis, [(i, (i + by) % size) for i in range(size)])]
    ppermute x14 -> x15, starting transfers between devices: 14.3 us -> 24.7 us  [shift(): lax.ppermute(value, axis, [(i, (i + by) % size) for i in range(size)])]
    unnamed x0 -> x12, local copies, waits for them, and re-layouts: none -> 5.46 us
  transfers between devices with their start and end apart: 14 -> 15, of which waited for: 10 -> 6; matrix products, arithmetic and copies ran while one was open for 0% -> 0% of each run, Pallas kernels for 8% -> 8%
where the time goes in v5:
time: 116 us
  blocking collectives  39.4 us (34%)
  waiting for transfers between devices  25.1 us (22%)
  starting transfers between devices  24.7 us (21%)
  Pallas kernels  20.3 us (18%)
  local copies, waits for them, and re-layouts  5.58 us (5%)
    all_to_all x1, blocking collectives, on_device(): lax.all_to_all(pieces, FREQ, split_axis=0, concat_axis=0, tiled=True)  39.4 us
    ppermute x15, waiting for transfers between devices, shift(): lax.ppermute(value, axis, [(i, (i + by) % size) for i in range(size)])  25.1 us
    ppermute x15, starting transfers between devices, shift(): lax.ppermute(value, axis, [(i, (i + by) % size) for i in range(size)])  24.7 us
    pallas_call x2, Pallas kernels, correlate(): pl.pallas_call(lambda *refs: correlate_kernel(plan, count, *refs), out_sh...  9.84 us
    pallas_call x1, Pallas kernels, filter_and_transform(): pl.pallas_call(lambda *refs: filter_kernel(rows, *refs), out_shape=jax.Sh...  7.64 us
    unnamed x12, local copies, waits for them, and re-layouts  5.46 us
  transfers between devices with their start and end apart: 15, of which 6 were waited for; matrix products, arithmetic and copies ran while one was open for 0% of the time, Pallas kernels for 8%

profile of v5, /device:TPU:8, one launch (start us, length us, event | category | flops | bytes accessed | tf_op | source)
XLA Modules:
  0.0 115.9 jit_solution(7918643546560555876)
XLA Ops:
  0.6 7.6 %filter_and_transform.1 = bf16[32,4,32,128]{3,2,1,0:T(8,128)(2,1)} custom-call(s32[131,64,128]{2,1,0:T(8,128)} %bitcast.15, f32[4,2048]{1,0:T(4,128)} %refs_1_.1, bf16[1024,2048]{1,0:T(8,128)(2,1)} %constant.77.clone.refs_2_), custom_call_target="tpu_custom_call" | custom-call | flops 1000 | bytes 1000 | tf_op jit(solution)/shard_map/filter_and_transform/pallas_call | solution.py:106
  8.3 39.4 %all_to_all.5 = bf16[32,4,32,128]{3,2,1,0:T(8,128)(2,1)S(1)} all-to-all(bf16[32,4,32,128]{3,2,1,0:T(8,128)(2,1)} %filter_and_transform.1), channel_id=1, replica_groups=mesh['x'=4,'z_lo'=2,'y'=4,'z_hi'=4,'core'=2] {'y','z_hi','core'}, dimensions={0} | all-to-all | bytes 2097152 | tf_op jit(solution)/shard_map/all_to_all | solution.py:276
  47.7 0.6 assemble.1
  48.2 0.1 collective-permute-start
  48.3 2.8 %collective-permute-start.1 = (bf16[7,128,256]{2,1,0:T(8,128)(2,1)S(1)}, bf16[7,128,256]{2,1,0:T(8,128)(2,1)}, u32[]{:S(2)}, u32[]{:S(2)}) collective-permute-start(bf16[7,128,256]{2,1,0:T(8,128)(2,1)S(1)} %get-tuple-element.16.refs_2_), channel_id=1, source_target_pairs={{0,192},{64,0},{128,64},{192,128},{1,193},{65,1},{129,65},{193,129... | collective-permute-start | bytes 1376264 | tf_op jit(solution)/shard_map/ppermute | solution.py:252
  51.2 0.0 collective-permute-start.2
  51.2 1.9 %collective-permute-start.7 = (bf16[7,128,256]{2,1,0:T(8,128)(2,1)S(1)}, bf16[7,128,256]{2,1,0:T(8,128)(2,1)S(1)}, u32[]{:S(2)}, u32[]{:S(2)}) collective-permute-start(bf16[7,128,256]{2,1,0:T(8,128)(2,1)S(1)} %get-tuple-element.16.refs_2_), channel_id=1, source_target_pairs={{0,32},{32,0},{1,33},{33,1},{2,34},{34,2},{3,35},{35,3},{4,36},{36... | collective-permute-start | bytes 1376264 | tf_op jit(solution)/shard_map/ppermute | solution.py:252
  53.1 0.9 collective-permute-start.5
  54.0 8.1 %collective-permute-done.1.refs_8_ = bf16[7,128,256]{2,1,0:T(8,128)(2,1)} collective-permute-done((bf16[7,128,256]{2,1,0:T(8,128)(2,1)S(1)}, bf16[7,128,256]{2,1,0:T(8,128)(2,1)}, u32[]{:S(2)}, u32[]{:S(2)}) %collective-permute-start.1) | collective-permute-done | bytes 458784 | tf_op jit(solution)/shard_map/ppermute | solution.py:252
  62.0 3.8 %collective-permute-start.6 = (bf16[9,128,256]{2,1,0:T(8,128)(2,1)S(1)}, bf16[9,128,256]{2,1,0:T(8,128)(2,1)S(1)}, u32[]{:S(2)}, u32[]{:S(2)}) collective-permute-start(bf16[9,128,256]{2,1,0:T(8,128)(2,1)S(1)} %get-tuple-element.15.refs_1_), channel_id=1, source_target_pairs={{0,192},{64,0},{128,64},{192,128},{1,193},{65,1},{129,65},{193,129... | collective-permute-start | bytes 1769480 | tf_op jit(solution)/shard_map/ppermute | solution.py:252
  65.8 0.0 collective-permute-done.2.refs_7_
  65.8 0.0 copy-start.2
  65.8 0.8 copy-done.2
  66.6 0.0 collective-permute-done.refs_3_
  66.6 0.0 collective-permute-start.3
  66.6 3.2 %collective-permute-start.4 = (bf16[7,128,256]{2,1,0:T(8,128)(2,1)}, bf16[7,128,256]{2,1,0:T(8,128)(2,1)}, u32[]{:S(2)}, u32[]{:S(2)}) collective-permute-start(bf16[7,128,256]{2,1,0:T(8,128)(2,1)} %collective-permute-done.1.refs_8_), channel_id=1, source_target_pairs={{0,192},{64,0},{128,64},{192,128},{1,193},{65,1},{129,65},{193,129... | collective-permute-start | bytes 1376264 | tf_op jit(solution)/shard_map/ppermute | solution.py:252
  69.8 4.5 %collective-permute-done.7.refs_6_ = bf16[7,128,256]{2,1,0:T(8,128)(2,1)S(1)} collective-permute-done((bf16[7,128,256]{2,1,0:T(8,128)(2,1)S(1)}, bf16[7,128,256]{2,1,0:T(8,128)(2,1)S(1)}, u32[]{:S(2)}, u32[]{:S(2)}) %collective-permute-start.7) | collective-permute-done | bytes 458784 | tf_op jit(solution)/shard_map/ppermute | solution.py:252
  74.3 0.0 copy-start.4
  74.3 0.8 copy-done.4
  75.1 2.7 %collective-permute-start.9 = (bf16[9,128,256]{2,1,0:T(8,128)(2,1)S(1)}, bf16[9,128,256]{2,1,0:T(8,128)(2,1)S(1)}, u32[]{:S(2)}, u32[]{:S(2)}) collective-permute-start(bf16[9,128,256]{2,1,0:T(8,128)(2,1)S(1)} %collective-permute-done.refs_3_), channel_id=1, source_target_pairs={{0,192},{64,0},{128,64},{192,128},{1,193},{65,1},{129,65},{193,129... | collective-permute-start | bytes 1769480 | tf_op jit(solution)/shard_map/ppermute | solution.py:252
  77.8 0.6 collective-permute-done.5.refs_4_
  78.4 1.9 %collective-permute-start.14 = (bf16[7,128,256]{2,1,0:T(8,128)(2,1)}, bf16[7,128,256]{2,1,0:T(8,128)(2,1)}, u32[]{:S(2)}, u32[]{:S(2)}) collective-permute-start(bf16[7,128,256]{2,1,0:T(8,128)(2,1)} %collective-permute-done.1.refs_8_), channel_id=1, source_target_pairs={{0,32},{32,0},{1,33},{33,1},{2,34},{34,2},{3,35},{35,3},{4,36},{36... | collective-permute-start | bytes 1376264 | tf_op jit(solution)/shard_map/ppermute | solution.py:252
  80.3 0.0 collective-permute-done.6.refs_5_
  80.3 0.8 copy-done
  81.1 0.0 collective-permute-start.12
  81.1 0.1 stack.35.refs_0_
  81.2 0.0 copy-start.1
  81.2 1.1 copy-done.1
  82.3 0.0 copy-start.3
  82.3 1.0 copy-done.3
  83.3 0.0 copy-start.5
  83.3 1.0 copy-done.5
  84.3 3.7 %correlate.2 = (bf16[16,128,1024]{2,1,0:T(8,128)(2,1)S(1)}, bf16[16,128,1024]{2,1,0:T(8,128)(2,1)S(1)}) custom-call(s32[8]{0:T(128)S(1)} %stack.35.refs_0_, bf16[9,128,256]{2,1,0:T(8,128)(2,1)S(1)} %get-tuple-element.15.refs_1_, bf16[7,128,256]{2,1,0:T(8,128)(2,1)S(1)} %get-tuple-element.16.refs_2_, bf16[9,128,256]{2,1,0:T(8,128)(2,1)S(1)} %collective-permute-done.refs_3_, ...), custom_call_target="tpu_custom_call" | custom-call | flops 1000 | bytes 1000 | tf_op jit(solution)/shard_map/correlate/pallas_call | solution.py:199
  88.0 1.4 %collective-permute-done.4.refs_8_ = bf16[7,128,256]{2,1,0:T(8,128)(2,1)} collective-permute-done((bf16[7,128,256]{2,1,0:T(8,128)(2,1)}, bf16[7,128,256]{2,1,0:T(8,128)(2,1)}, u32[]{:S(2)}, u32[]{:S(2)}) %collective-permute-start.4) | collective-permute-done | bytes 458784 | tf_op jit(solution)/shard_map/ppermute | solution.py:252
  89.4 1.6 %collective-permute-start.13 = (bf16[7,128,256]{2,1,0:T(8,128)(2,1)S(1)}, bf16[7,128,256]{2,1,0:T(8,128)(2,1)S(1)}, u32[]{:S(2)}, u32[]{:S(2)}) collective-permute-start(bf16[7,128,256]{2,1,0:T(8,128)(2,1)S(1)} %copy-done.3), channel_id=1, source_target_pairs={{0,32},{32,0},{1,33},{33,1},{2,34},{34,2},{3,35},{35,3},{4,36},{36... | collective-permute-start | bytes 1376264 | tf_op jit(solution)/shard_map/ppermute | solution.py:252
  91.1 0.0 collective-permute-done.3.refs_3_
  91.1 1.8 %collective-permute-start.11 = (bf16[7,128,256]{2,1,0:T(8,128)(2,1)}, bf16[7,128,256]{2,1,0:T(8,128)(2,1)S(1)}, u32[]{:S(2)}, u32[]{:S(2)}) collective-permute-start(bf16[7,128,256]{2,1,0:T(8,128)(2,1)} %collective-permute-done.4.refs_8_), channel_id=1, source_target_pairs={{0,32},{32,0},{1,33},{33,1},{2,34},{34,2},{3,35},{35,3},{4,36},{36... | collective-permute-start | bytes 1376264 | tf_op jit(solution)/shard_map/ppermute | solution.py:252
  92.9 8.2 %collective-permute-done.9.refs_4_ = bf16[9,128,256]{2,1,0:T(8,128)(2,1)S(1)} collective-permute-done((bf16[9,128,256]{2,1,0:T(8,128)(2,1)S(1)}, bf16[9,128,256]{2,1,0:T(8,128)(2,1)S(1)}, u32[]{:S(2)}, u32[]{:S(2)}) %collective-permute-start.9) | collective-permute-done | bytes 589856 | tf_op jit(solution)/shard_map/ppermute | solution.py:252
  101.2 3.8 %collective-permute-start.10 = (bf16[5,128,256]{2,1,0:T(8,128)(2,1)S(1)}, bf16[5,128,256]{2,1,0:T(8,128)(2,1)S(1)}, u32[]{:S(2)}, u32[]{:S(2)}) collective-permute-start(bf16[5,128,256]{2,1,0:T(8,128)(2,1)S(1)} %slice.8), channel_id=1, source_target_pairs={{0,192},{64,0},{128,64},{192,128},{1,193},{65,1},{129,65},{193,129... | collective-permute-start | bytes 983048 | tf_op jit(solution)/shard_map/ppermute | solution.py:252
  105.0 0.0 collective-permute-done.14.refs_7_
  105.0 0.1 collective-permute-start.8
  105.1 0.0 collective-permute-done.13.refs_6_
  105.1 0.0 collective-permute-done.12.refs_5_
  105.1 6.1 %correlate.3 = (bf16[16,128,1024]{2,1,0:T(8,128)(2,1)S(1)}, bf16[16,128,1024]{2,1,0:T(8,128)(2,1)S(1)}, bf16[16,128,1024]{2,1,0:T(8,128)(2,1)}, bf16[16,128,1024]{2,1,0:T(8,128)(2,1)}) custom-call(s32[8]{0:T(128)S(1)} %stack.35.refs_0_, bf16[9,128,256]{2,1,0:T(8,128)(2,1)S(1)} %get-tuple-element.15.refs_1_, ...), custom_call_target="tpu_custom_call", output_to_operand_aliasing={{0}: (9, {}), {1}: (10, {})} | custom-call | flops 1000 | bytes 1000 | tf_op jit(solution)/shard_map/correlate/pallas_call | solution.py:199
  111.2 2.3 %collective-permute-done.8.refs_3_ = bf16[4,128,256]{2,1,0:T(8,128)(2,1)S(1)} collective-permute-done((bf16[4,128,256]{2,1,0:T(8,128)(2,1)S(1)}, bf16[4,128,256]{2,1,0:T(8,128)(2,1)S(1)}, u32[]{:S(2)}, u32[]{:S(2)}) %collective-permute-start.8) | collective-permute-done | bytes 262176 | tf_op jit(solution)/shard_map/ppermute | solution.py:252
  113.5 0.0 collective-permute-done.10.refs_4_
  113.5 0.0 collective-permute-done.11.refs_5_
  113.5 2.3 %correlate_last.1 = (bf16[16,128,1024]{2,1,0:T(8,128)(2,1)}, bf16[16,128,1024]{2,1,0:T(8,128)(2,1)}) custom-call(s32[8]{0:T(128)S(1)} %stack.35.refs_0_, bf16[9,128,256]{2,1,0:T(8,128)(2,1)S(1)} %get-tuple-element.15.refs_1_, bf16[7,128,256]{2,1,0:T(8,128)(2,1)S(1)} %get-tuple-element.16.refs_2_, ...), custom_call_target="tpu_custom_call", output_to_operand_aliasing={{0}: (6, {}), {1}: (7, {})} | custom-call | flops 1000 | bytes 1000 | tf_op jit(solution)/shard_map/correlate_last/pallas_call | solution.py:237
  (3 shorter events, 0.0 us)
Async XLA Ops:
  48.2 18.4 %collective-permute-start = (bf16[9,128,256]{2,1,0:T(8,128)(2,1)S(1)}, bf16[9,128,256]{2,1,0:T(8,128)(2,1)S(1)}, u32[]{:S(2)}, u32[]{:S(2)}) collective-permute-start(bf16[9,128,256]{2,1,0:T(8,128)(2,1)S(1)} %get-tuple-element.15.refs_1_), channel_id=1, source_target_pairs={{0,32},{32,0},{1,33},{33,1},{2,34},{34,2},{3,35},{35,3},{4,36},{36... | collective-permute-start | bytes 1769480 | tf_op jit(solution)/shard_map/ppermute | solution.py:252
  48.3 13.7 %collective-permute-start.1 = (bf16[7,128,256]{2,1,0:T(8,128)(2,1)S(1)}, bf16[7,128,256]{2,1,0:T(8,128)(2,1)}, u32[]{:S(2)}, u32[]{:S(2)}) collective-permute-start(bf16[7,128,256]{2,1,0:T(8,128)(2,1)S(1)} %get-tuple-element.16.refs_2_), channel_id=1, source_target_pairs={{0,192},{64,0},{128,64},{192,128},{1,193},{65,1},{129,65},{193,129... | collective-permute-start | bytes 1376264 | tf_op jit(solution)/shard_map/ppermute | solution.py:252
  51.2 14.7 %collective-permute-start.2 = (bf16[7,128,256]{2,1,0:T(8,128)(2,1)S(1)}, bf16[7,128,256]{2,1,0:T(8,128)(2,1)S(1)}, u32[]{:S(2)}, u32[]{:S(2)}) collective-permute-start(bf16[7,128,256]{2,1,0:T(8,128)(2,1)S(1)} %get-tuple-element.16.refs_2_), channel_id=1, source_target_pairs={{0,64},{64,128},{128,192},{192,0},{1,65},{65,129},{129,193},{193,1... | collective-permute-start | bytes 1376264 | tf_op jit(solution)/shard_map/ppermute | solution.py:252
  51.2 23.1 %collective-permute-start.7 = (bf16[7,128,256]{2,1,0:T(8,128)(2,1)S(1)}, bf16[7,128,256]{2,1,0:T(8,128)(2,1)S(1)}, u32[]{:S(2)}, u32[]{:S(2)}) collective-permute-start(bf16[7,128,256]{2,1,0:T(8,128)(2,1)S(1)} %get-tuple-element.16.refs_2_), channel_id=1, source_target_pairs={{0,32},{32,0},{1,33},{33,1},{2,34},{34,2},{3,35},{35,3},{4,36},{36... | collective-permute-start | bytes 1376264 | tf_op jit(solution)/shard_map/ppermute | solution.py:252
  53.1 25.3 %collective-permute-start.5 = (bf16[9,128,256]{2,1,0:T(8,128)(2,1)S(1)}, bf16[9,128,256]{2,1,0:T(8,128)(2,1)S(1)}, u32[]{:S(2)}, u32[]{:S(2)}) collective-permute-start(bf16[9,128,256]{2,1,0:T(8,128)(2,1)S(1)} %get-tuple-element.15.refs_1_), channel_id=1, source_target_pairs={{0,64},{64,128},{128,192},{192,0},{1,65},{65,129},{129,193},{193,1... | collective-permute-start | bytes 1769480 | tf_op jit(solution)/shard_map/ppermute | solution.py:252
  62.0 18.3 %collective-permute-start.6 = (bf16[9,128,256]{2,1,0:T(8,128)(2,1)S(1)}, bf16[9,128,256]{2,1,0:T(8,128)(2,1)S(1)}, u32[]{:S(2)}, u32[]{:S(2)}) collective-permute-start(bf16[9,128,256]{2,1,0:T(8,128)(2,1)S(1)} %get-tuple-element.15.refs_1_), channel_id=1, source_target_pairs={{0,192},{64,0},{128,64},{192,128},{1,193},{65,1},{129,65},{193,129... | collective-permute-start | bytes 1769480 | tf_op jit(solution)/shard_map/ppermute | solution.py:252
  65.8 0.8 copy-start.2
  66.6 24.5 %collective-permute-start.3 = (bf16[9,128,256]{2,1,0:T(8,128)(2,1)S(1)}, bf16[9,128,256]{2,1,0:T(8,128)(2,1)S(1)}, u32[]{:S(2)}, u32[]{:S(2)}) collective-permute-start(bf16[9,128,256]{2,1,0:T(8,128)(2,1)S(1)} %collective-permute-done.refs_3_), channel_id=1, source_target_pairs={{0,64},{64,128},{128,192},{192,0},{1,65},{65,129},{129,193},{193,1... | collective-permute-start | bytes 1769480 | tf_op jit(solution)/shard_map/ppermute | solution.py:252
  66.6 22.9 %collective-permute-start.4 = (bf16[7,128,256]{2,1,0:T(8,128)(2,1)}, bf16[7,128,256]{2,1,0:T(8,128)(2,1)}, u32[]{:S(2)}, u32[]{:S(2)}) collective-permute-start(bf16[7,128,256]{2,1,0:T(8,128)(2,1)} %collective-permute-done.1.refs_8_), channel_id=1, source_target_pairs={{0,192},{64,0},{128,64},{192,128},{1,193},{65,1},{129,65},{193,129... | collective-permute-start | bytes 1376264 | tf_op jit(solution)/shard_map/ppermute | solution.py:252
  74.3 0.8 copy-start.4
  75.1 26.1 %collective-permute-start.9 = (bf16[9,128,256]{2,1,0:T(8,128)(2,1)S(1)}, bf16[9,128,256]{2,1,0:T(8,128)(2,1)S(1)}, u32[]{:S(2)}, u32[]{:S(2)}) collective-permute-start(bf16[9,128,256]{2,1,0:T(8,128)(2,1)S(1)} %collective-permute-done.refs_3_), channel_id=1, source_target_pairs={{0,192},{64,0},{128,64},{192,128},{1,193},{65,1},{129,65},{193,129... | collective-permute-start | bytes 1769480 | tf_op jit(solution)/shard_map/ppermute | solution.py:252
  78.4 26.6 %collective-permute-start.14 = (bf16[7,128,256]{2,1,0:T(8,128)(2,1)}, bf16[7,128,256]{2,1,0:T(8,128)(2,1)}, u32[]{:S(2)}, u32[]{:S(2)}) collective-permute-start(bf16[7,128,256]{2,1,0:T(8,128)(2,1)} %collective-permute-done.1.refs_8_), channel_id=1, source_target_pairs={{0,32},{32,0},{1,33},{33,1},{2,34},{34,2},{3,35},{35,3},{4,36},{36... | collective-permute-start | bytes 1376264 | tf_op jit(solution)/shard_map/ppermute | solution.py:252
  80.3 0.8 copy-start
  81.1 24.0 %collective-permute-start.12 = (bf16[9,128,256]{2,1,0:T(8,128)(2,1)S(1)}, bf16[9,128,256]{2,1,0:T(8,128)(2,1)}, u32[]{:S(2)}, u32[]{:S(2)}) collective-permute-start(bf16[9,128,256]{2,1,0:T(8,128)(2,1)S(1)} %collective-permute-done.5.refs_4_), channel_id=1, source_target_pairs={{0,64},{64,128},{128,192},{192,0},{1,65},{65,129},{129,193},{193,1... | collective-permute-start | bytes 1769480 | tf_op jit(solution)/shard_map/ppermute | solution.py:252
  81.2 1.1 copy-start.1
  82.3 1.0 copy-start.3
  83.3 1.0 copy-start.5
  89.4 15.6 %collective-permute-start.13 = (bf16[7,128,256]{2,1,0:T(8,128)(2,1)S(1)}, bf16[7,128,256]{2,1,0:T(8,128)(2,1)S(1)}, u32[]{:S(2)}, u32[]{:S(2)}) collective-permute-start(bf16[7,128,256]{2,1,0:T(8,128)(2,1)S(1)} %copy-done.3), channel_id=1, source_target_pairs={{0,32},{32,0},{1,33},{33,1},{2,34},{34,2},{3,35},{35,3},{4,36},{36... | collective-permute-start | bytes 1376264 | tf_op jit(solution)/shard_map/ppermute | solution.py:252
  91.1 22.4 %collective-permute-start.11 = (bf16[7,128,256]{2,1,0:T(8,128)(2,1)}, bf16[7,128,256]{2,1,0:T(8,128)(2,1)S(1)}, u32[]{:S(2)}, u32[]{:S(2)}) collective-permute-start(bf16[7,128,256]{2,1,0:T(8,128)(2,1)} %collective-permute-done.4.refs_8_), channel_id=1, source_target_pairs={{0,32},{32,0},{1,33},{33,1},{2,34},{34,2},{3,35},{35,3},{4,36},{36... | collective-permute-start | bytes 1376264 | tf_op jit(solution)/shard_map/ppermute | solution.py:252
  101.2 12.3 %collective-permute-start.10 = (bf16[5,128,256]{2,1,0:T(8,128)(2,1)S(1)}, bf16[5,128,256]{2,1,0:T(8,128)(2,1)S(1)}, u32[]{:S(2)}, u32[]{:S(2)}) collective-permute-start(bf16[5,128,256]{2,1,0:T(8,128)(2,1)S(1)} %slice.8), channel_id=1, source_target_pairs={{0,192},{64,0},{128,64},{192,128},{1,193},{65,1},{129,65},{193,129... | collective-permute-start | bytes 983048 | tf_op jit(solution)/shard_map/ppermute | solution.py:252
  105.0 8.5 %collective-permute-start.8 = (bf16[4,128,256]{2,1,0:T(8,128)(2,1)S(1)}, bf16[4,128,256]{2,1,0:T(8,128)(2,1)S(1)}, u32[]{:S(2)}, u32[]{:S(2)}) collective-permute-start(bf16[4,128,256]{2,1,0:T(8,128)(2,1)S(1)} %slice.6), channel_id=1, source_target_pairs={{0,64},{64,128},{128,192},{192,0},{1,65},{65,129},{129,193},{193,1... | collective-permute-start | bytes 786440 | tf_op jit(solution)/shard_map/ppermute | solution.py:252

commit v6 on v5

--- a/solution.py
+++ b/solution.py
@@ -28,7 +28,7 @@
 LIGHT = pl.CostEstimate(flops=1000, bytes_accessed=1000, transcendentals=0)
 
 EARLY = 9
-HALF = 4
+HALF = 5
 
 
 def table_rows(lo, count):

time: 116 us -> 115 us (level)
  waiting for transfers between devices: 25.1 us -> 23.7 us
    ppermute x15, waiting for transfers between devices: 25.1 us -> 23.7 us  [shift(): lax.ppermute(value, axis, [(i, (i + by) % size) for i in range(size)])]
  transfers between devices with their start and end apart: 15 -> 15, of which waited for: 6 -> 6; matrix products, arithmetic and copies ran while one was open for 0% -> 0% of each run, Pallas kernels for 8% -> 9%
where the time goes in v6:
time: 115 us; the launch traced here: 114 us
  blocking collectives  39.4 us (34%)
  starting transfers between devices  24.6 us (21%)
  waiting for transfers between devices  23.7 us (21%)
  Pallas kernels  20.3 us (18%)
  local copies, waits for them, and re-layouts  5.58 us (5%)
    all_to_all x1, blocking collectives, on_device(): lax.all_to_all(pieces, FREQ, split_axis=0, concat_axis=0, tiled=True)  39.4 us
    ppermute x15, starting transfers between devices, shift(): lax.ppermute(value, axis, [(i, (i + by) % size) for i in range(size)])  24.6 us
    ppermute x15, waiting for transfers between devices, shift(): lax.ppermute(value, axis, [(i, (i + by) % size) for i in range(size)])  23.7 us
    pallas_call x2, Pallas kernels, correlate(): pl.pallas_call(lambda *refs: correlate_kernel(plan, count, *refs), out_sh...  9.83 us
    pallas_call x1, Pallas kernels, filter_and_transform(): pl.pallas_call(lambda *refs: filter_kernel(rows, *refs), out_shape=jax.Sh...  7.64 us
    unnamed x12, local copies, waits for them, and re-layouts  5.46 us
  transfers between devices with their start and end apart: 15, of which 6 were waited for; matrix products, arithmetic and copies ran while one was open for 0% of the time, Pallas kernels for 9%

profile of v6, /device:TPU:8, one launch (start us, length us, event | category | flops | bytes accessed | tf_op | source)
XLA Modules:
  0.0 114.4 jit_solution(5083192145643067295)
XLA Ops:
  0.6 7.6 %filter_and_transform.1 = bf16[32,4,32,128]{3,2,1,0:T(8,128)(2,1)} custom-call(s32[131,64,128]{2,1,0:T(8,128)} %bitcast.15, f32[4,2048]{1,0:T(4,128)} %refs_1_.1, bf16[1024,2048]{1,0:T(8,128)(2,1)} %constant.77.clone.refs_2_), custom_call_target="tpu_custom_call" | custom-call | flops 1000 | bytes 1000 | tf_op jit(solution)/shard_map/filter_and_transform/pallas_call | solution.py:106
  8.3 39.4 %all_to_all.5 = bf16[32,4,32,128]{3,2,1,0:T(8,128)(2,1)S(1)} all-to-all(bf16[32,4,32,128]{3,2,1,0:T(8,128)(2,1)} %filter_and_transform.1), channel_id=1, replica_groups=mesh['x'=4,'z_lo'=2,'y'=4,'z_hi'=4,'core'=2] {'y','z_hi','core'}, dimensions={0} | all-to-all | bytes 2097152 | tf_op jit(solution)/shard_map/all_to_all | solution.py:276
  47.7 0.6 assemble.1
  48.2 0.1 collective-permute-start
  48.3 2.8 %collective-permute-start.1 = (bf16[7,128,256]{2,1,0:T(8,128)(2,1)S(1)}, bf16[7,128,256]{2,1,0:T(8,128)(2,1)}, u32[]{:S(2)}, u32[]{:S(2)}) collective-permute-start(bf16[7,128,256]{2,1,0:T(8,128)(2,1)S(1)} %get-tuple-element.16.refs_2_), channel_id=1, source_target_pairs={{0,192},{64,0},{128,64},{192,128},{1,193},{65,1},{129,65},{193,129... | collective-permute-start | bytes 1376264 | tf_op jit(solution)/shard_map/ppermute | solution.py:252
  51.2 0.0 collective-permute-start.2
  51.2 1.9 %collective-permute-start.7 = (bf16[7,128,256]{2,1,0:T(8,128)(2,1)S(1)}, bf16[7,128,256]{2,1,0:T(8,128)(2,1)S(1)}, u32[]{:S(2)}, u32[]{:S(2)}) collective-permute-start(bf16[7,128,256]{2,1,0:T(8,128)(2,1)S(1)} %get-tuple-element.16.refs_2_), channel_id=1, source_target_pairs={{0,32},{32,0},{1,33},{33,1},{2,34},{34,2},{3,35},{35,3},{4,36},{36... | collective-permute-start | bytes 1376264 | tf_op jit(solution)/shard_map/ppermute | solution.py:252
  53.1 0.9 collective-permute-start.5
  54.0 8.1 %collective-permute-done.1.refs_8_ = bf16[7,128,256]{2,1,0:T(8,128)(2,1)} collective-permute-done((bf16[7,128,256]{2,1,0:T(8,128)(2,1)S(1)}, bf16[7,128,256]{2,1,0:T(8,128)(2,1)}, u32[]{:S(2)}, u32[]{:S(2)}) %collective-permute-start.1) | collective-permute-done | bytes 458784 | tf_op jit(solution)/shard_map/ppermute | solution.py:252
  62.0 3.8 %collective-permute-start.6 = (bf16[9,128,256]{2,1,0:T(8,128)(2,1)S(1)}, bf16[9,128,256]{2,1,0:T(8,128)(2,1)S(1)}, u32[]{:S(2)}, u32[]{:S(2)}) collective-permute-start(bf16[9,128,256]{2,1,0:T(8,128)(2,1)S(1)} %get-tuple-element.15.refs_1_), channel_id=1, source_target_pairs={{0,192},{64,0},{128,64},{192,128},{1,193},{65,1},{129,65},{193,129... | collective-permute-start | bytes 1769480 | tf_op jit(solution)/shard_map/ppermute | solution.py:252
  65.8 0.0 collective-permute-done.2.refs_7_
  65.8 0.0 copy-start.2
  65.8 0.8 copy-done.2
  66.6 0.0 collective-permute-done.refs_3_
  66.6 0.0 collective-permute-start.3
  66.6 3.2 %collective-permute-start.4 = (bf16[7,128,256]{2,1,0:T(8,128)(2,1)}, bf16[7,128,256]{2,1,0:T(8,128)(2,1)}, u32[]{:S(2)}, u32[]{:S(2)}) collective-permute-start(bf16[7,128,256]{2,1,0:T(8,128)(2,1)} %collective-permute-done.1.refs_8_), channel_id=1, source_target_pairs={{0,192},{64,0},{128,64},{192,128},{1,193},{65,1},{129,65},{193,129... | collective-permute-start | bytes 1376264 | tf_op jit(solution)/shard_map/ppermute | solution.py:252
  69.8 4.5 %collective-permute-done.7.refs_6_ = bf16[7,128,256]{2,1,0:T(8,128)(2,1)S(1)} collective-permute-done((bf16[7,128,256]{2,1,0:T(8,128)(2,1)S(1)}, bf16[7,128,256]{2,1,0:T(8,128)(2,1)S(1)}, u32[]{:S(2)}, u32[]{:S(2)}) %collective-permute-start.7) | collective-permute-done | bytes 458784 | tf_op jit(solution)/shard_map/ppermute | solution.py:252
  74.3 0.0 copy-start.4
  74.3 0.8 copy-done.4
  75.1 2.7 %collective-permute-start.9 = (bf16[9,128,256]{2,1,0:T(8,128)(2,1)S(1)}, bf16[9,128,256]{2,1,0:T(8,128)(2,1)S(1)}, u32[]{:S(2)}, u32[]{:S(2)}) collective-permute-start(bf16[9,128,256]{2,1,0:T(8,128)(2,1)S(1)} %collective-permute-done.refs_3_), channel_id=1, source_target_pairs={{0,192},{64,0},{128,64},{192,128},{1,193},{65,1},{129,65},{193,129... | collective-permute-start | bytes 1769480 | tf_op jit(solution)/shard_map/ppermute | solution.py:252
  77.8 0.6 collective-permute-done.5.refs_4_
  78.4 1.9 %collective-permute-start.14 = (bf16[7,128,256]{2,1,0:T(8,128)(2,1)}, bf16[7,128,256]{2,1,0:T(8,128)(2,1)}, u32[]{:S(2)}, u32[]{:S(2)}) collective-permute-start(bf16[7,128,256]{2,1,0:T(8,128)(2,1)} %collective-permute-done.1.refs_8_), channel_id=1, source_target_pairs={{0,32},{32,0},{1,33},{33,1},{2,34},{34,2},{3,35},{35,3},{4,36},{36... | collective-permute-start | bytes 1376264 | tf_op jit(solution)/shard_map/ppermute | solution.py:252
  80.3 0.0 collective-permute-done.6.refs_5_
  80.3 0.0 copy-start
  80.3 0.8 copy-done
  81.1 0.0 collective-permute-start.12
  81.1 0.1 stack.35.refs_0_
  81.2 0.0 copy-start.1
  81.2 1.1 copy-done.1
  82.3 0.0 copy-start.3
  82.3 1.0 copy-done.3
  83.3 1.0 copy-done.5
  84.3 3.7 %correlate.2 = (bf16[16,128,1024]{2,1,0:T(8,128)(2,1)S(1)}, bf16[16,128,1024]{2,1,0:T(8,128)(2,1)S(1)}) custom-call(s32[8]{0:T(128)S(1)} %stack.35.refs_0_, bf16[9,128,256]{2,1,0:T(8,128)(2,1)S(1)} %get-tuple-element.15.refs_1_, bf16[7,128,256]{2,1,0:T(8,128)(2,1)S(1)} %get-tuple-element.16.refs_2_, bf16[9,128,256]{2,1,0:T(8,128)(2,1)S(1)} %collective-permute-done.refs_3_, ...), custom_call_target="tpu_custom_call" | custom-call | flops 1000 | bytes 1000 | tf_op jit(solution)/shard_map/correlate/pallas_call | solution.py:199
  88.0 1.4 %collective-permute-done.4.refs_8_ = bf16[7,128,256]{2,1,0:T(8,128)(2,1)} collective-permute-done((bf16[7,128,256]{2,1,0:T(8,128)(2,1)}, bf16[7,128,256]{2,1,0:T(8,128)(2,1)}, u32[]{:S(2)}, u32[]{:S(2)}) %collective-permute-start.4) | collective-permute-done | bytes 458784 | tf_op jit(solution)/shard_map/ppermute | solution.py:252
  89.4 1.6 %collective-permute-start.13 = (bf16[7,128,256]{2,1,0:T(8,128)(2,1)S(1)}, bf16[7,128,256]{2,1,0:T(8,128)(2,1)S(1)}, u32[]{:S(2)}, u32[]{:S(2)}) collective-permute-start(bf16[7,128,256]{2,1,0:T(8,128)(2,1)S(1)} %copy-done.3), channel_id=1, source_target_pairs={{0,32},{32,0},{1,33},{33,1},{2,34},{34,2},{3,35},{35,3},{4,36},{36... | collective-permute-start | bytes 1376264 | tf_op jit(solution)/shard_map/ppermute | solution.py:252
  91.1 0.0 collective-permute-done.3.refs_3_
  91.1 1.8 %collective-permute-start.11 = (bf16[7,128,256]{2,1,0:T(8,128)(2,1)}, bf16[7,128,256]{2,1,0:T(8,128)(2,1)S(1)}, u32[]{:S(2)}, u32[]{:S(2)}) collective-permute-start(bf16[7,128,256]{2,1,0:T(8,128)(2,1)} %collective-permute-done.4.refs_8_), channel_id=1, source_target_pairs={{0,32},{32,0},{1,33},{33,1},{2,34},{34,2},{3,35},{35,3},{4,36},{36... | collective-permute-start | bytes 1376264 | tf_op jit(solution)/shard_map/ppermute | solution.py:252
  92.9 8.2 %collective-permute-done.9.refs_4_ = bf16[9,128,256]{2,1,0:T(8,128)(2,1)S(1)} collective-permute-done((bf16[9,128,256]{2,1,0:T(8,128)(2,1)S(1)}, bf16[9,128,256]{2,1,0:T(8,128)(2,1)S(1)}, u32[]{:S(2)}, u32[]{:S(2)}) %collective-permute-start.9) | collective-permute-done | bytes 589856 | tf_op jit(solution)/shard_map/ppermute | solution.py:252
  101.2 0.1 collective-permute-start.8
  101.2 0.0 collective-permute-done.14.refs_7_
  101.2 3.7 %collective-permute-start.10 = (bf16[4,128,256]{2,1,0:T(8,128)(2,1)S(1)}, bf16[4,128,256]{2,1,0:T(8,128)(2,1)S(1)}, u32[]{:S(2)}, u32[]{:S(2)}) collective-permute-start(bf16[4,128,256]{2,1,0:T(8,128)(2,1)S(1)} %slice.8), channel_id=1, source_target_pairs={{0,192},{64,0},{128,64},{192,128},{1,193},{65,1},{129,65},{193,129... | collective-permute-start | bytes 786440 | tf_op jit(solution)/shard_map/ppermute | solution.py:252
  105.0 0.0 collective-permute-done.13.refs_6_
  105.0 0.0 collective-permute-done.12.refs_5_
  105.0 6.1 %correlate.3 = (bf16[16,128,1024]{2,1,0:T(8,128)(2,1)S(1)}, bf16[16,128,1024]{2,1,0:T(8,128)(2,1)S(1)}, bf16[16,128,1024]{2,1,0:T(8,128)(2,1)}, bf16[16,128,1024]{2,1,0:T(8,128)(2,1)}) custom-call(s32[8]{0:T(128)S(1)} %stack.35.refs_0_, bf16[9,128,256]{2,1,0:T(8,128)(2,1)S(1)} %get-tuple-element.15.refs_1_, ...), custom_call_target="tpu_custom_call", output_to_operand_aliasing={{0}: (9, {}), {1}: (10, {})} | custom-call | flops 1000 | bytes 1000 | tf_op jit(solution)/shard_map/correlate/pallas_call | solution.py:199
  111.1 0.0 collective-permute-done.10.refs_4_
  111.1 0.9 collective-permute-done.8.refs_3_
  112.0 0.0 collective-permute-done.11.refs_5_
  112.0 2.3 %correlate_last.1 = (bf16[16,128,1024]{2,1,0:T(8,128)(2,1)}, bf16[16,128,1024]{2,1,0:T(8,128)(2,1)}) custom-call(s32[8]{0:T(128)S(1)} %stack.35.refs_0_, bf16[9,128,256]{2,1,0:T(8,128)(2,1)S(1)} %get-tuple-element.15.refs_1_, bf16[7,128,256]{2,1,0:T(8,128)(2,1)S(1)} %get-tuple-element.16.refs_2_, ...), custom_call_target="tpu_custom_call", output_to_operand_aliasing={{0}: (6, {}), {1}: (7, {})} | custom-call | flops 1000 | bytes 1000 | tf_op jit(solution)/shard_map/correlate_last/pallas_call | solution.py:237
  (3 shorter events, 0.0 us)
Async XLA Ops:
  48.2 18.4 %collective-permute-start = (bf16[9,128,256]{2,1,0:T(8,128)(2,1)S(1)}, bf16[9,128,256]{2,1,0:T(8,128)(2,1)S(1)}, u32[]{:S(2)}, u32[]{:S(2)}) collective-permute-start(bf16[9,128,256]{2,1,0:T(8,128)(2,1)S(1)} %get-tuple-element.15.refs_1_), channel_id=1, source_target_pairs={{0,32},{32,0},{1,33},{33,1},{2,34},{34,2},{3,35},{35,3},{4,36},{36... | collective-permute-start | bytes 1769480 | tf_op jit(solution)/shard_map/ppermute | solution.py:252
  48.3 13.7 %collective-permute-start.1 = (bf16[7,128,256]{2,1,0:T(8,128)(2,1)S(1)}, bf16[7,128,256]{2,1,0:T(8,128)(2,1)}, u32[]{:S(2)}, u32[]{:S(2)}) collective-permute-start(bf16[7,128,256]{2,1,0:T(8,128)(2,1)S(1)} %get-tuple-element.16.refs_2_), channel_id=1, source_target_pairs={{0,192},{64,0},{128,64},{192,128},{1,193},{65,1},{129,65},{193,129... | collective-permute-start | bytes 1376264 | tf_op jit(solution)/shard_map/ppermute | solution.py:252
  51.2 14.7 %collective-permute-start.2 = (bf16[7,128,256]{2,1,0:T(8,128)(2,1)S(1)}, bf16[7,128,256]{2,1,0:T(8,128)(2,1)S(1)}, u32[]{:S(2)}, u32[]{:S(2)}) collective-permute-start(bf16[7,128,256]{2,1,0:T(8,128)(2,1)S(1)} %get-tuple-element.16.refs_2_), channel_id=1, source_target_pairs={{0,64},{64,128},{128,192},{192,0},{1,65},{65,129},{129,193},{193,1... | collective-permute-start | bytes 1376264 | tf_op jit(solution)/shard_map/ppermute | solution.py:252
  51.2 23.1 %collective-permute-start.7 = (bf16[7,128,256]{2,1,0:T(8,128)(2,1)S(1)}, bf16[7,128,256]{2,1,0:T(8,128)(2,1)S(1)}, u32[]{:S(2)}, u32[]{:S(2)}) collective-permute-start(bf16[7,128,256]{2,1,0:T(8,128)(2,1)S(1)} %get-tuple-element.16.refs_2_), channel_id=1, source_target_pairs={{0,32},{32,0},{1,33},{33,1},{2,34},{34,2},{3,35},{35,3},{4,36},{36... | collective-permute-start | bytes 1376264 | tf_op jit(solution)/shard_map/ppermute | solution.py:252
  53.1 25.3 %collective-permute-start.5 = (bf16[9,128,256]{2,1,0:T(8,128)(2,1)S(1)}, bf16[9,128,256]{2,1,0:T(8,128)(2,1)S(1)}, u32[]{:S(2)}, u32[]{:S(2)}) collective-permute-start(bf16[9,128,256]{2,1,0:T(8,128)(2,1)S(1)} %get-tuple-element.15.refs_1_), channel_id=1, source_target_pairs={{0,64},{64,128},{128,192},{192,0},{1,65},{65,129},{129,193},{193,1... | collective-permute-start | bytes 1769480 | tf_op jit(solution)/shard_map/ppermute | solution.py:252
  62.0 18.3 %collective-permute-start.6 = (bf16[9,128,256]{2,1,0:T(8,128)(2,1)S(1)}, bf16[9,128,256]{2,1,0:T(8,128)(2,1)S(1)}, u32[]{:S(2)}, u32[]{:S(2)}) collective-permute-start(bf16[9,128,256]{2,1,0:T(8,128)(2,1)S(1)} %get-tuple-element.15.refs_1_), channel_id=1, source_target_pairs={{0,192},{64,0},{128,64},{192,128},{1,193},{65,1},{129,65},{193,129... | collective-permute-start | bytes 1769480 | tf_op jit(solution)/shard_map/ppermute | solution.py:252
  65.8 0.8 copy-start.2
  66.6 24.5 %collective-permute-start.3 = (bf16[9,128,256]{2,1,0:T(8,128)(2,1)S(1)}, bf16[9,128,256]{2,1,0:T(8,128)(2,1)S(1)}, u32[]{:S(2)}, u32[]{:S(2)}) collective-permute-start(bf16[9,128,256]{2,1,0:T(8,128)(2,1)S(1)} %collective-permute-done.refs_3_), channel_id=1, source_target_pairs={{0,64},{64,128},{128,192},{192,0},{1,65},{65,129},{129,193},{193,1... | collective-permute-start | bytes 1769480 | tf_op jit(solution)/shard_map/ppermute | solution.py:252
  66.6 22.9 %collective-permute-start.4 = (bf16[7,128,256]{2,1,0:T(8,128)(2,1)}, bf16[7,128,256]{2,1,0:T(8,128)(2,1)}, u32[]{:S(2)}, u32[]{:S(2)}) collective-permute-start(bf16[7,128,256]{2,1,0:T(8,128)(2,1)} %collective-permute-done.1.refs_8_), channel_id=1, source_target_pairs={{0,192},{64,0},{128,64},{192,128},{1,193},{65,1},{129,65},{193,129... | collective-permute-start | bytes 1376264 | tf_op jit(solution)/shard_map/ppermute | solution.py:252
  74.3 0.8 copy-start.4
  75.1 26.1 %collective-permute-start.9 = (bf16[9,128,256]{2,1,0:T(8,128)(2,1)S(1)}, bf16[9,128,256]{2,1,0:T(8,128)(2,1)S(1)}, u32[]{:S(2)}, u32[]{:S(2)}) collective-permute-start(bf16[9,128,256]{2,1,0:T(8,128)(2,1)S(1)} %collective-permute-done.refs_3_), channel_id=1, source_target_pairs={{0,192},{64,0},{128,64},{192,128},{1,193},{65,1},{129,65},{193,129... | collective-permute-start | bytes 1769480 | tf_op jit(solution)/shard_map/ppermute | solution.py:252
  78.4 22.8 %collective-permute-start.14 = (bf16[7,128,256]{2,1,0:T(8,128)(2,1)}, bf16[7,128,256]{2,1,0:T(8,128)(2,1)}, u32[]{:S(2)}, u32[]{:S(2)}) collective-permute-start(bf16[7,128,256]{2,1,0:T(8,128)(2,1)} %collective-permute-done.1.refs_8_), channel_id=1, source_target_pairs={{0,32},{32,0},{1,33},{33,1},{2,34},{34,2},{3,35},{35,3},{4,36},{36... | collective-permute-start | bytes 1376264 | tf_op jit(solution)/shard_map/ppermute | solution.py:252
  80.3 0.8 copy-start
  81.1 23.9 %collective-permute-start.12 = (bf16[9,128,256]{2,1,0:T(8,128)(2,1)S(1)}, bf16[9,128,256]{2,1,0:T(8,128)(2,1)}, u32[]{:S(2)}, u32[]{:S(2)}) collective-permute-start(bf16[9,128,256]{2,1,0:T(8,128)(2,1)S(1)} %collective-permute-done.5.refs_4_), channel_id=1, source_target_pairs={{0,64},{64,128},{128,192},{192,0},{1,65},{65,129},{129,193},{193,1... | collective-permute-start | bytes 1769480 | tf_op jit(solution)/shard_map/ppermute | solution.py:252
  81.2 1.1 copy-start.1
  82.3 1.0 copy-start.3
  83.3 1.0 copy-start.5
  89.4 15.5 %collective-permute-start.13 = (bf16[7,128,256]{2,1,0:T(8,128)(2,1)S(1)}, bf16[7,128,256]{2,1,0:T(8,128)(2,1)S(1)}, u32[]{:S(2)}, u32[]{:S(2)}) collective-permute-start(bf16[7,128,256]{2,1,0:T(8,128)(2,1)S(1)} %copy-done.3), channel_id=1, source_target_pairs={{0,32},{32,0},{1,33},{33,1},{2,34},{34,2},{3,35},{35,3},{4,36},{36... | collective-permute-start | bytes 1376264 | tf_op jit(solution)/shard_map/ppermute | solution.py:252
  91.1 20.9 %collective-permute-start.11 = (bf16[7,128,256]{2,1,0:T(8,128)(2,1)}, bf16[7,128,256]{2,1,0:T(8,128)(2,1)S(1)}, u32[]{:S(2)}, u32[]{:S(2)}) collective-permute-start(bf16[7,128,256]{2,1,0:T(8,128)(2,1)} %collective-permute-done.4.refs_8_), channel_id=1, source_target_pairs={{0,32},{32,0},{1,33},{33,1},{2,34},{34,2},{3,35},{35,3},{4,36},{36... | collective-permute-start | bytes 1376264 | tf_op jit(solution)/shard_map/ppermute | solution.py:252
  101.2 10.8 %collective-permute-start.8 = (bf16[5,128,256]{2,1,0:T(8,128)(2,1)S(1)}, bf16[5,128,256]{2,1,0:T(8,128)(2,1)S(1)}, u32[]{:S(2)}, u32[]{:S(2)}) collective-permute-start(bf16[5,128,256]{2,1,0:T(8,128)(2,1)S(1)} %slice.6), channel_id=1, source_target_pairs={{0,64},{64,128},{128,192},{192,0},{1,65},{65,129},{129,193},{193,1... | collective-permute-start | bytes 983048 | tf_op jit(solution)/shard_map/ppermute | solution.py:252
  101.2 9.8 %collective-permute-start.10 = (bf16[4,128,256]{2,1,0:T(8,128)(2,1)S(1)}, bf16[4,128,256]{2,1,0:T(8,128)(2,1)S(1)}, u32[]{:S(2)}, u32[]{:S(2)}) collective-permute-start(bf16[4,128,256]{2,1,0:T(8,128)(2,1)S(1)} %slice.8), channel_id=1, source_target_pairs={{0,192},{64,0},{128,64},{192,128},{1,193},{65,1},{129,65},{193,129... | collective-permute-start | bytes 786440 | tf_op jit(solution)/shard_map/ppermute | solution.py:252
